TPU v7x, 256 devices: a whole 4x4x8 slice. The times are simulated.
256 devices in a mesh: dp: 8 (over z_lo, y), graph: 32 (over x, z_hi, core).
Axes of the slice: x: 4, y: 4, z: 8 (z_hi: 4, z_lo: 2; z = z_hi * 2 + z_lo), core: 2. Of those that a mesh axis runs over, the one named last changes fastest.
Arguments:
- node_embed: bfloat16 [8, 512, 1024], P('dp', 'graph'), may hold values from -6 to 6
- node_cotan: bfloat16 [8, 512, 1024], P('dp', 'graph'), may hold values from -6 to 6
- radial: bfloat16 [8, 24576, 128], P('dp', 'graph'), may hold values from -6 to 6
- source: int32 [8, 24576], P('dp', 'graph'), may hold values from 0 to 511
- target: int32 [8, 24576], P('dp', 'graph'), may hold values from 0 to 511
- edge_count: int32 [8, 32], P('dp', 'graph'), may hold values from 384 to 768, as said below
- w_source: bfloat16 [1024, 1024], replicated, may hold values from -0.1875 to 0.1875
- w_target: bfloat16 [1024, 1024], replicated, may hold values from -0.1875 to 0.1875
- w_out: bfloat16 [1024, 1024], replicated, may hold values from -0.1875 to 0.1875
- w_radial: bfloat16 [128, 1024], replicated, may hold values from -0.5 to 0.5
Outputs:
- node_grad: float32 [8, 512, 1024], P('dp', 'graph')
- grad_source: float32 [1024, 1024], P('graph')
- grad_target: float32 [1024, 1024], P('graph')
- grad_out: float32 [1024, 1024], P('graph')
- grad_radial: float32 [128, 1024], replicated
Inputs may be any that keep to these rules, and one draw needn't show every extreme that they name: `edge_count`: edge slots of one graph index at or past its count are padding; in every batch one graph index has all 768 slots live.
All inputs are finite; a program needn't handle non-finite values.
Results may differ from a plain program's by a relative error of at most 0.019.
Values may be sent and summed in bfloat16 or wider, within the bound.
No kernel may reach another device: no remote copies, remote signals or barrier semaphores. Data moves between devices by JAX's collectives and lax.ppermute only.
A program may use at most 128 MiB of HBM per device.

v0:
```python
import jax
import jax.numpy as jnp
from jax import lax
from jax.experimental import pallas as pl
from jax.experimental.pallas import tpu as pltpu
from jax.sharding import Mesh
from jax.sharding import PartitionSpec as P

BF = jnp.bfloat16
F32 = jnp.float32


def dot(left, right, dims=((1,), (0,))):
    return lax.dot_general(left, right, (dims, ((), ())), preferred_element_type=F32)


def pick(array, index, axis):
    return lax.dynamic_index_in_dim(array, index, axis, keepdims=False)


def send(array, axis, offset):
    size = lax.axis_size(axis)
    return lax.ppermute(array, axis, [(i, (i + offset) % size) for i in range(size)])


def gather_from(array, axis):
    return [array] + [send(array, axis, -o) for o in range(1, lax.axis_size(axis))]


def trade(pieces, axis):
    return [pieces[0]] + [send(pieces[o], axis, o) for o in range(1, len(pieces))]


def total(parts):
    out = parts[0].astype(F32)
    for part in parts[1:]:
        out = out + part.astype(F32)
    return out


def in_order(parts, me):
    size = len(parts)
    stacked = jnp.stack(parts)
    return jnp.stack([pick(stacked, (me - a) % size, 0) for a in range(size)])


def natural(array, lead):
    return array.reshape(lead, 4, 2, 4, 32).transpose(0, 1, 3, 2, 4).reshape(lead, 1024)


def edge_kernel(
    at_ref, mine_ref, sib_ref, edge_mine_ref, edge_sib_ref, ws, wt, wo, wr,
    *refs
):
    sums_refs, grad_refs = refs[:4], refs[4:8]
    grads_ref, embed, cotan, p_s, p_tq, w_r, acc_s, acc_t, acc_r = refs[8:]
    my_y, my_x, my_z, my_c = (at_ref[i] for i in range(4))

    def own(rows):
        parts = rows.reshape(4, 2, 32, rows.shape[1])
        return jnp.where(my_c == 0, parts[:, 0], parts[:, 1]).reshape(128, rows.shape[1])

    for half, ref in enumerate((mine_ref, sib_ref)):
        rows = pl.ds(half * 256, 256)
        embed[rows] = ref[:, :, 0].reshape(256, 1024)
        cotan[rows] = ref[:, :, 1].reshape(256, 1024)
    acc_s[...] = jnp.zeros_like(acc_s)
    acc_t[...] = jnp.zeros_like(acc_t)
    acc_r[...] = jnp.zeros_like(acc_r)
    p_s[...] = own(dot(embed[...], ws[...]).T).astype(BF)
    p_tq[:128] = own(dot(embed[...], wt[...]).T).astype(BF)
    p_tq[128:] = dot(own(wo[...]), cotan[...], ((1,), (1,))).astype(BF)
    w_r[...] = own(wr[...].astype(F32).T).astype(BF)
    spot = lax.broadcasted_iota(jnp.int32, (512, 768), 0).astype(jnp.int16)

    def block(ref, i):
        radial = ref[i, :768]
        coded = ref[i, 768:].astype(F32)
        node = (coded[:12] * 16.0 + coded[12:24]).astype(jnp.int32) - 1
        far_z = ((node >> 5) - my_z) & 3
        far_x = ((node >> 7) - my_x) & 3
        far_c = ((node >> 4) & 1) ^ my_c
        place = (far_c * 16 + far_x * 4 + far_z) * 16 + (node & 15)
        place = jnp.where(node >= 0, place, -1)

        def hot(first):
            row = jnp.concatenate([place[first + i : first + i + 1] for i in range(6)], axis=1)
            return jnp.where(spot == row.astype(jnp.int16), BF(1), BF(0))

        hot_s, hot_t = hot(0), hot(6)
        col = place.T
        spot_n = lax.broadcasted_iota(jnp.int32, (768, 512), 1).astype(jnp.int16)

        def hot_n(first):
            column = jnp.concatenate([col[:, first + i : first + i + 1] for i in range(6)], axis=0)
            return jnp.where(spot_n == jnp.broadcast_to(column, (768, 512)).astype(jnp.int16), BF(1), BF(0))

        both = dot(p_tq[...], hot_t)
        pre = dot(p_s[...], hot_s) + both[:128]
        gmsg = both[128:]
        rad = dot(w_r[...], radial, ((1,), (1,)))
        sig = 1.0 / (1.0 + jnp.exp(-pre))
        act = pre * sig
        message = (act * rad).astype(BF)
        grad_rad = (gmsg * act).astype(BF)
        grad_pre = (gmsg * rad * (sig + act * (1.0 - sig))).astype(BF)
        acc_t[...] += dot(jnp.concatenate([message, grad_pre]), hot_n(6))
        acc_s[...] += dot(grad_pre, hot_n(0))
        acc_r[...] += dot(grad_rad, radial)

    @pl.loop(0, 4)
    def _(i):
        block(edge_mine_ref, i)
        block(edge_sib_ref, i)

    for mat, flat in enumerate((acc_s[...], acc_t[128:])):
        nodes = flat.T.astype(BF)
        for c in range(2):
            for x in range(4):
                for z in range(4):
                    first = (c * 16 + x * 4 + z) * 16
                    sums_refs[z][x, c, mat] = nodes[first : first + 16]
        grad = dot(flat.astype(BF), embed[...]).T.astype(BF)
        for h in range(2):
            to = (2 * mat + h - my_y) & 3
            for i in range(32):
                grads_ref[to, i * 16 : i * 16 + 16] = grad[i * 32 + h * 16 : i * 32 + h * 16 + 16]
    grad = dot(acc_t[:128].astype(BF), cotan[...]).astype(BF)
    for k in range(2):
        for h in range(2):
            to = (2 * k + h - my_y) & 3
            for z in range(4):
                for b in range(4):
                    first, at = z * 32 + h * 16, 512 + (z * 4 + b) * 16
                    cols = slice(k * 512 + b * 128, k * 512 + b * 128 + 128)
                    grads_ref[to, at : at + 16] = grad[first : first + 16, cols]
    grad = acc_r[...].T.astype(BF)
    for y in range(4):
        grads_ref[(y - my_y) & 3, 768:800] = grad[y * 32 : y * 32 + 32]
    for o in range(4):
        grad_refs[o][...] = grads_ref[o]


def edge_pass(at, mine, sib, edge_mine, edge_sib, ws, wt, wo, wr):
    vmem = pl.BlockSpec(memory_space=pltpu.VMEM)
    return pl.pallas_call(
        edge_kernel,
        in_specs=[pl.BlockSpec(memory_space=pltpu.SMEM)] + [vmem] * 8,
        out_specs=[vmem] * 8,
        out_shape=[jax.ShapeDtypeStruct((4, 2, 2, 16, 128), BF)] * 4
        + [jax.ShapeDtypeStruct((800, 128), BF)] * 4,
        scratch_shapes=[
            pltpu.VMEM((4, 800, 128), BF),
            pltpu.VMEM((512, 1024), BF),
            pltpu.VMEM((512, 1024), BF),
            pltpu.VMEM((128, 512), BF),
            pltpu.VMEM((256, 512), BF),
            pltpu.VMEM((128, 128), BF),
            pltpu.VMEM((128, 512), F32),
            pltpu.VMEM((256, 512), F32),
            pltpu.VMEM((128, 128), F32),
        ],
        compiler_params=pltpu.CompilerParams(vmem_limit_bytes=16 * 1024 * 1024),
        cost_estimate=pl.CostEstimate(
            flops=6_000_000_000, bytes_accessed=8_000_000, transcendentals=1_600_000
        ),
    )(at, mine, sib, edge_mine, edge_sib, ws, wt, wo, wr)


def node_kernel(sums_ref, cotan_ref, ws_ref, wt_ref, out_ref):
    out_ref[...] = cotan_ref[...].astype(F32) + (
        dot(ws_ref[...], sums_ref[:16], ((1,), (1,))) + dot(wt_ref[...], sums_ref[16:], ((1,), (1,)))
    ).T


def node_pass(sums, cotan, ws, wt):
    vmem = pl.BlockSpec(memory_space=pltpu.VMEM)
    return pl.pallas_call(
        node_kernel,
        in_specs=[vmem] * 4,
        out_specs=vmem,
        out_shape=jax.ShapeDtypeStruct((16, 1024), F32),
        compiler_params=pltpu.CompilerParams(vmem_limit_bytes=8 * 1024 * 1024),
        cost_estimate=pl.CostEstimate(flops=70_000_000, bytes_accessed=4_300_000, transcendentals=0),
    )(sums, cotan, ws, wt)


def per_device(
    node_embed, node_cotan, radial, source, target, edge_count, w_source, w_target, w_out, w_radial
):
    my_y, my_x = lax.axis_index("y"), lax.axis_index("x")
    my_z, my_c = lax.axis_index("zhi"), lax.axis_index("core")
    cotan = node_cotan[0]

    nodes = jnp.stack(gather_from(jnp.concatenate([node_embed[0], cotan]).reshape(2, 16, 1024), "zhi"))

    live = jnp.arange(768, dtype=jnp.int32) < edge_count[0, 0]
    ids = jnp.where(live[None], jnp.stack([source[0], target[0]]) + 1, 0)
    ids = jnp.stack([ids >> 4, ids & 15]).astype(BF).reshape(24, 128)
    edges = jnp.concatenate([radial[0], ids, jnp.zeros((8, 128), BF)])
    edges = jnp.stack(gather_from(edges, "x"))
    edge_sib = send(edges, "core", 1)
    nodes = jnp.stack(gather_from(nodes, "x"))

    def mine(weight, axis):
        return lax.dynamic_slice_in_dim(weight, my_x * 256, 256, axis)

    weights = (mine(w_source, 1), mine(w_target, 1), mine(w_out, 0), mine(w_radial, 1))
    node_sib = send(nodes, "core", 1)
    at = jnp.stack([my_y, my_x, my_z, my_c]).astype(jnp.int32)
    out = edge_pass(at, nodes, node_sib, edges, edge_sib, *weights)
    sums, grads = out[:4], out[4:]

    y_parts = trade(grads, "y")
    sums = total(trade(sums, "zhi")).astype(BF).reshape(4, 64, 128)
    summed = total(y_parts).astype(BF)
    w_st = summed[:512].reshape(4, 4, 2, 16, 128)
    w_o = summed[512:768].reshape(4, 64, 128)
    w_r = summed[768:]

    def z_piece(o):
        at = (my_z + o) & 3
        return jnp.concatenate([pick(w_st, at, 1).reshape(128, 128), pick(w_o, at, 0), w_r])

    parts = trade([z_piece(o) for o in range(4)], "zhi")
    radial_part = total([in_order([p[192:] for p in parts], my_z)[a] for a in range(4)])
    summed = jnp.concatenate([total([p[:192] for p in parts]), radial_part]).astype(BF)
    summed = total(gather_from(summed, "zlo")).astype(BF)
    w_st = summed[:128].reshape(4, 32, 128)
    w_o = summed[128:192].reshape(4, 16, 128).transpose(1, 0, 2).reshape(8, 1024)
    w_r = summed[192:]

    parts = [jnp.concatenate([sums[o], pick(w_st, (my_x + o) & 3, 0), w_r]) for o in range(4)]
    parts = in_order(trade(parts, "x"), my_x)
    sums, w_st = parts[:, :64].reshape(4, 2, 32, 128), parts[:, 64:96].reshape(4, 2, 16, 128)

    def c_piece(o):
        return jnp.concatenate([sums[:, o], pick(w_st, my_c ^ o, 1), parts[:, 96:]], 1)

    both = jnp.stack(trade([c_piece(0), c_piece(1)], "core"))
    both = jnp.stack([pick(both, my_c, 0), pick(both, 1 - my_c, 0)])
    rows = natural(both.transpose(2, 1, 0, 3).reshape(80, 4, 2, 128), 80)
    node_grad = node_pass(rows[:32], cotan, w_source, w_target)
    rows = in_order(trade([jnp.concatenate([rows[32:], w_o])] * 4, "y"), my_y).astype(F32)
    grad_out = rows[:, 48:].reshape(2, 2, 16, 512).transpose(1, 2, 0, 3).reshape(32, 1024)
    return (
        node_grad[None],
        rows[:2, :16].reshape(32, 1024),
        rows[2:, :16].reshape(32, 1024),
        grad_out,
        rows[:, 16:48].reshape(128, 1024),
    )


def solution(mesh):
    fine = Mesh(mesh.devices.reshape(2, 4, 4, 4, 2), ("zlo", "y", "x", "zhi", "core"))
    dp, graph = ("zlo", "y"), ("x", "zhi", "core")
    placed = (
        P(dp, graph, None),
        P(dp, graph, None),
        P(dp, graph, None),
        P(dp, graph),
        P(dp, graph),
        P(dp, graph),
        P(),
        P(),
        P(),
        P(),
    )
    return jax.shard_map(
        per_device,
        mesh=fine,
        in_specs=placed,
        out_specs=(
            P(dp, graph, None),
            P(graph, None),
            P(graph, None),
            P(graph, None),
            P(),
        ),
        check_vma=False,
    )
```

profile of v0, /device:TPU:1, one launch (start us, length us, event | category | flops | bytes accessed | tf_op | source)
XLA Modules:
  0.0 116.9 jit_solution(10804261137121615513)
XLA Ops:
  0.6 0.9 pad_maximum_fusion.13
  1.6 3.8 %collective-permute-start.2 = (bf16[2,16,1024]{2,1,0:T(8,128)(2,1)S(1)}, bf16[2,16,1024]{2,1,0:T(8,128)(2,1)S(1)}, u32[]{:S(2)}, u32[]{:S(2)}) collective-permute-start(bf16[2,16,1024]{2,1,0:T(8,128)(2,1)S(1)} %bitcast.124), channel_id=1, source_target_pairs={{0,2},{2,4},{4,6},{6,0},{1,3},{3,5},{5,7},{7,1},{8,10},{10,12},{12... | collective-permute-start | bytes 196616 | tf_op jit(solution)/shard_map/ppermute | solution.py:23
  5.4 3.1 %collective-permute-start = (bf16[2,16,1024]{2,1,0:T(8,128)(2,1)S(1)}, bf16[2,16,1024]{2,1,0:T(8,128)(2,1)S(1)}, u32[]{:S(2)}, u32[]{:S(2)}) collective-permute-start(bf16[2,16,1024]{2,1,0:T(8,128)(2,1)S(1)} %bitcast.125), channel_id=1, source_target_pairs={{0,6},{2,0},{4,2},{6,4},{1,7},{3,1},{5,3},{7,5},{8,14},{10,8},{12,... | collective-permute-start | bytes 196616 | tf_op jit(solution)/shard_map/ppermute | solution.py:23
  8.5 4.4 %collective-permute-start.1 = (bf16[2,16,1024]{2,1,0:T(8,128)(2,1)S(1)}, bf16[2,16,1024]{2,1,0:T(8,128)(2,1)S(1)}, u32[]{:S(2)}, u32[]{:S(2)}) collective-permute-start(bf16[2,16,1024]{2,1,0:T(8,128)(2,1)S(1)} %bitcast.126), channel_id=1, source_target_pairs={{0,4},{2,6},{4,0},{6,2},{1,5},{3,7},{5,1},{7,3},{8,12},{10,14},{12... | collective-permute-start | bytes 196616 | tf_op jit(solution)/shard_map/ppermute | solution.py:23
  13.6 0.7 shift-right-arithmetic_convert_fusion
  14.3 1.3 %collective-permute-done.1 = bf16[2,16,1024]{2,1,0:T(8,128)(2,1)S(1)} collective-permute-done((bf16[2,16,1024]{2,1,0:T(8,128)(2,1)S(1)}, bf16[2,16,1024]{2,1,0:T(8,128)(2,1)S(1)}, u32[]{:S(2)}, u32[]{:S(2)}) %collective-permute-start.1) | collective-permute-done | bytes 65568 | tf_op jit(solution)/shard_map/ppermute | solution.py:23
  15.6 2.6 %collective-permute-start.3 = (bf16[4,2,16,1024]{3,2,1,0:T(8,128)(2,1)S(1)}, bf16[4,2,16,1024]{3,2,1,0:T(8,128)(2,1)S(1)}, u32[]{:S(2)}, u32[]{:S(2)}) collective-permute-start(bf16[4,2,16,1024]{3,2,1,0:T(8,128)(2,1)S(1)} %get-tuple-element.28), channel_id=1, source_target_pairs={{0,24},{8,0},{16,8},{24,16},{1,25},{9,1},{17,9},{25,17},{2,26},{10... | collective-permute-start | bytes 786440 | tf_op jit(solution)/shard_map/ppermute | solution.py:23
  18.2 0.5 collective-permute-start.4
  18.7 0.6 collective-permute-start.5
  19.3 0.1 pad.63.clone
  19.4 1.1 fusion.18
  20.5 2.1 %collective-permute-start.7 = (bf16[800,128]{1,0:T(8,128)(2,1)S(1)}, bf16[800,128]{1,0:T(8,128)(2,1)S(1)}, u32[]{:S(2)}, u32[]{:S(2)}) collective-permute-start(bf16[800,128]{1,0:T(8,128)(2,1)S(1)} %get-tuple-element.32), channel_id=1, source_target_pairs={{0,24},{8,0},{16,8},{24,16},{1,25},{9,1},{17,9},{25,17},{2,26},{10... | collective-permute-start | bytes 614408 | tf_op jit(solution)/shard_map/ppermute | solution.py:23
  22.7 1.2 %collective-permute-start.8 = (bf16[800,128]{1,0:T(8,128)(2,1)S(1)}, bf16[800,128]{1,0:T(8,128)(2,1)S(1)}, u32[]{:S(2)}, u32[]{:S(2)}) collective-permute-start(bf16[800,128]{1,0:T(8,128)(2,1)S(1)} %get-tuple-element.32), channel_id=1, source_target_pairs={{0,16},{8,24},{16,0},{24,8},{1,17},{9,25},{17,1},{25,9},{2,18},{10... | collective-permute-start | bytes 614408 | tf_op jit(solution)/shard_map/ppermute | solution.py:23
  23.9 0.2 collective-permute-done.3
  24.1 0.9 collective-permute-done.4
  25.0 9.7 %collective-permute-done.5 = bf16[4,2,16,1024]{3,2,1,0:T(8,128)(2,1)S(1)} collective-permute-done((bf16[4,2,16,1024]{3,2,1,0:T(8,128)(2,1)S(1)}, bf16[4,2,16,1024]{3,2,1,0:T(8,128)(2,1)S(1)}, u32[]{:S(2)}, u32[]{:S(2)}) %collective-permute-start.5) | collective-permute-done | bytes 262176 | tf_op jit(solution)/shard_map/ppermute | solution.py:23
  34.7 0.7 copy-done.7
  35.4 1.2 %pad_maximum_fusion.mine_ref = bf16[4,4,2,16,1024]{4,3,2,1,0:T(8,128)(2,1)S(1)} fusion(bf16[1,4,2,16,1024]{4,3,2,1,0:T(8,128)(2,1)} %bitcast.132, bf16[1,4,2,16,1024]{4,3,2,1,0:T(8,128)(2,1)} %bitcast.131, bf16[1,4,2,16,1024]{4,3,2,1,0:T(8,128)(2,1)} %bitcast.130, bf16[1,4,2,16,1024]{4,3,2,1,0:T(8,128)(2,1)S(1)} %get-tuple-element.27), kind=kLoop, calls=%fused_computation | loop fusion | flops 1572864 | bytes 2097152 | tf_op jit(solution)/shard_map/stack | solution.py:203
  36.6 2.7 %collective-permute-start.6 = (bf16[4,4,2,16,1024]{4,3,2,1,0:T(8,128)(2,1)S(1)}, bf16[4,4,2,16,1024]{4,3,2,1,0:T(8,128)(2,1)}, u32[]{:S(2)}, u32[]{:S(2)}) collective-permute-start(bf16[4,4,2,16,1024]{4,3,2,1,0:T(8,128)(2,1)S(1)} %pad_maximum_fusion.mine_ref), channel_id=1, source_target_pairs={{0,1},{1,0},{2,3},{3,2},{4,5},{5,4},{6,7},{7,6},{8,9},{9,8},{10,11... | collective-permute-start | bytes 3145736 | tf_op jit(solution)/shard_map/ppermute | solution.py:23
  39.4 1.0 pad_maximum_fusion.1.edge_mine_ref
  40.4 3.5 %collective-permute-start.10 = (bf16[4,800,128]{2,1,0:T(8,128)(2,1)}, bf16[4,800,128]{2,1,0:T(8,128)(2,1)}, u32[]{:S(2)}, u32[]{:S(2)}) collective-permute-start(bf16[4,800,128]{2,1,0:T(8,128)(2,1)} %pad_maximum_fusion.1.edge_mine_ref), channel_id=1, source_target_pairs={{0,1},{1,0},{2,3},{3,2},{4,5},{5,4},{6,7},{7,6},{8,9},{9,8},{10,11... | collective-permute-start | bytes 2457608 | tf_op jit(solution)/shard_map/ppermute | solution.py:23
  43.8 0.1 pad_add_fusion.at_ref
  43.9 0.8 constant_dynamic-slice_fusion.20.wr
  44.8 1.3 %constant_dynamic-slice_fusion.22 = (bf16[1024,256]{1,0:T(8,128)(2,1)S(1)}, bf16[1024,256]{1,0:T(8,128)(2,1)S(1)}) fusion(bf16[1024,1024]{1,0:T(8,128)(2,1)} %wt_ref.1, s32[]{:T(128)S(6)} %select_n.154, bf16[1024,1024]{1,0:T(8,128)(2,1)} %ws_ref.1), kind=kLoop, calls=%fused_computation.80 | loop fusion | bytes 2097156 | tf_op jit(solution)/shard_map/dynamic_slice | solution.py:206
  46.1 0.1 collective-permute-done.10.edge_sib_ref
  46.1 12.3 %shard_map.137 = (bf16[4,2,2,16,128]{4,3,2,1,0:T(8,128)(2,1)S(1)}, bf16[4,2,2,16,128]{4,3,2,1,0:T(8,128)(2,1)S(1)}, bf16[4,2,2,16,128]{4,3,2,1,0:T(8,128)(2,1)S(...) custom-call(s32[4]{0:T(128)S(1)} %pad_add_fusion.at_ref, ...), custom_call_target="tpu_custom_call" | custom-call | flops 6000000000 | bytes 8000000 | tf_op jit(solution)/shard_map/pallas_call | solution.py:146
  58.4 0.6 copy-done.4
  59.1 1.3 %collective-permute-start.14 = (bf16[800,128]{1,0:T(8,128)(2,1)}, bf16[800,128]{1,0:T(8,128)(2,1)S(1)}, u32[]{:S(2)}, u32[]{:S(2)}) collective-permute-start(bf16[800,128]{1,0:T(8,128)(2,1)} %get-tuple-element.18), channel_id=1, source_target_pairs={{0,32},{32,64},{64,96},{96,0},{1,33},{33,65},{65,97},{97,1},{2,34}... | collective-permute-start | bytes 614408 | tf_op jit(solution)/shard_map/ppermute | solution.py:23
  60.4 2.6 %collective-permute-start.15 = (bf16[800,128]{1,0:T(8,128)(2,1)}, bf16[800,128]{1,0:T(8,128)(2,1)S(1)}, u32[]{:S(2)}, u32[]{:S(2)}) collective-permute-start(bf16[800,128]{1,0:T(8,128)(2,1)} %get-tuple-element.19), channel_id=1, source_target_pairs={{0,64},{32,96},{64,0},{96,32},{1,65},{33,97},{65,1},{97,33},{2,66}... | collective-permute-start | bytes 614408 | tf_op jit(solution)/shard_map/ppermute | solution.py:23
  63.0 1.1 collective-permute-start.16
  64.1 1.2 collective-permute-start.11
  65.2 3.6 %collective-permute-start.12 = (bf16[4,2,2,16,128]{4,3,2,1,0:T(8,128)(2,1)S(1)}, bf16[4,2,2,16,128]{4,3,2,1,0:T(8,128)(2,1)S(1)}, u32[]{:S(2)}, u32[]{:S(2)}) collective-permute-start(bf16[4,2,2,16,128]{4,3,2,1,0:T(8,128)(2,1)S(1)} %get-tuple-element.15), channel_id=1, source_target_pairs={{0,4},{2,6},{4,0},{6,2},{1,5},{3,7},{5,1},{7,3},{8,12},{10,14},{12... | collective-permute-start | bytes 196616 | tf_op jit(solution)/shard_map/ppermute | solution.py:23
  68.9 3.6 %collective-permute-start.13 = (bf16[4,2,2,16,128]{4,3,2,1,0:T(8,128)(2,1)S(1)}, bf16[4,2,2,16,128]{4,3,2,1,0:T(8,128)(2,1)S(1)}, u32[]{:S(2)}, u32[]{:S(2)}) collective-permute-start(bf16[4,2,2,16,128]{4,3,2,1,0:T(8,128)(2,1)S(1)} %get-tuple-element.16), channel_id=1, source_target_pairs={{0,6},{2,0},{4,2},{6,4},{1,7},{3,1},{5,3},{7,5},{8,14},{10,8},{12,... | collective-permute-start | bytes 196616 | tf_op jit(solution)/shard_map/ppermute | solution.py:23
  72.4 0.1 add_convert_fusion
  72.7 2.4 %collective-permute-start.19 = (bf16[224,128]{1,0:T(8,128)(2,1)S(1)}, bf16[224,128]{1,0:T(8,128)(2,1)S(1)}, u32[]{:S(2)}, u32[]{:S(2)}) collective-permute-start(bf16[224,128]{1,0:T(8,128)(2,1)S(1)} %get-tuple-element.68), channel_id=1, source_target_pairs={{0,6},{2,0},{4,2},{6,4},{1,7},{3,1},{5,3},{7,5},{8,14},{10,8},{12,... | collective-permute-start | bytes 172040 | tf_op jit(solution)/shard_map/ppermute | solution.py:23
  75.1 1.9 %collective-permute-start.17 = (bf16[224,128]{1,0:T(8,128)(2,1)S(1)}, bf16[224,128]{1,0:T(8,128)(2,1)S(1)}, u32[]{:S(2)}, u32[]{:S(2)}) collective-permute-start(bf16[224,128]{1,0:T(8,128)(2,1)S(1)} %get-tuple-element.67), channel_id=1, source_target_pairs={{0,2},{2,4},{4,6},{6,0},{1,3},{3,5},{5,7},{7,1},{8,10},{10,12},{12... | collective-permute-start | bytes 172040 | tf_op jit(solution)/shard_map/ppermute | solution.py:23
  77.0 3.3 %collective-permute-start.18 = (bf16[224,128]{1,0:T(8,128)(2,1)S(1)}, bf16[224,128]{1,0:T(8,128)(2,1)S(1)}, u32[]{:S(2)}, u32[]{:S(2)}) collective-permute-start(bf16[224,128]{1,0:T(8,128)(2,1)S(1)} %get-tuple-element.69), channel_id=1, source_target_pairs={{0,4},{2,6},{4,0},{6,2},{1,5},{3,7},{5,1},{7,3},{8,12},{10,14},{12... | collective-permute-start | bytes 172040 | tf_op jit(solution)/shard_map/ppermute | solution.py:23
  80.2 3.7 %collective-permute-done.18 = bf16[224,128]{1,0:T(8,128)(2,1)S(1)} collective-permute-done((bf16[224,128]{1,0:T(8,128)(2,1)S(1)}, bf16[224,128]{1,0:T(8,128)(2,1)S(1)}, u32[]{:S(2)}, u32[]{:S(2)}) %collective-permute-start.18) | collective-permute-done | bytes 57376 | tf_op jit(solution)/shard_map/ppermute | solution.py:23
  84.0 1.7 %collective-permute-start.20 = (bf16[224,128]{1,0:T(8,128)(2,1)S(1)}, bf16[224,128]{1,0:T(8,128)(2,1)S(1)}, u32[]{:S(2)}, u32[]{:S(2)}) collective-permute-start(bf16[224,128]{1,0:T(8,128)(2,1)S(1)} %pad_maximum_fusion.18), channel_id=1, source_target_pairs={{0,128},{128,0},{1,129},{129,1},{2,130},{130,2},{3,131},{131,3},{4... | collective-permute-start | bytes 172040 | tf_op jit(solution)/shard_map/ppermute | solution.py:23
  85.7 1.9 %collective-permute-done.20 = bf16[224,128]{1,0:T(8,128)(2,1)S(1)} collective-permute-done((bf16[224,128]{1,0:T(8,128)(2,1)S(1)}, bf16[224,128]{1,0:T(8,128)(2,1)S(1)}, u32[]{:S(2)}, u32[]{:S(2)}) %collective-permute-start.20) | collective-permute-done | bytes 57376 | tf_op jit(solution)/shard_map/ppermute | solution.py:23
  87.6 0.1 collective-permute-start.21
  87.7 2.8 %collective-permute-start.22 = (bf16[128,128]{1,0:T(8,128)(2,1)S(1)}, bf16[128,128]{1,0:T(8,128)(2,1)S(1)}, u32[]{:S(2)}, u32[]{:S(2)}) collective-permute-start(bf16[128,128]{1,0:T(8,128)(2,1)S(1)} %get-tuple-element.65), channel_id=1, source_target_pairs={{0,16},{8,24},{16,0},{24,8},{1,17},{9,25},{17,1},{25,9},{2,18},{10... | collective-permute-start | bytes 98312 | tf_op jit(solution)/shard_map/ppermute | solution.py:23
  90.5 1.2 %collective-permute-done.21 = bf16[128,128]{1,0:T(8,128)(2,1)S(1)} collective-permute-done((bf16[128,128]{1,0:T(8,128)(2,1)S(1)}, bf16[128,128]{1,0:T(8,128)(2,1)S(1)}, u32[]{:S(2)}, u32[]{:S(2)}) %collective-permute-start.21) | collective-permute-done | bytes 32800 | tf_op jit(solution)/shard_map/ppermute | solution.py:23
  91.7 0.4 collective-permute-done.22
  92.1 1.1 collective-permute-done.23
  93.4 8.0 %collective-permute-start.24 = (bf16[4,80,128]{2,1,0:T(8,128)(2,1)S(1)}, bf16[4,80,128]{2,1,0:T(8,128)(2,1)S(1)}, u32[]{:S(2)}, u32[]{:S(2)}) collective-permute-start(bf16[4,80,128]{2,1,0:T(8,128)(2,1)S(1)} %get-tuple-element.35), channel_id=1, source_target_pairs={{0,1},{1,0},{2,3},{3,2},{4,5},{5,4},{6,7},{7,6},{8,9},{9,8},{10,11... | collective-permute-start | bytes 245768 | tf_op jit(solution)/shard_map/ppermute | solution.py:23
  101.5 0.9 collective-permute-done.24
  102.4 0.1 fusion.9
  102.5 0.2 copy.66
  102.7 0.1 slice.149
  102.8 0.1 copy.70
  103.0 0.5 collective-permute-start.25
  103.5 3.1 %collective-permute-start.26 = (bf16[56,1024]{1,0:T(8,128)(2,1)S(1)}, bf16[56,1024]{1,0:T(8,128)(2,1)S(1)}, u32[]{:S(2)}, u32[]{:S(2)}) collective-permute-start(bf16[56,1024]{1,0:T(8,128)(2,1)S(1)} %get-tuple-element.46), channel_id=1, source_target_pairs={{0,64},{32,96},{64,0},{96,32},{1,65},{33,97},{65,1},{97,33},{2,66}... | collective-permute-start | bytes 344072 | tf_op jit(solution)/shard_map/ppermute | solution.py:23
  106.6 2.0 %collective-permute-start.27 = (bf16[56,1024]{1,0:T(8,128)(2,1)S(1)}, bf16[56,1024]{1,0:T(8,128)(2,1)S(1)}, u32[]{:S(2)}, u32[]{:S(2)}) collective-permute-start(bf16[56,1024]{1,0:T(8,128)(2,1)S(1)} %get-tuple-element.46), channel_id=1, source_target_pairs={{0,96},{32,0},{64,32},{96,64},{1,97},{33,1},{65,33},{97,65},{2,98}... | collective-permute-start | bytes 344072 | tf_op jit(solution)/shard_map/ppermute | solution.py:23
  108.6 0.4 copy.67
  109.0 0.3 slice.122.sums_ref
  109.3 1.6 %copy-done.1 = bf16[1024,1024]{1,0:T(8,128)(2,1)S(1)} copy-done((bf16[1024,1024]{1,0:T(8,128)(2,1)S(1)}, bf16[1024,1024]{1,0:T(8,128)(2,1)}, u32[]{:S(2)}) %copy-start.1) | copy-done | bytes 2097176
  110.9 1.6 %copy-done.2 = bf16[1024,1024]{1,0:T(8,128)(2,1)S(1)} copy-done((bf16[1024,1024]{1,0:T(8,128)(2,1)S(1)}, bf16[1024,1024]{1,0:T(8,128)(2,1)}, u32[]{:S(2)}) %copy-start.2) | copy-done | bytes 2097176
  112.5 1.9 %shard_map.138 = f32[16,1024]{1,0:T(8,128)} custom-call(bf16[32,1024]{1,0:T(8,128)(2,1)S(1)} %slice.122.sums_ref, bf16[16,1024]{1,0:T(8,128)(2,1)S(1)} %bitcast.116, bf16[1024,1024]{1,0:T(8,128)(2,1)S(1)} %copy-done.2, bf16[1024,1024]{1,0:T(8,128)(2,1)S(1)} %copy-done.1), custom_call_target="tpu_custom_call" | custom-call | flops 70000000 | bytes 4300000 | tf_op jit(solution)/shard_map/pallas_call | solution.py:178
  114.4 0.1 pad_maximum_fusion.2
  114.5 0.8 fusion
  115.4 0.7 maximum_convert_fusion.1
  116.1 0.1 copy.71
  116.2 0.7 copy.77
  (74 shorter events, 0.7 us)
Async XLA Ops:
  0.6 44.1 %copy-start = (bf16[1024,1024]{1,0:T(8,128)(2,1)S(1)}, bf16[1024,1024]{1,0:T(8,128)(2,1)}, u32[]{:S(2)}) copy-start(bf16[1024,1024]{1,0:T(8,128)(2,1)} %param.18) | copy-start | bytes 6291460
  1.6 12.7 %collective-permute-start.2 = (bf16[2,16,1024]{2,1,0:T(8,128)(2,1)S(1)}, bf16[2,16,1024]{2,1,0:T(8,128)(2,1)S(1)}, u32[]{:S(2)}, u32[]{:S(2)}) collective-permute-start(bf16[2,16,1024]{2,1,0:T(8,128)(2,1)S(1)} %bitcast.124), channel_id=1, source_target_pairs={{0,2},{2,4},{4,6},{6,0},{1,3},{3,5},{5,7},{7,1},{8,10},{10,12},{12... | collective-permute-start | bytes 196616 | tf_op jit(solution)/shard_map/ppermute | solution.py:23
  5.4 8.9 %collective-permute-start = (bf16[2,16,1024]{2,1,0:T(8,128)(2,1)S(1)}, bf16[2,16,1024]{2,1,0:T(8,128)(2,1)S(1)}, u32[]{:S(2)}, u32[]{:S(2)}) collective-permute-start(bf16[2,16,1024]{2,1,0:T(8,128)(2,1)S(1)} %bitcast.125), channel_id=1, source_target_pairs={{0,6},{2,0},{4,2},{6,4},{1,7},{3,1},{5,3},{7,5},{8,14},{10,8},{12,... | collective-permute-start | bytes 196616 | tf_op jit(solution)/shard_map/ppermute | solution.py:23
  8.5 7.1 %collective-permute-start.1 = (bf16[2,16,1024]{2,1,0:T(8,128)(2,1)S(1)}, bf16[2,16,1024]{2,1,0:T(8,128)(2,1)S(1)}, u32[]{:S(2)}, u32[]{:S(2)}) collective-permute-start(bf16[2,16,1024]{2,1,0:T(8,128)(2,1)S(1)} %bitcast.126), channel_id=1, source_target_pairs={{0,4},{2,6},{4,0},{6,2},{1,5},{3,7},{5,1},{7,3},{8,12},{10,14},{12... | collective-permute-start | bytes 196616 | tf_op jit(solution)/shard_map/ppermute | solution.py:23
  15.6 8.4 %collective-permute-start.3 = (bf16[4,2,16,1024]{3,2,1,0:T(8,128)(2,1)S(1)}, bf16[4,2,16,1024]{3,2,1,0:T(8,128)(2,1)S(1)}, u32[]{:S(2)}, u32[]{:S(2)}) collective-permute-start(bf16[4,2,16,1024]{3,2,1,0:T(8,128)(2,1)S(1)} %get-tuple-element.28), channel_id=1, source_target_pairs={{0,24},{8,0},{16,8},{24,16},{1,25},{9,1},{17,9},{25,17},{2,26},{10... | collective-permute-start | bytes 786440 | tf_op jit(solution)/shard_map/ppermute | solution.py:23
  18.2 6.8 %collective-permute-start.4 = (bf16[4,2,16,1024]{3,2,1,0:T(8,128)(2,1)S(1)}, bf16[4,2,16,1024]{3,2,1,0:T(8,128)(2,1)S(1)}, u32[]{:S(2)}, u32[]{:S(2)}) collective-permute-start(bf16[4,2,16,1024]{3,2,1,0:T(8,128)(2,1)S(1)} %get-tuple-element.28), channel_id=1, source_target_pairs={{0,16},{8,24},{16,0},{24,8},{1,17},{9,25},{17,1},{25,9},{2,18},{10... | collective-permute-start | bytes 786440 | tf_op jit(solution)/shard_map/ppermute | solution.py:23
  18.7 16.0 %collective-permute-start.5 = (bf16[4,2,16,1024]{3,2,1,0:T(8,128)(2,1)S(1)}, bf16[4,2,16,1024]{3,2,1,0:T(8,128)(2,1)S(1)}, u32[]{:S(2)}, u32[]{:S(2)}) collective-permute-start(bf16[4,2,16,1024]{3,2,1,0:T(8,128)(2,1)S(1)} %get-tuple-element.28), channel_id=1, source_target_pairs={{0,8},{8,16},{16,24},{24,0},{1,9},{9,17},{17,25},{25,1},{2,10},{10... | collective-permute-start | bytes 786440 | tf_op jit(solution)/shard_map/ppermute | solution.py:23
  20.5 18.8 %collective-permute-start.7 = (bf16[800,128]{1,0:T(8,128)(2,1)S(1)}, bf16[800,128]{1,0:T(8,128)(2,1)S(1)}, u32[]{:S(2)}, u32[]{:S(2)}) collective-permute-start(bf16[800,128]{1,0:T(8,128)(2,1)S(1)} %get-tuple-element.32), channel_id=1, source_target_pairs={{0,24},{8,0},{16,8},{24,16},{1,25},{9,1},{17,9},{25,17},{2,26},{10... | collective-permute-start | bytes 614408 | tf_op jit(solution)/shard_map/ppermute | solution.py:23
  22.7 16.7 %collective-permute-start.8 = (bf16[800,128]{1,0:T(8,128)(2,1)S(1)}, bf16[800,128]{1,0:T(8,128)(2,1)S(1)}, u32[]{:S(2)}, u32[]{:S(2)}) collective-permute-start(bf16[800,128]{1,0:T(8,128)(2,1)S(1)} %get-tuple-element.32), channel_id=1, source_target_pairs={{0,16},{8,24},{16,0},{24,8},{1,17},{9,25},{17,1},{25,9},{2,18},{10... | collective-permute-start | bytes 614408 | tf_op jit(solution)/shard_map/ppermute | solution.py:23
  24.0 10.6 %copy-start.5 = (bf16[4,2,16,1024]{3,2,1,0:T(8,128)(2,1)}, bf16[4,2,16,1024]{3,2,1,0:T(8,128)(2,1)S(1)}, u32[]{:S(2)}) copy-start(bf16[4,2,16,1024]{3,2,1,0:T(8,128)(2,1)S(1)} %collective-permute-done.3) | copy-start | bytes 786436
  24.1 15.3 %collective-permute-start.9 = (bf16[800,128]{1,0:T(8,128)(2,1)S(1)}, bf16[800,128]{1,0:T(8,128)(2,1)S(1)}, u32[]{:S(2)}, u32[]{:S(2)}) collective-permute-start(bf16[800,128]{1,0:T(8,128)(2,1)S(1)} %get-tuple-element.32), channel_id=1, source_target_pairs={{0,8},{8,16},{16,24},{24,0},{1,9},{9,17},{17,25},{25,1},{2,10},{10... | collective-permute-start | bytes 614408 | tf_op jit(solution)/shard_map/ppermute | solution.py:23
  25.0 9.7 %copy-start.6 = (bf16[4,2,16,1024]{3,2,1,0:T(8,128)(2,1)}, bf16[4,2,16,1024]{3,2,1,0:T(8,128)(2,1)S(1)}, u32[]{:S(2)}) copy-start(bf16[4,2,16,1024]{3,2,1,0:T(8,128)(2,1)S(1)} %collective-permute-done.4) | copy-start | bytes 786436
  34.7 0.7 copy-start.7
  36.6 9.5 %collective-permute-start.6 = (bf16[4,4,2,16,1024]{4,3,2,1,0:T(8,128)(2,1)S(1)}, bf16[4,4,2,16,1024]{4,3,2,1,0:T(8,128)(2,1)}, u32[]{:S(2)}, u32[]{:S(2)}) collective-permute-start(bf16[4,4,2,16,1024]{4,3,2,1,0:T(8,128)(2,1)S(1)} %pad_maximum_fusion.mine_ref), channel_id=1, source_target_pairs={{0,1},{1,0},{2,3},{3,2},{4,5},{5,4},{6,7},{7,6},{8,9},{9,8},{10,11... | collective-permute-start | bytes 3145736 | tf_op jit(solution)/shard_map/ppermute | solution.py:23
  40.4 5.8 %collective-permute-start.10 = (bf16[4,800,128]{2,1,0:T(8,128)(2,1)}, bf16[4,800,128]{2,1,0:T(8,128)(2,1)}, u32[]{:S(2)}, u32[]{:S(2)}) collective-permute-start(bf16[4,800,128]{2,1,0:T(8,128)(2,1)} %pad_maximum_fusion.1.edge_mine_ref), channel_id=1, source_target_pairs={{0,1},{1,0},{2,3},{3,2},{4,5},{5,4},{6,7},{7,6},{8,9},{9,8},{10,11... | collective-permute-start | bytes 2457608 | tf_op jit(solution)/shard_map/ppermute | solution.py:23
  58.4 0.6 copy-start.4
  59.1 9.8 %collective-permute-start.14 = (bf16[800,128]{1,0:T(8,128)(2,1)}, bf16[800,128]{1,0:T(8,128)(2,1)S(1)}, u32[]{:S(2)}, u32[]{:S(2)}) collective-permute-start(bf16[800,128]{1,0:T(8,128)(2,1)} %get-tuple-element.18), channel_id=1, source_target_pairs={{0,32},{32,64},{64,96},{96,0},{1,33},{33,65},{65,97},{97,1},{2,34}... | collective-permute-start | bytes 614408 | tf_op jit(solution)/shard_map/ppermute | solution.py:23
  60.4 12.1 %collective-permute-start.15 = (bf16[800,128]{1,0:T(8,128)(2,1)}, bf16[800,128]{1,0:T(8,128)(2,1)S(1)}, u32[]{:S(2)}, u32[]{:S(2)}) collective-permute-start(bf16[800,128]{1,0:T(8,128)(2,1)} %get-tuple-element.19), channel_id=1, source_target_pairs={{0,64},{32,96},{64,0},{96,32},{1,65},{33,97},{65,1},{97,33},{2,66}... | collective-permute-start | bytes 614408 | tf_op jit(solution)/shard_map/ppermute | solution.py:23
  63.0 9.4 %collective-permute-start.16 = (bf16[800,128]{1,0:T(8,128)(2,1)}, bf16[800,128]{1,0:T(8,128)(2,1)S(1)}, u32[]{:S(2)}, u32[]{:S(2)}) collective-permute-start(bf16[800,128]{1,0:T(8,128)(2,1)} %get-tuple-element.20), channel_id=1, source_target_pairs={{0,96},{32,0},{64,32},{96,64},{1,97},{33,1},{65,33},{97,65},{2,98}... | collective-permute-start | bytes 614408 | tf_op jit(solution)/shard_map/ppermute | solution.py:23
  64.1 11.0 %collective-permute-start.11 = (bf16[4,2,2,16,128]{4,3,2,1,0:T(8,128)(2,1)}, bf16[4,2,2,16,128]{4,3,2,1,0:T(8,128)(2,1)S(1)}, u32[]{:S(2)}, u32[]{:S(2)}) collective-permute-start(bf16[4,2,2,16,128]{4,3,2,1,0:T(8,128)(2,1)} %copy-done.4), channel_id=1, source_target_pairs={{0,2},{2,4},{4,6},{6,0},{1,3},{3,5},{5,7},{7,1},{8,10},{10,12},{12... | collective-permute-start | bytes 196616 | tf_op jit(solution)/shard_map/ppermute | solution.py:23
  65.2 9.8 %collective-permute-start.12 = (bf16[4,2,2,16,128]{4,3,2,1,0:T(8,128)(2,1)S(1)}, bf16[4,2,2,16,128]{4,3,2,1,0:T(8,128)(2,1)S(1)}, u32[]{:S(2)}, u32[]{:S(2)}) collective-permute-start(bf16[4,2,2,16,128]{4,3,2,1,0:T(8,128)(2,1)S(1)} %get-tuple-element.15), channel_id=1, source_target_pairs={{0,4},{2,6},{4,0},{6,2},{1,5},{3,7},{5,1},{7,3},{8,12},{10,14},{12... | collective-permute-start | bytes 196616 | tf_op jit(solution)/shard_map/ppermute | solution.py:23
  68.9 6.2 %collective-permute-start.13 = (bf16[4,2,2,16,128]{4,3,2,1,0:T(8,128)(2,1)S(1)}, bf16[4,2,2,16,128]{4,3,2,1,0:T(8,128)(2,1)S(1)}, u32[]{:S(2)}, u32[]{:S(2)}) collective-permute-start(bf16[4,2,2,16,128]{4,3,2,1,0:T(8,128)(2,1)S(1)} %get-tuple-element.16), channel_id=1, source_target_pairs={{0,6},{2,0},{4,2},{6,4},{1,7},{3,1},{5,3},{7,5},{8,14},{10,8},{12,... | collective-permute-start | bytes 196616 | tf_op jit(solution)/shard_map/ppermute | solution.py:23
  72.7 7.6 %collective-permute-start.19 = (bf16[224,128]{1,0:T(8,128)(2,1)S(1)}, bf16[224,128]{1,0:T(8,128)(2,1)S(1)}, u32[]{:S(2)}, u32[]{:S(2)}) collective-permute-start(bf16[224,128]{1,0:T(8,128)(2,1)S(1)} %get-tuple-element.68), channel_id=1, source_target_pairs={{0,6},{2,0},{4,2},{6,4},{1,7},{3,1},{5,3},{7,5},{8,14},{10,8},{12,... | collective-permute-start | bytes 172040 | tf_op jit(solution)/shard_map/ppermute | solution.py:23
  75.1 8.8 %collective-permute-start.17 = (bf16[224,128]{1,0:T(8,128)(2,1)S(1)}, bf16[224,128]{1,0:T(8,128)(2,1)S(1)}, u32[]{:S(2)}, u32[]{:S(2)}) collective-permute-start(bf16[224,128]{1,0:T(8,128)(2,1)S(1)} %get-tuple-element.67), channel_id=1, source_target_pairs={{0,2},{2,4},{4,6},{6,0},{1,3},{3,5},{5,7},{7,1},{8,10},{10,12},{12... | collective-permute-start | bytes 172040 | tf_op jit(solution)/shard_map/ppermute | solution.py:23
  77.0 6.9 %collective-permute-start.18 = (bf16[224,128]{1,0:T(8,128)(2,1)S(1)}, bf16[224,128]{1,0:T(8,128)(2,1)S(1)}, u32[]{:S(2)}, u32[]{:S(2)}) collective-permute-start(bf16[224,128]{1,0:T(8,128)(2,1)S(1)} %get-tuple-element.69), channel_id=1, source_target_pairs={{0,4},{2,6},{4,0},{6,2},{1,5},{3,7},{5,1},{7,3},{8,12},{10,14},{12... | collective-permute-start | bytes 172040 | tf_op jit(solution)/shard_map/ppermute | solution.py:23
  84.0 3.5 %collective-permute-start.20 = (bf16[224,128]{1,0:T(8,128)(2,1)S(1)}, bf16[224,128]{1,0:T(8,128)(2,1)S(1)}, u32[]{:S(2)}, u32[]{:S(2)}) collective-permute-start(bf16[224,128]{1,0:T(8,128)(2,1)S(1)} %pad_maximum_fusion.18), channel_id=1, source_target_pairs={{0,128},{128,0},{1,129},{129,1},{2,130},{130,2},{3,131},{131,3},{4... | collective-permute-start | bytes 172040 | tf_op jit(solution)/shard_map/ppermute | solution.py:23
  87.6 4.1 %collective-permute-start.21 = (bf16[128,128]{1,0:T(8,128)(2,1)S(1)}, bf16[128,128]{1,0:T(8,128)(2,1)S(1)}, u32[]{:S(2)}, u32[]{:S(2)}) collective-permute-start(bf16[128,128]{1,0:T(8,128)(2,1)S(1)} %get-tuple-element.64), channel_id=1, source_target_pairs={{0,8},{8,16},{16,24},{24,0},{1,9},{9,17},{17,25},{25,1},{2,10},{10... | collective-permute-start | bytes 98312 | tf_op jit(solution)/shard_map/ppermute | solution.py:23
  87.7 4.4 %collective-permute-start.22 = (bf16[128,128]{1,0:T(8,128)(2,1)S(1)}, bf16[128,128]{1,0:T(8,128)(2,1)S(1)}, u32[]{:S(2)}, u32[]{:S(2)}) collective-permute-start(bf16[128,128]{1,0:T(8,128)(2,1)S(1)} %get-tuple-element.65), channel_id=1, source_target_pairs={{0,16},{8,24},{16,0},{24,8},{1,17},{9,25},{17,1},{25,9},{2,18},{10... | collective-permute-start | bytes 98312 | tf_op jit(solution)/shard_map/ppermute | solution.py:23
  90.5 2.8 %collective-permute-start.23 = (bf16[128,128]{1,0:T(8,128)(2,1)S(1)}, bf16[128,128]{1,0:T(8,128)(2,1)S(1)}, u32[]{:S(2)}, u32[]{:S(2)}) collective-permute-start(bf16[128,128]{1,0:T(8,128)(2,1)S(1)} %get-tuple-element.66), channel_id=1, source_target_pairs={{0,24},{8,0},{16,8},{24,16},{1,25},{9,1},{17,9},{25,17},{2,26},{10... | collective-permute-start | bytes 98312 | tf_op jit(solution)/shard_map/ppermute | solution.py:23
  93.4 15.9 %copy-start.3 = (bf16[1,16,1024]{2,1,0:T(8,128)(2,1)S(1)}, bf16[1,16,1024]{2,1,0:T(8,128)(2,1)}, u32[]{:S(2)}) copy-start(bf16[1,16,1024]{2,1,0:T(8,128)(2,1)} %param.11) | copy-start | bytes 98308
  93.4 8.9 %collective-permute-start.24 = (bf16[4,80,128]{2,1,0:T(8,128)(2,1)S(1)}, bf16[4,80,128]{2,1,0:T(8,128)(2,1)S(1)}, u32[]{:S(2)}, u32[]{:S(2)}) collective-permute-start(bf16[4,80,128]{2,1,0:T(8,128)(2,1)S(1)} %get-tuple-element.35), channel_id=1, source_target_pairs={{0,1},{1,0},{2,3},{3,2},{4,5},{5,4},{6,7},{7,6},{8,9},{9,8},{10,11... | collective-permute-start | bytes 245768 | tf_op jit(solution)/shard_map/ppermute | solution.py:23
  103.0 11.4 %collective-permute-start.25 = (bf16[56,1024]{1,0:T(8,128)(2,1)S(1)}, bf16[56,1024]{1,0:T(8,128)(2,1)S(1)}, u32[]{:S(2)}, u32[]{:S(2)}) collective-permute-start(bf16[56,1024]{1,0:T(8,128)(2,1)S(1)} %get-tuple-element.46), channel_id=1, source_target_pairs={{0,32},{32,64},{64,96},{96,0},{1,33},{33,65},{65,97},{97,1},{2,34}... | collective-permute-start | bytes 344072 | tf_op jit(solution)/shard_map/ppermute | solution.py:23
  103.5 10.9 %collective-permute-start.26 = (bf16[56,1024]{1,0:T(8,128)(2,1)S(1)}, bf16[56,1024]{1,0:T(8,128)(2,1)S(1)}, u32[]{:S(2)}, u32[]{:S(2)}) collective-permute-start(bf16[56,1024]{1,0:T(8,128)(2,1)S(1)} %get-tuple-element.46), channel_id=1, source_target_pairs={{0,64},{32,96},{64,0},{96,32},{1,65},{33,97},{65,1},{97,33},{2,66}... | collective-permute-start | bytes 344072 | tf_op jit(solution)/shard_map/ppermute | solution.py:23
  106.6 7.8 %collective-permute-start.27 = (bf16[56,1024]{1,0:T(8,128)(2,1)S(1)}, bf16[56,1024]{1,0:T(8,128)(2,1)S(1)}, u32[]{:S(2)}, u32[]{:S(2)}) collective-permute-start(bf16[56,1024]{1,0:T(8,128)(2,1)S(1)} %get-tuple-element.46), channel_id=1, source_target_pairs={{0,96},{32,0},{64,32},{96,64},{1,97},{33,1},{65,33},{97,65},{2,98}... | collective-permute-start | bytes 344072 | tf_op jit(solution)/shard_map/ppermute | solution.py:23
  109.3 1.6 %copy-start.1 = (bf16[1024,1024]{1,0:T(8,128)(2,1)S(1)}, bf16[1024,1024]{1,0:T(8,128)(2,1)}, u32[]{:S(2)}) copy-start(bf16[1024,1024]{1,0:T(8,128)(2,1)} %wt_ref.1) | copy-start | bytes 6291460
  110.9 1.6 %copy-start.2 = (bf16[1024,1024]{1,0:T(8,128)(2,1)S(1)}, bf16[1024,1024]{1,0:T(8,128)(2,1)}, u32[]{:S(2)}) copy-start(bf16[1024,1024]{1,0:T(8,128)(2,1)} %ws_ref.1) | copy-start | bytes 6291460
where the time goes:
time: 117 us
  starting transfers between devices  63.6 us (54%)
  waiting for transfers between devices  21.3 us (18%)
  Pallas kernels  14.2 us (12%)
  local copies, waits for them, and re-layouts  8.94 us (8%)
  other arithmetic  7.2 us (6%)
  between operations  1.69 us (1%)
    ppermute x28, starting transfers between devices, send(): lax.ppermute(array, axis, [(i, (i + offset) % size) for i in range(size)])  63.6 us
    ppermute x28, waiting for transfers between devices, send(): lax.ppermute(array, axis, [(i, (i + offset) % size) for i in range(size)])  21.3 us
    pallas_call x1, Pallas kernels, edge_pass(): pl.pallas_call(edge_kernel, in_specs=[pl.BlockSpec(memory_space=pltpu.SME...  12.3 us
    unnamed x17, local copies, waits for them, and re-layouts  5.21 us
  transfers between devices with their start and end apart: 28, of which 10 were waited for; matrix products, arithmetic and copies ran while one was open for 6% of the time, Pallas kernels for 2%

commit v1 on v0

--- a/solution.py
+++ b/solution.py
@@ -108,8 +108,7 @@
         acc_s[...] += dot(grad_pre, hot_n(0))
         acc_r[...] += dot(grad_rad, radial)
 
-    @pl.loop(0, 4)
-    def _(i):
+    for i in range(4):
         block(edge_mine_ref, i)
         block(edge_sib_ref, i)
 
@@ -192,15 +191,17 @@
     my_z, my_c = lax.axis_index("zhi"), lax.axis_index("core")
     cotan = node_cotan[0]
 
-    nodes = jnp.stack(gather_from(jnp.concatenate([node_embed[0], cotan]).reshape(2, 16, 1024), "zhi"))
+    nodes = gather_from(jnp.concatenate([node_embed[0], cotan]).reshape(2, 16, 1024), "zhi")
 
     live = jnp.arange(768, dtype=jnp.int32) < edge_count[0, 0]
     ids = jnp.where(live[None], jnp.stack([source[0], target[0]]) + 1, 0)
     ids = jnp.stack([ids >> 4, ids & 15]).astype(BF).reshape(24, 128)
     edges = jnp.concatenate([radial[0], ids, jnp.zeros((8, 128), BF)])
-    edges = jnp.stack(gather_from(edges, "x"))
+    edges = gather_from(edges, "x")
+    nodes, edges[2] = lax.optimization_barrier((nodes, edges[2]))
+    edges = jnp.stack(edges)
     edge_sib = send(edges, "core", 1)
-    nodes = jnp.stack(gather_from(nodes, "x"))
+    nodes = jnp.stack(gather_from(jnp.stack(nodes), "x"))
 
     def mine(weight, axis):
         return lax.dynamic_slice_in_dim(weight, my_x * 256, 256, axis)
@@ -212,7 +213,7 @@
     sums, grads = out[:4], out[4:]
 
     y_parts = trade(grads, "y")
-    sums = total(trade(sums, "zhi")).astype(BF).reshape(4, 64, 128)
+    sums = trade(sums, "zhi")
     summed = total(y_parts).astype(BF)
     w_st = summed[:512].reshape(4, 4, 2, 16, 128)
     w_o = summed[512:768].reshape(4, 64, 128)
@@ -223,6 +224,8 @@
         return jnp.concatenate([pick(w_st, at, 1).reshape(128, 128), pick(w_o, at, 0), w_r])
 
     parts = trade([z_piece(o) for o in range(4)], "zhi")
+    parts, sums = lax.optimization_barrier((parts, sums))
+    sums = total(sums).astype(BF).reshape(4, 64, 128)
     radial_part = total([in_order([p[192:] for p in parts], my_z)[a] for a in range(4)])
     summed = jnp.concatenate([total([p[:192] for p in parts]), radial_part]).astype(BF)
     summed = total(gather_from(summed, "zlo")).astype(BF)

time: 117 us -> 112 us (0.957)
  starting transfers between devices: 63.6 us -> 59.5 us
  waiting for transfers between devices: 21.3 us -> 22.9 us
  other arithmetic: 7.2 us -> 5.95 us
    ppermute x28, starting transfers between devices: 63.6 us -> 59.5 us  [send(): lax.ppermute(array, axis, [(i, (i + offset) % size) for i in range(size)])]
    ppermute x28, waiting for transfers between devices: 21.3 us -> 22.9 us  [send(): lax.ppermute(array, axis, [(i, (i + offset) % size) for i in range(size)])]
    unnamed x17 -> x11, local copies, waits for them, and re-layouts: 5.21 us -> 4.5 us
  transfers between devices with their start and end apart: 28 -> 28, of which waited for: 10 -> 13; matrix products, arithmetic and copies ran while one was open for 6% -> 5% of each run, Pallas kernels for 2% -> 2%
where the time goes in v1:
time: 112 us
  starting transfers between devices  59.5 us (53%)
  waiting for transfers between devices  22.9 us (20%)
  Pallas kernels  13.2 us (12%)
  local copies, waits for them, and re-layouts  8.24 us (7%)
  other arithmetic  5.95 us (5%)
  between operations  1.83 us (2%)
    ppermute x28, starting transfers between devices, send(): lax.ppermute(array, axis, [(i, (i + offset) % size) for i in range(size)])  59.5 us
    ppermute x28, waiting for transfers between devices, send(): lax.ppermute(array, axis, [(i, (i + offset) % size) for i in range(size)])  22.9 us
    pallas_call x1, Pallas kernels, edge_pass(): pl.pallas_call(edge_kernel, in_specs=[pl.BlockSpec(memory_space=pltpu.SME...  11.3 us
    unnamed x11, local copies, waits for them, and re-layouts  4.5 us
  transfers between devices with their start and end apart: 28, of which 13 were waited for; matrix products, arithmetic and copies ran while one was open for 5% of the time, Pallas kernels for 2%

profile of v1, /device:TPU:1, one launch (start us, length us, event | category | flops | bytes accessed | tf_op | source)
XLA Modules:
  0.0 111.6 jit_solution(974323385199992698)
XLA Ops:
  1.5 0.7 shift-right-arithmetic_convert_fusion
  2.2 0.1 pad.72.clone
  2.3 1.1 fusion.18
  3.4 3.7 %collective-permute-start.3 = (bf16[800,128]{1,0:T(8,128)(2,1)S(1)}, bf16[800,128]{1,0:T(8,128)(2,1)S(1)}, u32[]{:S(2)}, u32[]{:S(2)}) collective-permute-start(bf16[800,128]{1,0:T(8,128)(2,1)S(1)} %get-tuple-element.56), channel_id=1, source_target_pairs={{0,16},{8,24},{16,0},{24,8},{1,17},{9,25},{17,1},{25,9},{2,18},{10... | collective-permute-start | bytes 614408 | tf_op jit(solution)/shard_map/ppermute | solution.py:23
  7.1 0.8 pad_maximum_fusion.14
  7.8 6.0 %collective-permute-start = (bf16[2,16,1024]{2,1,0:T(8,128)(2,1)S(1)}, bf16[2,16,1024]{2,1,0:T(8,128)(2,1)S(1)}, u32[]{:S(2)}, u32[]{:S(2)}) collective-permute-start(bf16[2,16,1024]{2,1,0:T(8,128)(2,1)S(1)} %bitcast.116), channel_id=1, source_target_pairs={{0,6},{2,0},{4,2},{6,4},{1,7},{3,1},{5,3},{7,5},{8,14},{10,8},{12,... | collective-permute-start | bytes 196616 | tf_op jit(solution)/shard_map/ppermute | solution.py:23
  13.9 1.0 collective-permute-start.1
  14.8 2.3 %collective-permute-start.2 = (bf16[2,16,1024]{2,1,0:T(8,128)(2,1)S(1)}, bf16[2,16,1024]{2,1,0:T(8,128)(2,1)S(1)}, u32[]{:S(2)}, u32[]{:S(2)}) collective-permute-start(bf16[2,16,1024]{2,1,0:T(8,128)(2,1)S(1)} %bitcast.118), channel_id=1, source_target_pairs={{0,2},{2,4},{4,6},{6,0},{1,3},{3,5},{5,7},{7,1},{8,10},{10,12},{12... | collective-permute-start | bytes 196616 | tf_op jit(solution)/shard_map/ppermute | solution.py:23
  17.1 4.0 %collective-permute-done.1 = bf16[2,16,1024]{2,1,0:T(8,128)(2,1)S(1)} collective-permute-done((bf16[2,16,1024]{2,1,0:T(8,128)(2,1)S(1)}, bf16[2,16,1024]{2,1,0:T(8,128)(2,1)S(1)}, u32[]{:S(2)}, u32[]{:S(2)}) %collective-permute-start.1) | collective-permute-done | bytes 65568 | tf_op jit(solution)/shard_map/ppermute | solution.py:23
  21.1 0.7 collective-permute-done.2
  21.8 0.9 collective-permute-start.4
  22.8 1.2 %collective-permute-start.5 = (bf16[4,2,16,1024]{3,2,1,0:T(8,128)(2,1)S(1)}, bf16[4,2,16,1024]{3,2,1,0:T(8,128)(2,1)S(1)}, u32[]{:S(2)}, u32[]{:S(2)}) collective-permute-start(bf16[4,2,16,1024]{3,2,1,0:T(8,128)(2,1)S(1)} %get-tuple-element.54), channel_id=1, source_target_pairs={{0,16},{8,24},{16,0},{24,8},{1,17},{9,25},{17,1},{25,9},{2,18},{10... | collective-permute-start | bytes 786440 | tf_op jit(solution)/shard_map/ppermute | solution.py:23
  24.0 2.7 %collective-permute-start.8 = (bf16[800,128]{1,0:T(8,128)(2,1)S(1)}, bf16[800,128]{1,0:T(8,128)(2,1)S(1)}, u32[]{:S(2)}, u32[]{:S(2)}) collective-permute-start(bf16[800,128]{1,0:T(8,128)(2,1)S(1)} %get-tuple-element.56), channel_id=1, source_target_pairs={{0,24},{8,0},{16,8},{24,16},{1,25},{9,1},{17,9},{25,17},{2,26},{10... | collective-permute-start | bytes 614408 | tf_op jit(solution)/shard_map/ppermute | solution.py:23
  26.7 0.4 collective-permute-done.4
  27.1 2.5 %collective-permute-done.5 = bf16[4,2,16,1024]{3,2,1,0:T(8,128)(2,1)S(1)} collective-permute-done((bf16[4,2,16,1024]{3,2,1,0:T(8,128)(2,1)S(1)}, bf16[4,2,16,1024]{3,2,1,0:T(8,128)(2,1)S(1)}, u32[]{:S(2)}, u32[]{:S(2)}) %collective-permute-start.5) | collective-permute-done | bytes 262176 | tf_op jit(solution)/shard_map/ppermute | solution.py:23
  29.6 7.7 %collective-permute-done.6 = bf16[4,2,16,1024]{3,2,1,0:T(8,128)(2,1)S(1)} collective-permute-done((bf16[4,2,16,1024]{3,2,1,0:T(8,128)(2,1)S(1)}, bf16[4,2,16,1024]{3,2,1,0:T(8,128)(2,1)S(1)}, u32[]{:S(2)}, u32[]{:S(2)}) %collective-permute-start.6) | collective-permute-done | bytes 262176 | tf_op jit(solution)/shard_map/ppermute | solution.py:23
  37.3 0.1 pad_maximum_fusion.mine_ref
  37.4 2.3 %collective-permute-start.7 = (bf16[4,4,2,16,1024]{4,3,2,1,0:T(8,128)(2,1)S(1)}, bf16[4,4,2,16,1024]{4,3,2,1,0:T(8,128)(2,1)}, u32[]{:S(2)}, u32[]{:S(2)}) collective-permute-start(bf16[4,4,2,16,1024]{4,3,2,1,0:T(8,128)(2,1)S(1)} %pad_maximum_fusion.mine_ref), channel_id=1, source_target_pairs={{0,1},{1,0},{2,3},{3,2},{4,5},{5,4},{6,7},{7,6},{8,9},{9,8},{10,11... | collective-permute-start | bytes 3145736 | tf_op jit(solution)/shard_map/ppermute | solution.py:23
  39.7 1.9 %collective-permute-done.9 = bf16[800,128]{1,0:T(8,128)(2,1)S(1)} collective-permute-done((bf16[800,128]{1,0:T(8,128)(2,1)S(1)}, bf16[800,128]{1,0:T(8,128)(2,1)S(1)}, u32[]{:S(2)}, u32[]{:S(2)}) %collective-permute-start.9) | collective-permute-done | bytes 204832 | tf_op jit(solution)/shard_map/ppermute | solution.py:23
  41.7 1.0 pad_maximum_fusion.1.edge_mine_ref
  42.7 1.3 %collective-permute-start.10 = (bf16[4,800,128]{2,1,0:T(8,128)(2,1)}, bf16[4,800,128]{2,1,0:T(8,128)(2,1)}, u32[]{:S(2)}, u32[]{:S(2)}) collective-permute-start(bf16[4,800,128]{2,1,0:T(8,128)(2,1)} %pad_maximum_fusion.1.edge_mine_ref), channel_id=1, source_target_pairs={{0,1},{1,0},{2,3},{3,2},{4,5},{5,4},{6,7},{7,6},{8,9},{9,8},{10,11... | collective-permute-start | bytes 2457608 | tf_op jit(solution)/shard_map/ppermute | solution.py:23
  44.0 0.1 pad_add_fusion.at_ref
  44.1 0.8 constant_dynamic-slice_fusion.20.wr
  45.0 1.3 %constant_dynamic-slice_fusion.22 = (bf16[1024,256]{1,0:T(8,128)(2,1)S(1)}, bf16[1024,256]{1,0:T(8,128)(2,1)S(1)}) fusion(bf16[1024,1024]{1,0:T(8,128)(2,1)} %wt_ref.1, s32[]{:T(128)S(6)} %select_n.154, bf16[1024,1024]{1,0:T(8,128)(2,1)} %ws_ref.1), kind=kLoop, calls=%fused_computation.81 | loop fusion | bytes 2097156 | tf_op jit(solution)/shard_map/dynamic_slice | solution.py:207
  46.3 11.3 %shard_map.137 = (bf16[4,2,2,16,128]{4,3,2,1,0:T(8,128)(2,1)S(1)}, bf16[4,2,2,16,128]{4,3,2,1,0:T(8,128)(2,1)S(1)}, bf16[4,2,2,16,128]{4,3,2,1,0:T(8,128)(2,1)S(...) custom-call(s32[4]{0:T(128)S(1)} %pad_add_fusion.at_ref, ...), custom_call_target="tpu_custom_call" | custom-call | flops 6000000000 | bytes 8000000 | tf_op jit(solution)/shard_map/pallas_call | solution.py:145
  57.6 0.6 copy-done.4
  58.2 1.3 %collective-permute-start.11 = (bf16[800,128]{1,0:T(8,128)(2,1)}, bf16[800,128]{1,0:T(8,128)(2,1)S(1)}, u32[]{:S(2)}, u32[]{:S(2)}) collective-permute-start(bf16[800,128]{1,0:T(8,128)(2,1)} %get-tuple-element.32), channel_id=1, source_target_pairs={{0,32},{32,64},{64,96},{96,0},{1,33},{33,65},{65,97},{97,1},{2,34}... | collective-permute-start | bytes 614408 | tf_op jit(solution)/shard_map/ppermute | solution.py:23
  59.5 2.6 %collective-permute-start.12 = (bf16[800,128]{1,0:T(8,128)(2,1)}, bf16[800,128]{1,0:T(8,128)(2,1)S(1)}, u32[]{:S(2)}, u32[]{:S(2)}) collective-permute-start(bf16[800,128]{1,0:T(8,128)(2,1)} %get-tuple-element.33), channel_id=1, source_target_pairs={{0,64},{32,96},{64,0},{96,32},{1,65},{33,97},{65,1},{97,33},{2,66}... | collective-permute-start | bytes 614408 | tf_op jit(solution)/shard_map/ppermute | solution.py:23
  62.1 1.1 collective-permute-start.13
  63.2 0.6 collective-permute-start.17
  63.8 4.2 %collective-permute-start.18 = (bf16[4,2,2,16,128]{4,3,2,1,0:T(8,128)(2,1)S(1)}, bf16[4,2,2,16,128]{4,3,2,1,0:T(8,128)(2,1)S(1)}, u32[]{:S(2)}, u32[]{:S(2)}) collective-permute-start(bf16[4,2,2,16,128]{4,3,2,1,0:T(8,128)(2,1)S(1)} %get-tuple-element.37), channel_id=1, source_target_pairs={{0,4},{2,6},{4,0},{6,2},{1,5},{3,7},{5,1},{7,3},{8,12},{10,14},{12... | collective-permute-start | bytes 196616 | tf_op jit(solution)/shard_map/ppermute | solution.py:23
  68.0 3.6 %collective-permute-start.19 = (bf16[4,2,2,16,128]{4,3,2,1,0:T(8,128)(2,1)S(1)}, bf16[4,2,2,16,128]{4,3,2,1,0:T(8,128)(2,1)S(1)}, u32[]{:S(2)}, u32[]{:S(2)}) collective-permute-start(bf16[4,2,2,16,128]{4,3,2,1,0:T(8,128)(2,1)S(1)} %get-tuple-element.38), channel_id=1, source_target_pairs={{0,6},{2,0},{4,2},{6,4},{1,7},{3,1},{5,3},{7,5},{8,14},{10,8},{12,... | collective-permute-start | bytes 196616 | tf_op jit(solution)/shard_map/ppermute | solution.py:23
  71.6 0.1 add_convert_fusion
  71.9 0.7 collective-permute-start.14
  72.5 4.3 %collective-permute-start.15 = (bf16[224,128]{1,0:T(8,128)(2,1)S(1)}, bf16[224,128]{1,0:T(8,128)(2,1)S(1)}, u32[]{:S(2)}, u32[]{:S(2)}) collective-permute-start(bf16[224,128]{1,0:T(8,128)(2,1)S(1)} %get-tuple-element.93), channel_id=1, source_target_pairs={{0,4},{2,6},{4,0},{6,2},{1,5},{3,7},{5,1},{7,3},{8,12},{10,14},{12... | collective-permute-start | bytes 172040 | tf_op jit(solution)/shard_map/ppermute | solution.py:23
  76.8 3.5 %collective-permute-start.16 = (bf16[224,128]{1,0:T(8,128)(2,1)S(1)}, bf16[224,128]{1,0:T(8,128)(2,1)S(1)}, u32[]{:S(2)}, u32[]{:S(2)}) collective-permute-start(bf16[224,128]{1,0:T(8,128)(2,1)S(1)} %get-tuple-element.91), channel_id=1, source_target_pairs={{0,6},{2,0},{4,2},{6,4},{1,7},{3,1},{5,3},{7,5},{8,14},{10,8},{12,... | collective-permute-start | bytes 172040 | tf_op jit(solution)/shard_map/ppermute | solution.py:23
  80.3 0.3 collective-permute-done.15
  80.6 1.4 %collective-permute-done.16 = bf16[224,128]{1,0:T(8,128)(2,1)S(1)} collective-permute-done((bf16[224,128]{1,0:T(8,128)(2,1)S(1)}, bf16[224,128]{1,0:T(8,128)(2,1)S(1)}, u32[]{:S(2)}, u32[]{:S(2)}) %collective-permute-start.16) | collective-permute-done | bytes 57376 | tf_op jit(solution)/shard_map/ppermute | solution.py:23
  82.1 2.1 %collective-permute-start.20 = (bf16[224,128]{1,0:T(8,128)(2,1)S(1)}, bf16[224,128]{1,0:T(8,128)(2,1)S(1)}, u32[]{:S(2)}, u32[]{:S(2)}) collective-permute-start(bf16[224,128]{1,0:T(8,128)(2,1)S(1)} %pad_maximum_fusion.19), channel_id=1, source_target_pairs={{0,128},{128,0},{1,129},{129,1},{2,130},{130,2},{3,131},{131,3},{4... | collective-permute-start | bytes 172040 | tf_op jit(solution)/shard_map/ppermute | solution.py:23
  84.2 1.5 %collective-permute-done.20 = bf16[224,128]{1,0:T(8,128)(2,1)S(1)} collective-permute-done((bf16[224,128]{1,0:T(8,128)(2,1)S(1)}, bf16[224,128]{1,0:T(8,128)(2,1)S(1)}, u32[]{:S(2)}, u32[]{:S(2)}) %collective-permute-start.20) | collective-permute-done | bytes 57376 | tf_op jit(solution)/shard_map/ppermute | solution.py:23
  85.8 0.1 collective-permute-start.21
  85.9 1.6 %collective-permute-start.22 = (bf16[128,128]{1,0:T(8,128)(2,1)S(1)}, bf16[128,128]{1,0:T(8,128)(2,1)S(1)}, u32[]{:S(2)}, u32[]{:S(2)}) collective-permute-start(bf16[128,128]{1,0:T(8,128)(2,1)S(1)} %get-tuple-element.89), channel_id=1, source_target_pairs={{0,16},{8,24},{16,0},{24,8},{1,17},{9,25},{17,1},{25,9},{2,18},{10... | collective-permute-start | bytes 98312 | tf_op jit(solution)/shard_map/ppermute | solution.py:23
  87.4 1.8 %collective-permute-start.23 = (bf16[128,128]{1,0:T(8,128)(2,1)S(1)}, bf16[128,128]{1,0:T(8,128)(2,1)S(1)}, u32[]{:S(2)}, u32[]{:S(2)}) collective-permute-start(bf16[128,128]{1,0:T(8,128)(2,1)S(1)} %get-tuple-element.90), channel_id=1, source_target_pairs={{0,24},{8,0},{16,8},{24,16},{1,25},{9,1},{17,9},{25,17},{2,26},{10... | collective-permute-start | bytes 98312 | tf_op jit(solution)/shard_map/ppermute | solution.py:23
  89.2 0.6 collective-permute-done.21
  89.9 0.4 collective-permute-done.22
  90.3 0.5 collective-permute-done.23
  91.0 5.2 %collective-permute-start.24 = (bf16[4,80,128]{2,1,0:T(8,128)(2,1)S(1)}, bf16[4,80,128]{2,1,0:T(8,128)(2,1)S(1)}, u32[]{:S(2)}, u32[]{:S(2)}) collective-permute-start(bf16[4,80,128]{2,1,0:T(8,128)(2,1)S(1)} %get-tuple-element.59), channel_id=1, source_target_pairs={{0,1},{1,0},{2,3},{3,2},{4,5},{5,4},{6,7},{7,6},{8,9},{9,8},{10,11... | collective-permute-start | bytes 245768 | tf_op jit(solution)/shard_map/ppermute | solution.py:23
  96.3 0.9 collective-permute-done.24
  97.1 0.1 fusion.9
  97.2 0.2 copy.45
  97.4 0.1 slice.154
  97.6 0.1 copy.49
  97.8 1.2 %collective-permute-start.25 = (bf16[56,1024]{1,0:T(8,128)(2,1)S(1)}, bf16[56,1024]{1,0:T(8,128)(2,1)S(1)}, u32[]{:S(2)}, u32[]{:S(2)}) collective-permute-start(bf16[56,1024]{1,0:T(8,128)(2,1)S(1)} %get-tuple-element.70), channel_id=1, source_target_pairs={{0,32},{32,64},{64,96},{96,0},{1,33},{33,65},{65,97},{97,1},{2,34}... | collective-permute-start | bytes 344072 | tf_op jit(solution)/shard_map/ppermute | solution.py:23
  98.9 2.6 %collective-permute-start.26 = (bf16[56,1024]{1,0:T(8,128)(2,1)S(1)}, bf16[56,1024]{1,0:T(8,128)(2,1)S(1)}, u32[]{:S(2)}, u32[]{:S(2)}) collective-permute-start(bf16[56,1024]{1,0:T(8,128)(2,1)S(1)} %get-tuple-element.70), channel_id=1, source_target_pairs={{0,64},{32,96},{64,0},{96,32},{1,65},{33,97},{65,1},{97,33},{2,66}... | collective-permute-start | bytes 344072 | tf_op jit(solution)/shard_map/ppermute | solution.py:23
  101.6 1.8 %collective-permute-start.27 = (bf16[56,1024]{1,0:T(8,128)(2,1)S(1)}, bf16[56,1024]{1,0:T(8,128)(2,1)S(1)}, u32[]{:S(2)}, u32[]{:S(2)}) collective-permute-start(bf16[56,1024]{1,0:T(8,128)(2,1)S(1)} %get-tuple-element.70), channel_id=1, source_target_pairs={{0,96},{32,0},{64,32},{96,64},{1,97},{33,1},{65,33},{97,65},{2,98}... | collective-permute-start | bytes 344072 | tf_op jit(solution)/shard_map/ppermute | solution.py:23
  103.3 0.4 copy.46
  103.7 0.3 slice.133.sums_ref
  104.0 1.6 %copy-done.1 = bf16[1024,1024]{1,0:T(8,128)(2,1)S(1)} copy-done((bf16[1024,1024]{1,0:T(8,128)(2,1)S(1)}, bf16[1024,1024]{1,0:T(8,128)(2,1)}, u32[]{:S(2)}) %copy-start.1) | copy-done | bytes 2097176
  105.6 1.6 %copy-done.2 = bf16[1024,1024]{1,0:T(8,128)(2,1)S(1)} copy-done((bf16[1024,1024]{1,0:T(8,128)(2,1)S(1)}, bf16[1024,1024]{1,0:T(8,128)(2,1)}, u32[]{:S(2)}) %copy-start.2) | copy-done | bytes 2097176
  107.2 1.9 %shard_map.138 = f32[16,1024]{1,0:T(8,128)} custom-call(bf16[32,1024]{1,0:T(8,128)(2,1)S(1)} %slice.133.sums_ref, bf16[16,1024]{1,0:T(8,128)(2,1)S(1)} %bitcast.108, bf16[1024,1024]{1,0:T(8,128)(2,1)S(1)} %copy-done.2, bf16[1024,1024]{1,0:T(8,128)(2,1)S(1)} %copy-done.1), custom_call_target="tpu_custom_call" | custom-call | flops 70000000 | bytes 4300000 | tf_op jit(solution)/shard_map/pallas_call | solution.py:177
  109.2 0.8 fusion
  110.1 0.7 maximum_convert_fusion.1
  110.8 0.1 copy.50
  110.9 0.7 copy.52
  (69 shorter events, 0.8 us)
Async XLA Ops:
  0.6 44.3 %copy-start = (bf16[1024,1024]{1,0:T(8,128)(2,1)S(1)}, bf16[1024,1024]{1,0:T(8,128)(2,1)}, u32[]{:S(2)}) copy-start(bf16[1024,1024]{1,0:T(8,128)(2,1)} %param.18) | copy-start | bytes 6291460
  3.4 18.4 %collective-permute-start.3 = (bf16[800,128]{1,0:T(8,128)(2,1)S(1)}, bf16[800,128]{1,0:T(8,128)(2,1)S(1)}, u32[]{:S(2)}, u32[]{:S(2)}) collective-permute-start(bf16[800,128]{1,0:T(8,128)(2,1)S(1)} %get-tuple-element.56), channel_id=1, source_target_pairs={{0,16},{8,24},{16,0},{24,8},{1,17},{9,25},{17,1},{25,9},{2,18},{10... | collective-permute-start | bytes 614408 | tf_op jit(solution)/shard_map/ppermute | solution.py:23
  7.8 9.3 %collective-permute-start = (bf16[2,16,1024]{2,1,0:T(8,128)(2,1)S(1)}, bf16[2,16,1024]{2,1,0:T(8,128)(2,1)S(1)}, u32[]{:S(2)}, u32[]{:S(2)}) collective-permute-start(bf16[2,16,1024]{2,1,0:T(8,128)(2,1)S(1)} %bitcast.116), channel_id=1, source_target_pairs={{0,6},{2,0},{4,2},{6,4},{1,7},{3,1},{5,3},{7,5},{8,14},{10,8},{12,... | collective-permute-start | bytes 196616 | tf_op jit(solution)/shard_map/ppermute | solution.py:23
  13.9 7.2 %collective-permute-start.1 = (bf16[2,16,1024]{2,1,0:T(8,128)(2,1)S(1)}, bf16[2,16,1024]{2,1,0:T(8,128)(2,1)S(1)}, u32[]{:S(2)}, u32[]{:S(2)}) collective-permute-start(bf16[2,16,1024]{2,1,0:T(8,128)(2,1)S(1)} %bitcast.117), channel_id=1, source_target_pairs={{0,4},{2,6},{4,0},{6,2},{1,5},{3,7},{5,1},{7,3},{8,12},{10,14},{12... | collective-permute-start | bytes 196616 | tf_op jit(solution)/shard_map/ppermute | solution.py:23
  14.8 6.9 %collective-permute-start.2 = (bf16[2,16,1024]{2,1,0:T(8,128)(2,1)S(1)}, bf16[2,16,1024]{2,1,0:T(8,128)(2,1)S(1)}, u32[]{:S(2)}, u32[]{:S(2)}) collective-permute-start(bf16[2,16,1024]{2,1,0:T(8,128)(2,1)S(1)} %bitcast.118), channel_id=1, source_target_pairs={{0,2},{2,4},{4,6},{6,0},{1,3},{3,5},{5,7},{7,1},{8,10},{10,12},{12... | collective-permute-start | bytes 196616 | tf_op jit(solution)/shard_map/ppermute | solution.py:23
  21.8 5.3 %collective-permute-start.4 = (bf16[4,2,16,1024]{3,2,1,0:T(8,128)(2,1)S(1)}, bf16[4,2,16,1024]{3,2,1,0:T(8,128)(2,1)S(1)}, u32[]{:S(2)}, u32[]{:S(2)}) collective-permute-start(bf16[4,2,16,1024]{3,2,1,0:T(8,128)(2,1)S(1)} %get-tuple-element.54), channel_id=1, source_target_pairs={{0,24},{8,0},{16,8},{24,16},{1,25},{9,1},{17,9},{25,17},{2,26},{10... | collective-permute-start | bytes 786440 | tf_op jit(solution)/shard_map/ppermute | solution.py:23
  22.8 6.8 %collective-permute-start.5 = (bf16[4,2,16,1024]{3,2,1,0:T(8,128)(2,1)S(1)}, bf16[4,2,16,1024]{3,2,1,0:T(8,128)(2,1)S(1)}, u32[]{:S(2)}, u32[]{:S(2)}) collective-permute-start(bf16[4,2,16,1024]{3,2,1,0:T(8,128)(2,1)S(1)} %get-tuple-element.54), channel_id=1, source_target_pairs={{0,16},{8,24},{16,0},{24,8},{1,17},{9,25},{17,1},{25,9},{2,18},{10... | collective-permute-start | bytes 786440 | tf_op jit(solution)/shard_map/ppermute | solution.py:23
  24.0 13.3 %collective-permute-start.6 = (bf16[4,2,16,1024]{3,2,1,0:T(8,128)(2,1)S(1)}, bf16[4,2,16,1024]{3,2,1,0:T(8,128)(2,1)S(1)}, u32[]{:S(2)}, u32[]{:S(2)}) collective-permute-start(bf16[4,2,16,1024]{3,2,1,0:T(8,128)(2,1)S(1)} %get-tuple-element.54), channel_id=1, source_target_pairs={{0,8},{8,16},{16,24},{24,0},{1,9},{9,17},{17,25},{25,1},{2,10},{10... | collective-permute-start | bytes 786440 | tf_op jit(solution)/shard_map/ppermute | solution.py:23
  24.0 15.7 %collective-permute-start.8 = (bf16[800,128]{1,0:T(8,128)(2,1)S(1)}, bf16[800,128]{1,0:T(8,128)(2,1)S(1)}, u32[]{:S(2)}, u32[]{:S(2)}) collective-permute-start(bf16[800,128]{1,0:T(8,128)(2,1)S(1)} %get-tuple-element.56), channel_id=1, source_target_pairs={{0,24},{8,0},{16,8},{24,16},{1,25},{9,1},{17,9},{25,17},{2,26},{10... | collective-permute-start | bytes 614408 | tf_op jit(solution)/shard_map/ppermute | solution.py:23
  26.7 15.0 %collective-permute-start.9 = (bf16[800,128]{1,0:T(8,128)(2,1)S(1)}, bf16[800,128]{1,0:T(8,128)(2,1)S(1)}, u32[]{:S(2)}, u32[]{:S(2)}) collective-permute-start(bf16[800,128]{1,0:T(8,128)(2,1)S(1)} %get-tuple-element.56), channel_id=1, source_target_pairs={{0,8},{8,16},{16,24},{24,0},{1,9},{9,17},{17,25},{25,1},{2,10},{10... | collective-permute-start | bytes 614408 | tf_op jit(solution)/shard_map/ppermute | solution.py:23
  37.4 8.9 %collective-permute-start.7 = (bf16[4,4,2,16,1024]{4,3,2,1,0:T(8,128)(2,1)S(1)}, bf16[4,4,2,16,1024]{4,3,2,1,0:T(8,128)(2,1)}, u32[]{:S(2)}, u32[]{:S(2)}) collective-permute-start(bf16[4,4,2,16,1024]{4,3,2,1,0:T(8,128)(2,1)S(1)} %pad_maximum_fusion.mine_ref), channel_id=1, source_target_pairs={{0,1},{1,0},{2,3},{3,2},{4,5},{5,4},{6,7},{7,6},{8,9},{9,8},{10,11... | collective-permute-start | bytes 3145736 | tf_op jit(solution)/shard_map/ppermute | solution.py:23
  42.7 3.6 %collective-permute-start.10 = (bf16[4,800,128]{2,1,0:T(8,128)(2,1)}, bf16[4,800,128]{2,1,0:T(8,128)(2,1)}, u32[]{:S(2)}, u32[]{:S(2)}) collective-permute-start(bf16[4,800,128]{2,1,0:T(8,128)(2,1)} %pad_maximum_fusion.1.edge_mine_ref), channel_id=1, source_target_pairs={{0,1},{1,0},{2,3},{3,2},{4,5},{5,4},{6,7},{7,6},{8,9},{9,8},{10,11... | collective-permute-start | bytes 2457608 | tf_op jit(solution)/shard_map/ppermute | solution.py:23
  57.6 0.6 copy-start.4
  58.2 9.8 %collective-permute-start.11 = (bf16[800,128]{1,0:T(8,128)(2,1)}, bf16[800,128]{1,0:T(8,128)(2,1)S(1)}, u32[]{:S(2)}, u32[]{:S(2)}) collective-permute-start(bf16[800,128]{1,0:T(8,128)(2,1)} %get-tuple-element.32), channel_id=1, source_target_pairs={{0,32},{32,64},{64,96},{96,0},{1,33},{33,65},{65,97},{97,1},{2,34}... | collective-permute-start | bytes 614408 | tf_op jit(solution)/shard_map/ppermute | solution.py:23
  59.5 12.1 %collective-permute-start.12 = (bf16[800,128]{1,0:T(8,128)(2,1)}, bf16[800,128]{1,0:T(8,128)(2,1)S(1)}, u32[]{:S(2)}, u32[]{:S(2)}) collective-permute-start(bf16[800,128]{1,0:T(8,128)(2,1)} %get-tuple-element.33), channel_id=1, source_target_pairs={{0,64},{32,96},{64,0},{96,32},{1,65},{33,97},{65,1},{97,33},{2,66}... | collective-permute-start | bytes 614408 | tf_op jit(solution)/shard_map/ppermute | solution.py:23
  62.1 9.5 %collective-permute-start.13 = (bf16[800,128]{1,0:T(8,128)(2,1)}, bf16[800,128]{1,0:T(8,128)(2,1)S(1)}, u32[]{:S(2)}, u32[]{:S(2)}) collective-permute-start(bf16[800,128]{1,0:T(8,128)(2,1)} %get-tuple-element.34), channel_id=1, source_target_pairs={{0,96},{32,0},{64,32},{96,64},{1,97},{33,1},{65,33},{97,65},{2,98}... | collective-permute-start | bytes 614408 | tf_op jit(solution)/shard_map/ppermute | solution.py:23
  63.2 13.6 %collective-permute-start.17 = (bf16[4,2,2,16,128]{4,3,2,1,0:T(8,128)(2,1)}, bf16[4,2,2,16,128]{4,3,2,1,0:T(8,128)(2,1)S(1)}, u32[]{:S(2)}, u32[]{:S(2)}) collective-permute-start(bf16[4,2,2,16,128]{4,3,2,1,0:T(8,128)(2,1)} %copy-done.4), channel_id=1, source_target_pairs={{0,2},{2,4},{4,6},{6,0},{1,3},{3,5},{5,7},{7,1},{8,10},{10,12},{12... | collective-permute-start | bytes 196616 | tf_op jit(solution)/shard_map/ppermute | solution.py:23
  63.8 16.5 %collective-permute-start.18 = (bf16[4,2,2,16,128]{4,3,2,1,0:T(8,128)(2,1)S(1)}, bf16[4,2,2,16,128]{4,3,2,1,0:T(8,128)(2,1)S(1)}, u32[]{:S(2)}, u32[]{:S(2)}) collective-permute-start(bf16[4,2,2,16,128]{4,3,2,1,0:T(8,128)(2,1)S(1)} %get-tuple-element.37), channel_id=1, source_target_pairs={{0,4},{2,6},{4,0},{6,2},{1,5},{3,7},{5,1},{7,3},{8,12},{10,14},{12... | collective-permute-start | bytes 196616 | tf_op jit(solution)/shard_map/ppermute | solution.py:23
  68.0 12.3 %collective-permute-start.19 = (bf16[4,2,2,16,128]{4,3,2,1,0:T(8,128)(2,1)S(1)}, bf16[4,2,2,16,128]{4,3,2,1,0:T(8,128)(2,1)S(1)}, u32[]{:S(2)}, u32[]{:S(2)}) collective-permute-start(bf16[4,2,2,16,128]{4,3,2,1,0:T(8,128)(2,1)S(1)} %get-tuple-element.38), channel_id=1, source_target_pairs={{0,6},{2,0},{4,2},{6,4},{1,7},{3,1},{5,3},{7,5},{8,14},{10,8},{12,... | collective-permute-start | bytes 196616 | tf_op jit(solution)/shard_map/ppermute | solution.py:23
  71.9 8.5 %collective-permute-start.14 = (bf16[224,128]{1,0:T(8,128)(2,1)S(1)}, bf16[224,128]{1,0:T(8,128)(2,1)S(1)}, u32[]{:S(2)}, u32[]{:S(2)}) collective-permute-start(bf16[224,128]{1,0:T(8,128)(2,1)S(1)} %get-tuple-element.92), channel_id=1, source_target_pairs={{0,2},{2,4},{4,6},{6,0},{1,3},{3,5},{5,7},{7,1},{8,10},{10,12},{12... | collective-permute-start | bytes 172040 | tf_op jit(solution)/shard_map/ppermute | solution.py:23
  72.5 8.1 %collective-permute-start.15 = (bf16[224,128]{1,0:T(8,128)(2,1)S(1)}, bf16[224,128]{1,0:T(8,128)(2,1)S(1)}, u32[]{:S(2)}, u32[]{:S(2)}) collective-permute-start(bf16[224,128]{1,0:T(8,128)(2,1)S(1)} %get-tuple-element.93), channel_id=1, source_target_pairs={{0,4},{2,6},{4,0},{6,2},{1,5},{3,7},{5,1},{7,3},{8,12},{10,14},{12... | collective-permute-start | bytes 172040 | tf_op jit(solution)/shard_map/ppermute | solution.py:23
  76.8 5.2 %collective-permute-start.16 = (bf16[224,128]{1,0:T(8,128)(2,1)S(1)}, bf16[224,128]{1,0:T(8,128)(2,1)S(1)}, u32[]{:S(2)}, u32[]{:S(2)}) collective-permute-start(bf16[224,128]{1,0:T(8,128)(2,1)S(1)} %get-tuple-element.91), channel_id=1, source_target_pairs={{0,6},{2,0},{4,2},{6,4},{1,7},{3,1},{5,3},{7,5},{8,14},{10,8},{12,... | collective-permute-start | bytes 172040 | tf_op jit(solution)/shard_map/ppermute | solution.py:23
  82.1 3.6 %collective-permute-start.20 = (bf16[224,128]{1,0:T(8,128)(2,1)S(1)}, bf16[224,128]{1,0:T(8,128)(2,1)S(1)}, u32[]{:S(2)}, u32[]{:S(2)}) collective-permute-start(bf16[224,128]{1,0:T(8,128)(2,1)S(1)} %pad_maximum_fusion.19), channel_id=1, source_target_pairs={{0,128},{128,0},{1,129},{129,1},{2,130},{130,2},{3,131},{131,3},{4... | collective-permute-start | bytes 172040 | tf_op jit(solution)/shard_map/ppermute | solution.py:23
  85.8 4.1 %collective-permute-start.21 = (bf16[128,128]{1,0:T(8,128)(2,1)S(1)}, bf16[128,128]{1,0:T(8,128)(2,1)S(1)}, u32[]{:S(2)}, u32[]{:S(2)}) collective-permute-start(bf16[128,128]{1,0:T(8,128)(2,1)S(1)} %get-tuple-element.88), channel_id=1, source_target_pairs={{0,8},{8,16},{16,24},{24,0},{1,9},{9,17},{17,25},{25,1},{2,10},{10... | collective-permute-start | bytes 98312 | tf_op jit(solution)/shard_map/ppermute | solution.py:23
  85.9 4.4 %collective-permute-start.22 = (bf16[128,128]{1,0:T(8,128)(2,1)S(1)}, bf16[128,128]{1,0:T(8,128)(2,1)S(1)}, u32[]{:S(2)}, u32[]{:S(2)}) collective-permute-start(bf16[128,128]{1,0:T(8,128)(2,1)S(1)} %get-tuple-element.89), channel_id=1, source_target_pairs={{0,16},{8,24},{16,0},{24,8},{1,17},{9,25},{17,1},{25,9},{2,18},{10... | collective-permute-start | bytes 98312 | tf_op jit(solution)/shard_map/ppermute | solution.py:23
  87.4 3.3 %collective-permute-start.23 = (bf16[128,128]{1,0:T(8,128)(2,1)S(1)}, bf16[128,128]{1,0:T(8,128)(2,1)S(1)}, u32[]{:S(2)}, u32[]{:S(2)}) collective-permute-start(bf16[128,128]{1,0:T(8,128)(2,1)S(1)} %get-tuple-element.90), channel_id=1, source_target_pairs={{0,24},{8,0},{16,8},{24,16},{1,25},{9,1},{17,9},{25,17},{2,26},{10... | collective-permute-start | bytes 98312 | tf_op jit(solution)/shard_map/ppermute | solution.py:23
  90.9 13.1 %copy-start.3 = (bf16[1,16,1024]{2,1,0:T(8,128)(2,1)S(1)}, bf16[1,16,1024]{2,1,0:T(8,128)(2,1)}, u32[]{:S(2)}) copy-start(bf16[1,16,1024]{2,1,0:T(8,128)(2,1)} %param.11) | copy-start | bytes 98308
  91.0 6.2 %collective-permute-start.24 = (bf16[4,80,128]{2,1,0:T(8,128)(2,1)S(1)}, bf16[4,80,128]{2,1,0:T(8,128)(2,1)S(1)}, u32[]{:S(2)}, u32[]{:S(2)}) collective-permute-start(bf16[4,80,128]{2,1,0:T(8,128)(2,1)S(1)} %get-tuple-element.59), channel_id=1, source_target_pairs={{0,1},{1,0},{2,3},{3,2},{4,5},{5,4},{6,7},{7,6},{8,9},{9,8},{10,11... | collective-permute-start | bytes 245768 | tf_op jit(solution)/shard_map/ppermute | solution.py:23
  97.8 11.4 %collective-permute-start.25 = (bf16[56,1024]{1,0:T(8,128)(2,1)S(1)}, bf16[56,1024]{1,0:T(8,128)(2,1)S(1)}, u32[]{:S(2)}, u32[]{:S(2)}) collective-permute-start(bf16[56,1024]{1,0:T(8,128)(2,1)S(1)} %get-tuple-element.70), channel_id=1, source_target_pairs={{0,32},{32,64},{64,96},{96,0},{1,33},{33,65},{65,97},{97,1},{2,34}... | collective-permute-start | bytes 344072 | tf_op jit(solution)/shard_map/ppermute | solution.py:23
  98.9 10.2 %collective-permute-start.26 = (bf16[56,1024]{1,0:T(8,128)(2,1)S(1)}, bf16[56,1024]{1,0:T(8,128)(2,1)S(1)}, u32[]{:S(2)}, u32[]{:S(2)}) collective-permute-start(bf16[56,1024]{1,0:T(8,128)(2,1)S(1)} %get-tuple-element.70), channel_id=1, source_target_pairs={{0,64},{32,96},{64,0},{96,32},{1,65},{33,97},{65,1},{97,33},{2,66}... | collective-permute-start | bytes 344072 | tf_op jit(solution)/shard_map/ppermute | solution.py:23
  101.6 7.6 %collective-permute-start.27 = (bf16[56,1024]{1,0:T(8,128)(2,1)S(1)}, bf16[56,1024]{1,0:T(8,128)(2,1)S(1)}, u32[]{:S(2)}, u32[]{:S(2)}) collective-permute-start(bf16[56,1024]{1,0:T(8,128)(2,1)S(1)} %get-tuple-element.70), channel_id=1, source_target_pairs={{0,96},{32,0},{64,32},{96,64},{1,97},{33,1},{65,33},{97,65},{2,98}... | collective-permute-start | bytes 344072 | tf_op jit(solution)/shard_map/ppermute | solution.py:23
  104.0 1.6 %copy-start.1 = (bf16[1024,1024]{1,0:T(8,128)(2,1)S(1)}, bf16[1024,1024]{1,0:T(8,128)(2,1)}, u32[]{:S(2)}) copy-start(bf16[1024,1024]{1,0:T(8,128)(2,1)} %wt_ref.1) | copy-start | bytes 6291460
  105.6 1.6 %copy-start.2 = (bf16[1024,1024]{1,0:T(8,128)(2,1)S(1)}, bf16[1024,1024]{1,0:T(8,128)(2,1)}, u32[]{:S(2)}) copy-start(bf16[1024,1024]{1,0:T(8,128)(2,1)} %ws_ref.1) | copy-start | bytes 6291460

commit v2 on v1

--- a/solution.py
+++ b/solution.py
@@ -48,34 +48,14 @@
     return array.reshape(lead, 4, 2, 4, 32).transpose(0, 1, 3, 2, 4).reshape(lead, 1024)
 
 
-def edge_kernel(
-    at_ref, mine_ref, sib_ref, edge_mine_ref, edge_sib_ref, ws, wt, wo, wr,
-    *refs
-):
-    sums_refs, grad_refs = refs[:4], refs[4:8]
-    grads_ref, embed, cotan, p_s, p_tq, w_r, acc_s, acc_t, acc_r = refs[8:]
+def edge_blocks(at_ref, refs, p_s, p_tq, w_r, acc_s, acc_t, acc_r):
     my_y, my_x, my_z, my_c = (at_ref[i] for i in range(4))
-
-    def own(rows):
-        parts = rows.reshape(4, 2, 32, rows.shape[1])
-        return jnp.where(my_c == 0, parts[:, 0], parts[:, 1]).reshape(128, rows.shape[1])
-
-    for half, ref in enumerate((mine_ref, sib_ref)):
-        rows = pl.ds(half * 256, 256)
-        embed[rows] = ref[:, :, 0].reshape(256, 1024)
-        cotan[rows] = ref[:, :, 1].reshape(256, 1024)
-    acc_s[...] = jnp.zeros_like(acc_s)
-    acc_t[...] = jnp.zeros_like(acc_t)
-    acc_r[...] = jnp.zeros_like(acc_r)
-    p_s[...] = own(dot(embed[...], ws[...]).T).astype(BF)
-    p_tq[:128] = own(dot(embed[...], wt[...]).T).astype(BF)
-    p_tq[128:] = dot(own(wo[...]), cotan[...], ((1,), (1,))).astype(BF)
-    w_r[...] = own(wr[...].astype(F32).T).astype(BF)
     spot = lax.broadcasted_iota(jnp.int32, (512, 768), 0).astype(jnp.int16)
 
-    def block(ref, i):
-        radial = ref[i, :768]
-        coded = ref[i, 768:].astype(F32)
+    for i in range(4):
+        edges = refs[i % 2][i // 2]
+        radial = edges[:768]
+        coded = edges[768:].astype(F32)
         node = (coded[:12] * 16.0 + coded[12:24]).astype(jnp.int32) - 1
         far_z = ((node >> 5) - my_z) & 3
         far_x = ((node >> 7) - my_x) & 3
@@ -108,9 +88,41 @@
         acc_s[...] += dot(grad_pre, hot_n(0))
         acc_r[...] += dot(grad_rad, radial)
 
-    for i in range(4):
-        block(edge_mine_ref, i)
-        block(edge_sib_ref, i)
+
+def first_kernel(
+    at_ref, mine_ref, sib_ref, edge_ref, edge_sib_ref, ws, wt, wo, wr,
+    embed, cotan, p_s, p_tq, w_r, acc_s, acc_t, acc_r
+):
+    my_c = at_ref[3]
+
+    def own(rows):
+        parts = rows.reshape(4, 2, 32, rows.shape[1])
+        return jnp.where(my_c == 0, parts[:, 0], parts[:, 1]).reshape(128, rows.shape[1])
+
+    for half, ref in enumerate((mine_ref, sib_ref)):
+        rows = pl.ds(half * 256, 256)
+        embed[rows] = ref[:, :, 0].reshape(256, 1024)
+        cotan[rows] = ref[:, :, 1].reshape(256, 1024)
+    acc_s[...] = jnp.zeros_like(acc_s)
+    acc_t[...] = jnp.zeros_like(acc_t)
+    acc_r[...] = jnp.zeros_like(acc_r)
+    p_s[...] = own(dot(embed[...], ws[...]).T).astype(BF)
+    p_tq[:128] = own(dot(embed[...], wt[...]).T).astype(BF)
+    p_tq[128:] = dot(own(wo[...]), cotan[...], ((1,), (1,))).astype(BF)
+    w_r[...] = own(wr[...].astype(F32).T).astype(BF)
+    edge_blocks(at_ref, (edge_ref, edge_sib_ref), p_s, p_tq, w_r, acc_s, acc_t, acc_r)
+
+
+def second_kernel(
+    at_ref, edge_ref, edge_sib_ref, embed, cotan, p_s, p_tq, w_r, in_s, in_t, in_r, *refs
+):
+    sums_refs, grad_refs = refs[:4], refs[4:8]
+    grads_ref, acc_s, acc_t, acc_r = refs[8:]
+    my_y, my_x, my_z, my_c = (at_ref[i] for i in range(4))
+    acc_s[...] = in_s[...]
+    acc_t[...] = in_t[...]
+    acc_r[...] = in_r[...]
+    edge_blocks(at_ref, (edge_ref, edge_sib_ref), p_s, p_tq, w_r, acc_s, acc_t, acc_r)
 
     for mat, flat in enumerate((acc_s[...], acc_t[128:])):
         nodes = flat.T.astype(BF)
@@ -140,30 +152,43 @@
         grad_refs[o][...] = grads_ref[o]
 
 
-def edge_pass(at, mine, sib, edge_mine, edge_sib, ws, wt, wo, wr):
+def edge_pass(at, mine, sib, early, early_sib, late, late_sib, ws, wt, wo, wr):
+    smem = pl.BlockSpec(memory_space=pltpu.SMEM)
     vmem = pl.BlockSpec(memory_space=pltpu.VMEM)
+    half = pl.CostEstimate(
+        flops=3_000_000_000, bytes_accessed=4_000_000, transcendentals=800_000
+    )
+    accumulators = [
+        jax.ShapeDtypeStruct((128, 512), F32),
+        jax.ShapeDtypeStruct((256, 512), F32),
+        jax.ShapeDtypeStruct((128, 128), F32),
+    ]
+    state = pl.pallas_call(
+        first_kernel,
+        in_specs=[smem] + [vmem] * 8,
+        out_specs=[vmem] * 8,
+        out_shape=[
+            jax.ShapeDtypeStruct((512, 1024), BF),
+            jax.ShapeDtypeStruct((512, 1024), BF),
+            jax.ShapeDtypeStruct((128, 512), BF),
+            jax.ShapeDtypeStruct((256, 512), BF),
+            jax.ShapeDtypeStruct((128, 128), BF),
+        ]
+        + accumulators,
+        compiler_params=pltpu.CompilerParams(vmem_limit_bytes=16 * 1024 * 1024),
+        cost_estimate=half,
+    )(at, mine, sib, early, early_sib, ws, wt, wo, wr)
     return pl.pallas_call(
-        edge_kernel,
-        in_specs=[pl.BlockSpec(memory_space=pltpu.SMEM)] + [vmem] * 8,
+        second_kernel,
+        in_specs=[smem] + [vmem] * 10,
         out_specs=[vmem] * 8,
         out_shape=[jax.ShapeDtypeStruct((4, 2, 2, 16, 128), BF)] * 4
         + [jax.ShapeDtypeStruct((800, 128), BF)] * 4,
-        scratch_shapes=[
-            pltpu.VMEM((4, 800, 128), BF),
-            pltpu.VMEM((512, 1024), BF),
-            pltpu.VMEM((512, 1024), BF),
-            pltpu.VMEM((128, 512), BF),
-            pltpu.VMEM((256, 512), BF),
-            pltpu.VMEM((128, 128), BF),
-            pltpu.VMEM((128, 512), F32),
-            pltpu.VMEM((256, 512), F32),
-            pltpu.VMEM((128, 128), F32),
-        ],
+        scratch_shapes=[pltpu.VMEM((4, 800, 128), BF)]
+        + [pltpu.VMEM(leaf.shape, leaf.dtype) for leaf in accumulators],
         compiler_params=pltpu.CompilerParams(vmem_limit_bytes=16 * 1024 * 1024),
-        cost_estimate=pl.CostEstimate(
-            flops=6_000_000_000, bytes_accessed=8_000_000, transcendentals=1_600_000
-        ),
-    )(at, mine, sib, edge_mine, edge_sib, ws, wt, wo, wr)
+        cost_estimate=half,
+    )(at, late, late_sib, *state)
 
 
 def node_kernel(sums_ref, cotan_ref, ws_ref, wt_ref, out_ref):
@@ -199,17 +224,19 @@
     edges = jnp.concatenate([radial[0], ids, jnp.zeros((8, 128), BF)])
     edges = gather_from(edges, "x")
     nodes, edges[2] = lax.optimization_barrier((nodes, edges[2]))
-    edges = jnp.stack(edges)
-    edge_sib = send(edges, "core", 1)
+    early, late = jnp.stack([edges[0], edges[2]]), jnp.stack([edges[1], edges[3]])
+    early_sib = send(early, "core", 1)
     nodes = jnp.stack(gather_from(jnp.stack(nodes), "x"))
 
     def mine(weight, axis):
         return lax.dynamic_slice_in_dim(weight, my_x * 256, 256, axis)
 
     weights = (mine(w_source, 1), mine(w_target, 1), mine(w_out, 0), mine(w_radial, 1))
+    nodes, late, early_sib = lax.optimization_barrier((nodes, late, early_sib))
     node_sib = send(nodes, "core", 1)
+    late_sib = send(late, "core", 1)
     at = jnp.stack([my_y, my_x, my_z, my_c]).astype(jnp.int32)
-    out = edge_pass(at, nodes, node_sib, edges, edge_sib, *weights)
+    out = edge_pass(at, nodes, node_sib, early, early_sib, late, late_sib, *weights)
     sums, grads = out[:4], out[4:]
 
     y_parts = trade(grads, "y")

time: 112 us -> 109 us (0.973)
  starting transfers between devices: 59.5 us -> 52.5 us
  waiting for transfers between devices: 22.9 us -> 26.4 us
    ppermute x28 -> x29, starting transfers between devices: 59.5 us -> 52.5 us  [send(): lax.ppermute(array, axis, [(i, (i + offset) % size) for i in range(size)])]
    ppermute x28 -> x29, waiting for transfers between devices: 22.9 us -> 26.4 us  [send(): lax.ppermute(array, axis, [(i, (i + offset) % size) for i in range(size)])]
    pallas_call x1 -> x2, Pallas kernels: 11.3 us -> 10.8 us  [the longest x1 5.92 us: edge_pass(): pl.pallas_call(first_kernel, in_specs=[smem] + [vmem] * 8, out_specs=[vme...]
    another operation x4 -> x5, other arithmetic: 2.85 us -> 2.68 us  [the longest x2 1.14 us: per_device(): jnp.stack([edges[0], edges[2]])]
    unnamed x11 -> x15, local copies, waits for them, and re-layouts: 4.5 us -> 4.66 us
  transfers between devices with their start and end apart: 28 -> 29, of which waited for: 13 -> 13; matrix products, arithmetic and copies ran while one was open for 5% -> 6% of each run, Pallas kernels for 2% -> 7%
where the time goes in v2:
time: 109 us
  starting transfers between devices  52.5 us (48%)
  waiting for transfers between devices  26.4 us (24%)
  Pallas kernels  12.6 us (12%)
  local copies, waits for them, and re-layouts  8.47 us (8%)
  other arithmetic  6.8 us (6%)
  between operations  1.91 us (2%)
    ppermute x29, starting transfers between devices, send(): lax.ppermute(array, axis, [(i, (i + offset) % size) for i in range(size)])  52.5 us
    ppermute x29, waiting for transfers between devices, send(): lax.ppermute(array, axis, [(i, (i + offset) % size) for i in range(size)])  26.4 us
    pallas_call x1, Pallas kernels, edge_pass(): pl.pallas_call(first_kernel, in_specs=[smem] + [vmem] * 8, out_specs=[vme...  5.92 us
    pallas_call x1, Pallas kernels, edge_pass(): pl.pallas_call(second_kernel, in_specs=[smem] + [vmem] * 10, out_specs=[v...  4.83 us
    unnamed x15, local copies, waits for them, and re-layouts  4.66 us
    dynamic_slice x3, local copies, waits for them, and re-layouts, mine(): return lax.dynamic_slice_in_dim(weight, my_x * 256, 256, axis)  2.23 us
  transfers between devices with their start and end apart: 29, of which 13 were waited for; matrix products, arithmetic and copies ran while one was open for 6% of the time, Pallas kernels for 7%

profile of v2, /device:TPU:1, one launch (start us, length us, event | category | flops | bytes accessed | tf_op | source)
XLA Modules:
  0.0 108.7 jit_solution(9470505968861258880)
XLA Ops:
  1.5 0.7 shift-right-arithmetic_convert_fusion
  2.3 1.1 %fusion.18 = (bf16[1,800,128]{2,1,0:T(8,128)(2,1)S(1)}, bf16[800,128]{1,0:T(8,128)(2,1)S(1)}) fusion(bf16[800]{0:T(1024)(128)(2,1)S(1)} %pad.72.clone, bf16[24,128]{1,0:T(8,128)(2,1)S(1)} %convert_element_type.76, bf16[768,128]{1,0:T(8,128)(2,1)} %bitcast.128), kind=kLoop, calls=%fused_computation.101 | loop fusion | flops 614400 | bytes 613952 | tf_op jit(solution)/shard_map/stack | solution.py:227
  3.4 3.7 %collective-permute-start.3 = (bf16[800,128]{1,0:T(8,128)(2,1)S(1)}, bf16[800,128]{1,0:T(8,128)(2,1)S(1)}, u32[]{:S(2)}, u32[]{:S(2)}) collective-permute-start(bf16[800,128]{1,0:T(8,128)(2,1)S(1)} %get-tuple-element.78), channel_id=1, source_target_pairs={{0,16},{8,24},{16,0},{24,8},{1,17},{9,25},{17,1},{25,9},{2,18},{10... | collective-permute-start | bytes 614408 | tf_op jit(solution)/shard_map/ppermute | solution.py:23
  7.1 0.8 pad_maximum_fusion.15
  7.8 6.0 %collective-permute-start = (bf16[2,16,1024]{2,1,0:T(8,128)(2,1)S(1)}, bf16[2,16,1024]{2,1,0:T(8,128)(2,1)S(1)}, u32[]{:S(2)}, u32[]{:S(2)}) collective-permute-start(bf16[2,16,1024]{2,1,0:T(8,128)(2,1)S(1)} %bitcast.116), channel_id=1, source_target_pairs={{0,6},{2,0},{4,2},{6,4},{1,7},{3,1},{5,3},{7,5},{8,14},{10,8},{12,... | collective-permute-start | bytes 196616 | tf_op jit(solution)/shard_map/ppermute | solution.py:23
  13.9 1.0 collective-permute-start.1
  14.8 2.3 %collective-permute-start.2 = (bf16[2,16,1024]{2,1,0:T(8,128)(2,1)S(1)}, bf16[2,16,1024]{2,1,0:T(8,128)(2,1)S(1)}, u32[]{:S(2)}, u32[]{:S(2)}) collective-permute-start(bf16[2,16,1024]{2,1,0:T(8,128)(2,1)S(1)} %bitcast.118), channel_id=1, source_target_pairs={{0,2},{2,4},{4,6},{6,0},{1,3},{3,5},{5,7},{7,1},{8,10},{10,12},{12... | collective-permute-start | bytes 196616 | tf_op jit(solution)/shard_map/ppermute | solution.py:23
  17.1 0.9 collective-permute-start.7
  18.0 0.6 collective-permute-start.8
  18.6 2.5 %collective-permute-done.1 = bf16[2,16,1024]{2,1,0:T(8,128)(2,1)S(1)} collective-permute-done((bf16[2,16,1024]{2,1,0:T(8,128)(2,1)S(1)}, bf16[2,16,1024]{2,1,0:T(8,128)(2,1)S(1)}, u32[]{:S(2)}, u32[]{:S(2)}) %collective-permute-start.1) | collective-permute-done | bytes 65568 | tf_op jit(solution)/shard_map/ppermute | solution.py:23
  21.1 0.7 collective-permute-done.2
  21.8 2.4 %collective-permute-start.9 = (bf16[2,800,128]{2,1,0:T(8,128)(2,1)S(1)}, bf16[2,800,128]{2,1,0:T(8,128)(2,1)S(1)}, u32[]{:S(2)}, u32[]{:S(2)}) collective-permute-start(bf16[2,800,128]{2,1,0:T(8,128)(2,1)S(1)} %pad_maximum_fusion.3.edge_ref), channel_id=1, source_target_pairs={{0,1},{1,0},{2,3},{3,2},{4,5},{5,4},{6,7},{7,6},{8,9},{9,8},{10,11... | collective-permute-start | bytes 1228808 | tf_op jit(solution)/shard_map/ppermute | solution.py:23
  24.2 0.9 collective-permute-start.4
  25.2 1.2 %collective-permute-start.5 = (bf16[4,2,16,1024]{3,2,1,0:T(8,128)(2,1)S(1)}, bf16[4,2,16,1024]{3,2,1,0:T(8,128)(2,1)S(1)}, u32[]{:S(2)}, u32[]{:S(2)}) collective-permute-start(bf16[4,2,16,1024]{3,2,1,0:T(8,128)(2,1)S(1)} %get-tuple-element.76), channel_id=1, source_target_pairs={{0,16},{8,24},{16,0},{24,8},{1,17},{9,25},{17,1},{25,9},{2,18},{10... | collective-permute-start | bytes 786440 | tf_op jit(solution)/shard_map/ppermute | solution.py:23
  26.4 0.8 pad_maximum_fusion.2.edge_ref
  27.2 5.0 %collective-permute-done.4 = bf16[4,2,16,1024]{3,2,1,0:T(8,128)(2,1)S(1)} collective-permute-done((bf16[4,2,16,1024]{3,2,1,0:T(8,128)(2,1)S(1)}, bf16[4,2,16,1024]{3,2,1,0:T(8,128)(2,1)S(1)}, u32[]{:S(2)}, u32[]{:S(2)}) %collective-permute-start.4) | collective-permute-done | bytes 262176 | tf_op jit(solution)/shard_map/ppermute | solution.py:23
  32.2 2.1 %collective-permute-done.5 = bf16[4,2,16,1024]{3,2,1,0:T(8,128)(2,1)S(1)} collective-permute-done((bf16[4,2,16,1024]{3,2,1,0:T(8,128)(2,1)S(1)}, bf16[4,2,16,1024]{3,2,1,0:T(8,128)(2,1)S(1)}, u32[]{:S(2)}, u32[]{:S(2)}) %collective-permute-start.5) | collective-permute-done | bytes 262176 | tf_op jit(solution)/shard_map/ppermute | solution.py:23
  34.3 6.2 %collective-permute-done.6 = bf16[4,2,16,1024]{3,2,1,0:T(8,128)(2,1)S(1)} collective-permute-done((bf16[4,2,16,1024]{3,2,1,0:T(8,128)(2,1)S(1)}, bf16[4,2,16,1024]{3,2,1,0:T(8,128)(2,1)S(1)}, u32[]{:S(2)}, u32[]{:S(2)}) %collective-permute-start.6) | collective-permute-done | bytes 262176 | tf_op jit(solution)/shard_map/ppermute | solution.py:23
  40.5 0.1 pad_maximum_fusion.mine_ref
  40.7 0.8 copy-done.5
  41.5 0.5 collective-permute-start.11
  42.0 0.9 constant_dynamic-slice_fusion.20.wr
  42.9 1.3 %constant_dynamic-slice_fusion.22 = (bf16[1024,256]{1,0:T(8,128)(2,1)S(1)}, bf16[1024,256]{1,0:T(8,128)(2,1)S(1)}) fusion(bf16[1024,1024]{1,0:T(8,128)(2,1)} %wt_ref.1, s32[]{:T(128)S(6)} %select_n.154, bf16[1024,1024]{1,0:T(8,128)(2,1)} %ws_ref.1), kind=kLoop, calls=%fused_computation.82 | loop fusion | bytes 2097156 | tf_op jit(solution)/shard_map/dynamic_slice | solution.py:232
  44.2 0.3 collective-permute-start.10
  44.6 5.9 %shard_map.137 = (bf16[512,1024]{1,0:T(8,128)(2,1)S(1)}, bf16[512,1024]{1,0:T(8,128)(2,1)S(1)}, bf16[128,512]{1,0:T(8,128)(2,1)S(1)}, bf16[256,512]{1,0:T(8,128)...) custom-call(s32[4]{0:T(128)S(1)} %pad_add_fusion.at_ref, ...), custom_call_target="tpu_custom_call" | custom-call | flops 3000000000 | bytes 4000000 | tf_op jit(solution)/shard_map/pallas_call | solution.py:166
  50.5 4.8 %shard_map.138 = (bf16[4,2,2,16,128]{4,3,2,1,0:T(8,128)(2,1)S(1)}, bf16[4,2,2,16,128]{4,3,2,1,0:T(8,128)(2,1)S(1)}, bf16[4,2,2,16,128]{4,3,2,1,0:T(8,128)(2,1)S(...) custom-call(s32[4]{0:T(128)S(1)} %pad_add_fusion.at_ref, ...), custom_call_target="tpu_custom_call" | custom-call | flops 3000000000 | bytes 4000000 | tf_op jit(solution)/shard_map/pallas_call | solution.py:181
  55.4 1.4 %collective-permute-start.12 = (bf16[800,128]{1,0:T(8,128)(2,1)S(1)}, bf16[800,128]{1,0:T(8,128)(2,1)S(1)}, u32[]{:S(2)}, u32[]{:S(2)}) collective-permute-start(bf16[800,128]{1,0:T(8,128)(2,1)S(1)} %get-tuple-element.54), channel_id=1, source_target_pairs={{0,32},{32,64},{64,96},{96,0},{1,33},{33,65},{65,97},{97,1},{2,34}... | collective-permute-start | bytes 614408 | tf_op jit(solution)/shard_map/ppermute | solution.py:23
  56.7 2.6 %collective-permute-start.13 = (bf16[800,128]{1,0:T(8,128)(2,1)S(1)}, bf16[800,128]{1,0:T(8,128)(2,1)}, u32[]{:S(2)}, u32[]{:S(2)}) collective-permute-start(bf16[800,128]{1,0:T(8,128)(2,1)S(1)} %get-tuple-element.55), channel_id=1, source_target_pairs={{0,64},{32,96},{64,0},{96,32},{1,65},{33,97},{65,1},{97,33},{2,66}... | collective-permute-start | bytes 614408 | tf_op jit(solution)/shard_map/ppermute | solution.py:23
  59.4 1.1 collective-permute-start.14
  60.4 0.5 collective-permute-start.18
  61.0 3.9 %collective-permute-start.19 = (bf16[4,2,2,16,128]{4,3,2,1,0:T(8,128)(2,1)S(1)}, bf16[4,2,2,16,128]{4,3,2,1,0:T(8,128)(2,1)S(1)}, u32[]{:S(2)}, u32[]{:S(2)}) collective-permute-start(bf16[4,2,2,16,128]{4,3,2,1,0:T(8,128)(2,1)S(1)} %get-tuple-element.59), channel_id=1, source_target_pairs={{0,4},{2,6},{4,0},{6,2},{1,5},{3,7},{5,1},{7,3},{8,12},{10,14},{12... | collective-permute-start | bytes 196616 | tf_op jit(solution)/shard_map/ppermute | solution.py:23
  64.9 3.0 %collective-permute-start.20 = (bf16[4,2,2,16,128]{4,3,2,1,0:T(8,128)(2,1)S(1)}, bf16[4,2,2,16,128]{4,3,2,1,0:T(8,128)(2,1)S(1)}, u32[]{:S(2)}, u32[]{:S(2)}) collective-permute-start(bf16[4,2,2,16,128]{4,3,2,1,0:T(8,128)(2,1)S(1)} %get-tuple-element.60), channel_id=1, source_target_pairs={{0,6},{2,0},{4,2},{6,4},{1,7},{3,1},{5,3},{7,5},{8,14},{10,8},{12,... | collective-permute-start | bytes 196616 | tf_op jit(solution)/shard_map/ppermute | solution.py:23
  67.9 0.7 collective-permute-done.13
  68.6 1.1 %add_convert_fusion = bf16[800,128]{1,0:T(8,128)(2,1)S(1)} fusion(bf16[800,128]{1,0:T(8,128)(2,1)} %collective-permute-done.14, bf16[800,128]{1,0:T(8,128)(2,1)} %collective-permute-done.13, bf16[800,128]{1,0:T(8,128)(2,1)S(1)} %collective-permute-done.12, bf16[800,128]{1,0:T(8,128)(2,1)S(1)} %get-tuple-element.53), kind=kLoop, calls=%fused_computation.4 | loop fusion | flops 819200 | bytes 1024000 | tf_op jit(solution)/shard_map/convert_element_type | solution.py:244
  69.8 0.6 collective-permute-start.15
  70.4 4.0 %collective-permute-start.16 = (bf16[224,128]{1,0:T(8,128)(2,1)S(1)}, bf16[224,128]{1,0:T(8,128)(2,1)S(1)}, u32[]{:S(2)}, u32[]{:S(2)}) collective-permute-start(bf16[224,128]{1,0:T(8,128)(2,1)S(1)} %get-tuple-element.115), channel_id=1, source_target_pairs={{0,4},{2,6},{4,0},{6,2},{1,5},{3,7},{5,1},{7,3},{8,12},{10,14},{12... | collective-permute-start | bytes 172040 | tf_op jit(solution)/shard_map/ppermute | solution.py:23
  74.4 3.0 %collective-permute-start.17 = (bf16[224,128]{1,0:T(8,128)(2,1)S(1)}, bf16[224,128]{1,0:T(8,128)(2,1)S(1)}, u32[]{:S(2)}, u32[]{:S(2)}) collective-permute-start(bf16[224,128]{1,0:T(8,128)(2,1)S(1)} %get-tuple-element.113), channel_id=1, source_target_pairs={{0,6},{2,0},{4,2},{6,4},{1,7},{3,1},{5,3},{7,5},{8,14},{10,8},{12,... | collective-permute-start | bytes 172040 | tf_op jit(solution)/shard_map/ppermute | solution.py:23
  77.4 0.4 collective-permute-done.16
  77.8 3.4 %collective-permute-done.17 = bf16[224,128]{1,0:T(8,128)(2,1)S(1)} collective-permute-done((bf16[224,128]{1,0:T(8,128)(2,1)S(1)}, bf16[224,128]{1,0:T(8,128)(2,1)S(1)}, u32[]{:S(2)}, u32[]{:S(2)}) %collective-permute-start.17) | collective-permute-done | bytes 57376 | tf_op jit(solution)/shard_map/ppermute | solution.py:23
  81.3 0.1 collective-permute-start.21
  81.5 3.0 %collective-permute-done.21 = bf16[224,128]{1,0:T(8,128)(2,1)S(1)} collective-permute-done((bf16[224,128]{1,0:T(8,128)(2,1)S(1)}, bf16[224,128]{1,0:T(8,128)(2,1)S(1)}, u32[]{:S(2)}, u32[]{:S(2)}) %collective-permute-start.21) | collective-permute-done | bytes 57376 | tf_op jit(solution)/shard_map/ppermute | solution.py:23
  84.5 0.1 collective-permute-start.22
  84.6 1.4 %collective-permute-start.23 = (bf16[128,128]{1,0:T(8,128)(2,1)S(1)}, bf16[128,128]{1,0:T(8,128)(2,1)S(1)}, u32[]{:S(2)}, u32[]{:S(2)}) collective-permute-start(bf16[128,128]{1,0:T(8,128)(2,1)S(1)} %get-tuple-element.111), channel_id=1, source_target_pairs={{0,16},{8,24},{16,0},{24,8},{1,17},{9,25},{17,1},{25,9},{2,18},{10... | collective-permute-start | bytes 98312 | tf_op jit(solution)/shard_map/ppermute | solution.py:23
  86.0 1.9 %collective-permute-start.24 = (bf16[128,128]{1,0:T(8,128)(2,1)S(1)}, bf16[128,128]{1,0:T(8,128)(2,1)S(1)}, u32[]{:S(2)}, u32[]{:S(2)}) collective-permute-start(bf16[128,128]{1,0:T(8,128)(2,1)S(1)} %get-tuple-element.112), channel_id=1, source_target_pairs={{0,24},{8,0},{16,8},{24,16},{1,25},{9,1},{17,9},{25,17},{2,26},{10... | collective-permute-start | bytes 98312 | tf_op jit(solution)/shard_map/ppermute | solution.py:23
  87.9 0.7 collective-permute-done.22
  88.6 0.4 collective-permute-done.23
  88.9 0.5 collective-permute-done.24
  89.7 4.7 %collective-permute-start.25 = (bf16[4,80,128]{2,1,0:T(8,128)(2,1)S(1)}, bf16[4,80,128]{2,1,0:T(8,128)(2,1)S(1)}, u32[]{:S(2)}, u32[]{:S(2)}) collective-permute-start(bf16[4,80,128]{2,1,0:T(8,128)(2,1)S(1)} %get-tuple-element.81), channel_id=1, source_target_pairs={{0,1},{1,0},{2,3},{3,2},{4,5},{5,4},{6,7},{7,6},{8,9},{9,8},{10,11... | collective-permute-start | bytes 245768 | tf_op jit(solution)/shard_map/ppermute | solution.py:23
  94.4 0.9 collective-permute-done.25
  95.3 0.2 copy.45
  95.5 0.1 slice.154
  95.7 0.1 copy.49
  95.9 1.1 %collective-permute-start.26 = (bf16[56,1024]{1,0:T(8,128)(2,1)S(1)}, bf16[56,1024]{1,0:T(8,128)(2,1)S(1)}, u32[]{:S(2)}, u32[]{:S(2)}) collective-permute-start(bf16[56,1024]{1,0:T(8,128)(2,1)S(1)} %get-tuple-element.92), channel_id=1, source_target_pairs={{0,32},{32,64},{64,96},{96,0},{1,33},{33,65},{65,97},{97,1},{2,34}... | collective-permute-start | bytes 344072 | tf_op jit(solution)/shard_map/ppermute | solution.py:23
  97.0 2.7 %collective-permute-start.27 = (bf16[56,1024]{1,0:T(8,128)(2,1)S(1)}, bf16[56,1024]{1,0:T(8,128)(2,1)S(1)}, u32[]{:S(2)}, u32[]{:S(2)}) collective-permute-start(bf16[56,1024]{1,0:T(8,128)(2,1)S(1)} %get-tuple-element.92), channel_id=1, source_target_pairs={{0,64},{32,96},{64,0},{96,32},{1,65},{33,97},{65,1},{97,33},{2,66}... | collective-permute-start | bytes 344072 | tf_op jit(solution)/shard_map/ppermute | solution.py:23
  99.8 0.7 collective-permute-start.28
  100.4 0.4 copy.46
  100.8 0.3 slice.133.sums_ref
  101.1 1.6 %copy-done.1 = bf16[1024,1024]{1,0:T(8,128)(2,1)S(1)} copy-done((bf16[1024,1024]{1,0:T(8,128)(2,1)S(1)}, bf16[1024,1024]{1,0:T(8,128)(2,1)}, u32[]{:S(2)}) %copy-start.1) | copy-done | bytes 2097176
  102.7 1.6 %copy-done.2 = bf16[1024,1024]{1,0:T(8,128)(2,1)S(1)} copy-done((bf16[1024,1024]{1,0:T(8,128)(2,1)S(1)}, bf16[1024,1024]{1,0:T(8,128)(2,1)}, u32[]{:S(2)}) %copy-start.2) | copy-done | bytes 2097176
  104.3 1.9 %shard_map.139 = f32[16,1024]{1,0:T(8,128)} custom-call(bf16[32,1024]{1,0:T(8,128)(2,1)S(1)} %slice.133.sums_ref, bf16[16,1024]{1,0:T(8,128)(2,1)S(1)} %bitcast.108, bf16[1024,1024]{1,0:T(8,128)(2,1)S(1)} %copy-done.2, bf16[1024,1024]{1,0:T(8,128)(2,1)S(1)} %copy-done.1), custom_call_target="tpu_custom_call" | custom-call | flops 70000000 | bytes 4300000 | tf_op jit(solution)/shard_map/pallas_call | solution.py:202
  106.3 0.8 fusion
  107.2 0.7 maximum_convert_fusion.1
  107.9 0.1 copy.50
  108.0 0.7 copy.52
  (77 shorter events, 1.0 us)
Async XLA Ops:
  0.6 43.9 %copy-start = (bf16[1024,1024]{1,0:T(8,128)(2,1)S(1)}, bf16[1024,1024]{1,0:T(8,128)(2,1)}, u32[]{:S(2)}) copy-start(bf16[1024,1024]{1,0:T(8,128)(2,1)} %param.18) | copy-start | bytes 6291460
  3.4 18.4 %collective-permute-start.3 = (bf16[800,128]{1,0:T(8,128)(2,1)S(1)}, bf16[800,128]{1,0:T(8,128)(2,1)S(1)}, u32[]{:S(2)}, u32[]{:S(2)}) collective-permute-start(bf16[800,128]{1,0:T(8,128)(2,1)S(1)} %get-tuple-element.78), channel_id=1, source_target_pairs={{0,16},{8,24},{16,0},{24,8},{1,17},{9,25},{17,1},{25,9},{2,18},{10... | collective-permute-start | bytes 614408 | tf_op jit(solution)/shard_map/ppermute | solution.py:23
  7.8 10.1 %collective-permute-start = (bf16[2,16,1024]{2,1,0:T(8,128)(2,1)S(1)}, bf16[2,16,1024]{2,1,0:T(8,128)(2,1)S(1)}, u32[]{:S(2)}, u32[]{:S(2)}) collective-permute-start(bf16[2,16,1024]{2,1,0:T(8,128)(2,1)S(1)} %bitcast.116), channel_id=1, source_target_pairs={{0,6},{2,0},{4,2},{6,4},{1,7},{3,1},{5,3},{7,5},{8,14},{10,8},{12,... | collective-permute-start | bytes 196616 | tf_op jit(solution)/shard_map/ppermute | solution.py:23
  13.9 7.2 %collective-permute-start.1 = (bf16[2,16,1024]{2,1,0:T(8,128)(2,1)S(1)}, bf16[2,16,1024]{2,1,0:T(8,128)(2,1)S(1)}, u32[]{:S(2)}, u32[]{:S(2)}) collective-permute-start(bf16[2,16,1024]{2,1,0:T(8,128)(2,1)S(1)} %bitcast.117), channel_id=1, source_target_pairs={{0,4},{2,6},{4,0},{6,2},{1,5},{3,7},{5,1},{7,3},{8,12},{10,14},{12... | collective-permute-start | bytes 196616 | tf_op jit(solution)/shard_map/ppermute | solution.py:23
  14.8 6.9 %collective-permute-start.2 = (bf16[2,16,1024]{2,1,0:T(8,128)(2,1)S(1)}, bf16[2,16,1024]{2,1,0:T(8,128)(2,1)S(1)}, u32[]{:S(2)}, u32[]{:S(2)}) collective-permute-start(bf16[2,16,1024]{2,1,0:T(8,128)(2,1)S(1)} %bitcast.118), channel_id=1, source_target_pairs={{0,2},{2,4},{4,6},{6,0},{1,3},{3,5},{5,7},{7,1},{8,10},{10,12},{12... | collective-permute-start | bytes 196616 | tf_op jit(solution)/shard_map/ppermute | solution.py:23
  17.1 9.3 %collective-permute-start.7 = (bf16[800,128]{1,0:T(8,128)(2,1)S(1)}, bf16[800,128]{1,0:T(8,128)(2,1)S(1)}, u32[]{:S(2)}, u32[]{:S(2)}) collective-permute-start(bf16[800,128]{1,0:T(8,128)(2,1)S(1)} %get-tuple-element.78), channel_id=1, source_target_pairs={{0,24},{8,0},{16,8},{24,16},{1,25},{9,1},{17,9},{25,17},{2,26},{10... | collective-permute-start | bytes 614408 | tf_op jit(solution)/shard_map/ppermute | solution.py:23
  18.0 8.4 %collective-permute-start.8 = (bf16[800,128]{1,0:T(8,128)(2,1)S(1)}, bf16[800,128]{1,0:T(8,128)(2,1)S(1)}, u32[]{:S(2)}, u32[]{:S(2)}) collective-permute-start(bf16[800,128]{1,0:T(8,128)(2,1)S(1)} %get-tuple-element.78), channel_id=1, source_target_pairs={{0,8},{8,16},{16,24},{24,0},{1,9},{9,17},{17,25},{25,1},{2,10},{10... | collective-permute-start | bytes 614408 | tf_op jit(solution)/shard_map/ppermute | solution.py:23
  21.8 18.8 %collective-permute-start.9 = (bf16[2,800,128]{2,1,0:T(8,128)(2,1)S(1)}, bf16[2,800,128]{2,1,0:T(8,128)(2,1)S(1)}, u32[]{:S(2)}, u32[]{:S(2)}) collective-permute-start(bf16[2,800,128]{2,1,0:T(8,128)(2,1)S(1)} %pad_maximum_fusion.3.edge_ref), channel_id=1, source_target_pairs={{0,1},{1,0},{2,3},{3,2},{4,5},{5,4},{6,7},{7,6},{8,9},{9,8},{10,11... | collective-permute-start | bytes 1228808 | tf_op jit(solution)/shard_map/ppermute | solution.py:23
  24.2 8.0 %collective-permute-start.4 = (bf16[4,2,16,1024]{3,2,1,0:T(8,128)(2,1)S(1)}, bf16[4,2,16,1024]{3,2,1,0:T(8,128)(2,1)S(1)}, u32[]{:S(2)}, u32[]{:S(2)}) collective-permute-start(bf16[4,2,16,1024]{3,2,1,0:T(8,128)(2,1)S(1)} %get-tuple-element.76), channel_id=1, source_target_pairs={{0,24},{8,0},{16,8},{24,16},{1,25},{9,1},{17,9},{25,17},{2,26},{10... | collective-permute-start | bytes 786440 | tf_op jit(solution)/shard_map/ppermute | solution.py:23
  25.2 9.1 %collective-permute-start.5 = (bf16[4,2,16,1024]{3,2,1,0:T(8,128)(2,1)S(1)}, bf16[4,2,16,1024]{3,2,1,0:T(8,128)(2,1)S(1)}, u32[]{:S(2)}, u32[]{:S(2)}) collective-permute-start(bf16[4,2,16,1024]{3,2,1,0:T(8,128)(2,1)S(1)} %get-tuple-element.76), channel_id=1, source_target_pairs={{0,16},{8,24},{16,0},{24,8},{1,17},{9,25},{17,1},{25,9},{2,18},{10... | collective-permute-start | bytes 786440 | tf_op jit(solution)/shard_map/ppermute | solution.py:23
  26.4 14.1 %collective-permute-start.6 = (bf16[4,2,16,1024]{3,2,1,0:T(8,128)(2,1)S(1)}, bf16[4,2,16,1024]{3,2,1,0:T(8,128)(2,1)S(1)}, u32[]{:S(2)}, u32[]{:S(2)}) collective-permute-start(bf16[4,2,16,1024]{3,2,1,0:T(8,128)(2,1)S(1)} %get-tuple-element.76), channel_id=1, source_target_pairs={{0,8},{8,16},{16,24},{24,0},{1,9},{9,17},{17,25},{25,1},{2,10},{10... | collective-permute-start | bytes 786440 | tf_op jit(solution)/shard_map/ppermute | solution.py:23
  40.7 0.8 copy-start.5
  41.5 3.1 %collective-permute-start.11 = (bf16[4,4,2,16,1024]{4,3,2,1,0:T(8,128)(2,1)S(1)}, bf16[4,4,2,16,1024]{4,3,2,1,0:T(8,128)(2,1)}, u32[]{:S(2)}, u32[]{:S(2)}) collective-permute-start(bf16[4,4,2,16,1024]{4,3,2,1,0:T(8,128)(2,1)S(1)} %pad_maximum_fusion.mine_ref), channel_id=1, source_target_pairs={{0,1},{1,0},{2,3},{3,2},{4,5},{5,4},{6,7},{7,6},{8,9},{9,8},{10,11... | collective-permute-start | bytes 3145736 | tf_op jit(solution)/shard_map/ppermute | solution.py:23
  41.9 2.2 %copy-start.3 = (bf16[2,800,128]{2,1,0:T(8,128)(2,1)S(1)}, bf16[2,800,128]{2,1,0:T(8,128)(2,1)}, u32[]{:S(2)}) copy-start(bf16[2,800,128]{2,1,0:T(8,128)(2,1)} %pad_maximum_fusion.2.edge_ref) | copy-start | bytes 1228804
  41.9 2.6 %copy-start.6 = (bf16[2,800,128]{2,1,0:T(8,128)(2,1)S(1)}, bf16[2,800,128]{2,1,0:T(8,128)(2,1)}, u32[]{:S(2)}) copy-start(bf16[2,800,128]{2,1,0:T(8,128)(2,1)} %copy-done.5) | copy-start | bytes 1228804
  44.2 6.4 %collective-permute-start.10 = (bf16[2,800,128]{2,1,0:T(8,128)(2,1)S(1)}, bf16[2,800,128]{2,1,0:T(8,128)(2,1)S(1)}, u32[]{:S(2)}, u32[]{:S(2)}) collective-permute-start(bf16[2,800,128]{2,1,0:T(8,128)(2,1)S(1)} %copy-done.3), channel_id=1, source_target_pairs={{0,1},{1,0},{2,3},{3,2},{4,5},{5,4},{6,7},{7,6},{8,9},{9,8},{10,11... | collective-permute-start | bytes 1228808 | tf_op jit(solution)/shard_map/ppermute | solution.py:23
  55.4 9.5 %collective-permute-start.12 = (bf16[800,128]{1,0:T(8,128)(2,1)S(1)}, bf16[800,128]{1,0:T(8,128)(2,1)S(1)}, u32[]{:S(2)}, u32[]{:S(2)}) collective-permute-start(bf16[800,128]{1,0:T(8,128)(2,1)S(1)} %get-tuple-element.54), channel_id=1, source_target_pairs={{0,32},{32,64},{64,96},{96,0},{1,33},{33,65},{65,97},{97,1},{2,34}... | collective-permute-start | bytes 614408 | tf_op jit(solution)/shard_map/ppermute | solution.py:23
  56.7 11.8 %collective-permute-start.13 = (bf16[800,128]{1,0:T(8,128)(2,1)S(1)}, bf16[800,128]{1,0:T(8,128)(2,1)}, u32[]{:S(2)}, u32[]{:S(2)}) collective-permute-start(bf16[800,128]{1,0:T(8,128)(2,1)S(1)} %get-tuple-element.55), channel_id=1, source_target_pairs={{0,64},{32,96},{64,0},{96,32},{1,65},{33,97},{65,1},{97,33},{2,66}... | collective-permute-start | bytes 614408 | tf_op jit(solution)/shard_map/ppermute | solution.py:23
  59.4 9.2 %collective-permute-start.14 = (bf16[800,128]{1,0:T(8,128)(2,1)S(1)}, bf16[800,128]{1,0:T(8,128)(2,1)}, u32[]{:S(2)}, u32[]{:S(2)}) collective-permute-start(bf16[800,128]{1,0:T(8,128)(2,1)S(1)} %get-tuple-element.56), channel_id=1, source_target_pairs={{0,96},{32,0},{64,32},{96,64},{1,97},{33,1},{65,33},{97,65},{2,98}... | collective-permute-start | bytes 614408 | tf_op jit(solution)/shard_map/ppermute | solution.py:23
  60.4 13.9 %collective-permute-start.18 = (bf16[4,2,2,16,128]{4,3,2,1,0:T(8,128)(2,1)S(1)}, bf16[4,2,2,16,128]{4,3,2,1,0:T(8,128)(2,1)S(1)}, u32[]{:S(2)}, u32[]{:S(2)}) collective-permute-start(bf16[4,2,2,16,128]{4,3,2,1,0:T(8,128)(2,1)S(1)} %get-tuple-element.58), channel_id=1, source_target_pairs={{0,2},{2,4},{4,6},{6,0},{1,3},{3,5},{5,7},{7,1},{8,10},{10,12},{12... | collective-permute-start | bytes 196616 | tf_op jit(solution)/shard_map/ppermute | solution.py:23
  61.0 16.4 %collective-permute-start.19 = (bf16[4,2,2,16,128]{4,3,2,1,0:T(8,128)(2,1)S(1)}, bf16[4,2,2,16,128]{4,3,2,1,0:T(8,128)(2,1)S(1)}, u32[]{:S(2)}, u32[]{:S(2)}) collective-permute-start(bf16[4,2,2,16,128]{4,3,2,1,0:T(8,128)(2,1)S(1)} %get-tuple-element.59), channel_id=1, source_target_pairs={{0,4},{2,6},{4,0},{6,2},{1,5},{3,7},{5,1},{7,3},{8,12},{10,14},{12... | collective-permute-start | bytes 196616 | tf_op jit(solution)/shard_map/ppermute | solution.py:23
  64.9 12.5 %collective-permute-start.20 = (bf16[4,2,2,16,128]{4,3,2,1,0:T(8,128)(2,1)S(1)}, bf16[4,2,2,16,128]{4,3,2,1,0:T(8,128)(2,1)S(1)}, u32[]{:S(2)}, u32[]{:S(2)}) collective-permute-start(bf16[4,2,2,16,128]{4,3,2,1,0:T(8,128)(2,1)S(1)} %get-tuple-element.60), channel_id=1, source_target_pairs={{0,6},{2,0},{4,2},{6,4},{1,7},{3,1},{5,3},{7,5},{8,14},{10,8},{12,... | collective-permute-start | bytes 196616 | tf_op jit(solution)/shard_map/ppermute | solution.py:23
  69.8 7.5 %collective-permute-start.15 = (bf16[224,128]{1,0:T(8,128)(2,1)S(1)}, bf16[224,128]{1,0:T(8,128)(2,1)S(1)}, u32[]{:S(2)}, u32[]{:S(2)}) collective-permute-start(bf16[224,128]{1,0:T(8,128)(2,1)S(1)} %get-tuple-element.114), channel_id=1, source_target_pairs={{0,2},{2,4},{4,6},{6,0},{1,3},{3,5},{5,7},{7,1},{8,10},{10,12},{12... | collective-permute-start | bytes 172040 | tf_op jit(solution)/shard_map/ppermute | solution.py:23
  70.4 7.4 %collective-permute-start.16 = (bf16[224,128]{1,0:T(8,128)(2,1)S(1)}, bf16[224,128]{1,0:T(8,128)(2,1)S(1)}, u32[]{:S(2)}, u32[]{:S(2)}) collective-permute-start(bf16[224,128]{1,0:T(8,128)(2,1)S(1)} %get-tuple-element.115), channel_id=1, source_target_pairs={{0,4},{2,6},{4,0},{6,2},{1,5},{3,7},{5,1},{7,3},{8,12},{10,14},{12... | collective-permute-start | bytes 172040 | tf_op jit(solution)/shard_map/ppermute | solution.py:23
  74.4 6.8 %collective-permute-start.17 = (bf16[224,128]{1,0:T(8,128)(2,1)S(1)}, bf16[224,128]{1,0:T(8,128)(2,1)S(1)}, u32[]{:S(2)}, u32[]{:S(2)}) collective-permute-start(bf16[224,128]{1,0:T(8,128)(2,1)S(1)} %get-tuple-element.113), channel_id=1, source_target_pairs={{0,6},{2,0},{4,2},{6,4},{1,7},{3,1},{5,3},{7,5},{8,14},{10,8},{12,... | collective-permute-start | bytes 172040 | tf_op jit(solution)/shard_map/ppermute | solution.py:23
  81.3 3.1 %collective-permute-start.21 = (bf16[224,128]{1,0:T(8,128)(2,1)S(1)}, bf16[224,128]{1,0:T(8,128)(2,1)S(1)}, u32[]{:S(2)}, u32[]{:S(2)}) collective-permute-start(bf16[224,128]{1,0:T(8,128)(2,1)S(1)} %pad_maximum_fusion.20), channel_id=1, source_target_pairs={{0,128},{128,0},{1,129},{129,1},{2,130},{130,2},{3,131},{131,3},{4... | collective-permute-start | bytes 172040 | tf_op jit(solution)/shard_map/ppermute | solution.py:23
  84.5 4.1 %collective-permute-start.22 = (bf16[128,128]{1,0:T(8,128)(2,1)S(1)}, bf16[128,128]{1,0:T(8,128)(2,1)S(1)}, u32[]{:S(2)}, u32[]{:S(2)}) collective-permute-start(bf16[128,128]{1,0:T(8,128)(2,1)S(1)} %get-tuple-element.110), channel_id=1, source_target_pairs={{0,8},{8,16},{16,24},{24,0},{1,9},{9,17},{17,25},{25,1},{2,10},{10... | collective-permute-start | bytes 98312 | tf_op jit(solution)/shard_map/ppermute | solution.py:23
  84.6 4.4 %collective-permute-start.23 = (bf16[128,128]{1,0:T(8,128)(2,1)S(1)}, bf16[128,128]{1,0:T(8,128)(2,1)S(1)}, u32[]{:S(2)}, u32[]{:S(2)}) collective-permute-start(bf16[128,128]{1,0:T(8,128)(2,1)S(1)} %get-tuple-element.111), channel_id=1, source_target_pairs={{0,16},{8,24},{16,0},{24,8},{1,17},{9,25},{17,1},{25,9},{2,18},{10... | collective-permute-start | bytes 98312 | tf_op jit(solution)/shard_map/ppermute | solution.py:23
  86.0 3.5 %collective-permute-start.24 = (bf16[128,128]{1,0:T(8,128)(2,1)S(1)}, bf16[128,128]{1,0:T(8,128)(2,1)S(1)}, u32[]{:S(2)}, u32[]{:S(2)}) collective-permute-start(bf16[128,128]{1,0:T(8,128)(2,1)S(1)} %get-tuple-element.112), channel_id=1, source_target_pairs={{0,24},{8,0},{16,8},{24,16},{1,25},{9,1},{17,9},{25,17},{2,26},{10... | collective-permute-start | bytes 98312 | tf_op jit(solution)/shard_map/ppermute | solution.py:23
  89.6 11.5 %copy-start.4 = (bf16[1,16,1024]{2,1,0:T(8,128)(2,1)S(1)}, bf16[1,16,1024]{2,1,0:T(8,128)(2,1)}, u32[]{:S(2)}) copy-start(bf16[1,16,1024]{2,1,0:T(8,128)(2,1)} %param.11) | copy-start | bytes 98308
  89.7 5.6 %collective-permute-start.25 = (bf16[4,80,128]{2,1,0:T(8,128)(2,1)S(1)}, bf16[4,80,128]{2,1,0:T(8,128)(2,1)S(1)}, u32[]{:S(2)}, u32[]{:S(2)}) collective-permute-start(bf16[4,80,128]{2,1,0:T(8,128)(2,1)S(1)} %get-tuple-element.81), channel_id=1, source_target_pairs={{0,1},{1,0},{2,3},{3,2},{4,5},{5,4},{6,7},{7,6},{8,9},{9,8},{10,11... | collective-permute-start | bytes 245768 | tf_op jit(solution)/shard_map/ppermute | solution.py:23
  95.9 10.3 %collective-permute-start.26 = (bf16[56,1024]{1,0:T(8,128)(2,1)S(1)}, bf16[56,1024]{1,0:T(8,128)(2,1)S(1)}, u32[]{:S(2)}, u32[]{:S(2)}) collective-permute-start(bf16[56,1024]{1,0:T(8,128)(2,1)S(1)} %get-tuple-element.92), channel_id=1, source_target_pairs={{0,32},{32,64},{64,96},{96,0},{1,33},{33,65},{65,97},{97,1},{2,34}... | collective-permute-start | bytes 344072 | tf_op jit(solution)/shard_map/ppermute | solution.py:23
  97.0 9.2 %collective-permute-start.27 = (bf16[56,1024]{1,0:T(8,128)(2,1)S(1)}, bf16[56,1024]{1,0:T(8,128)(2,1)S(1)}, u32[]{:S(2)}, u32[]{:S(2)}) collective-permute-start(bf16[56,1024]{1,0:T(8,128)(2,1)S(1)} %get-tuple-element.92), channel_id=1, source_target_pairs={{0,64},{32,96},{64,0},{96,32},{1,65},{33,97},{65,1},{97,33},{2,66}... | collective-permute-start | bytes 344072 | tf_op jit(solution)/shard_map/ppermute | solution.py:23
  99.8 6.5 %collective-permute-start.28 = (bf16[56,1024]{1,0:T(8,128)(2,1)S(1)}, bf16[56,1024]{1,0:T(8,128)(2,1)S(1)}, u32[]{:S(2)}, u32[]{:S(2)}) collective-permute-start(bf16[56,1024]{1,0:T(8,128)(2,1)S(1)} %get-tuple-element.92), channel_id=1, source_target_pairs={{0,96},{32,0},{64,32},{96,64},{1,97},{33,1},{65,33},{97,65},{2,98}... | collective-permute-start | bytes 344072 | tf_op jit(solution)/shard_map/ppermute | solution.py:23
  101.1 1.6 %copy-start.1 = (bf16[1024,1024]{1,0:T(8,128)(2,1)S(1)}, bf16[1024,1024]{1,0:T(8,128)(2,1)}, u32[]{:S(2)}) copy-start(bf16[1024,1024]{1,0:T(8,128)(2,1)} %wt_ref.1) | copy-start | bytes 6291460
  102.7 1.6 %copy-start.2 = (bf16[1024,1024]{1,0:T(8,128)(2,1)S(1)}, bf16[1024,1024]{1,0:T(8,128)(2,1)}, u32[]{:S(2)}) copy-start(bf16[1024,1024]{1,0:T(8,128)(2,1)} %ws_ref.1) | copy-start | bytes 6291460

commit v3 on v2

--- a/solution.py
+++ b/solution.py
@@ -223,7 +223,6 @@
     ids = jnp.stack([ids >> 4, ids & 15]).astype(BF).reshape(24, 128)
     edges = jnp.concatenate([radial[0], ids, jnp.zeros((8, 128), BF)])
     edges = gather_from(edges, "x")
-    nodes, edges[2] = lax.optimization_barrier((nodes, edges[2]))
     early, late = jnp.stack([edges[0], edges[2]]), jnp.stack([edges[1], edges[3]])
     early_sib = send(early, "core", 1)
     nodes = jnp.stack(gather_from(jnp.stack(nodes), "x"))

time: 109 us -> 107 us (0.982)
  waiting for transfers between devices: 26.4 us -> 23.5 us
    ppermute x29, waiting for transfers between devices: 26.4 us -> 23.5 us  [send(): lax.ppermute(array, axis, [(i, (i + offset) % size) for i in range(size)])]
  transfers between devices with their start and end apart: 29 -> 29, of which waited for: 13 -> 11; matrix products, arithmetic and copies ran while one was open for 6% -> 6% of each run, Pallas kernels for 7% -> 7%
where the time goes in v3:
time: 107 us; the launch traced here: 106 us
  starting transfers between devices  52.9 us (49%)
  waiting for transfers between devices  23.5 us (22%)
  Pallas kernels  12.7 us (12%)
  local copies, waits for them, and re-layouts  8.47 us (8%)
  other arithmetic  6.8 us (6%)
  between operations  1.9 us (2%)
    ppermute x29, starting transfers between devices, send(): lax.ppermute(array, axis, [(i, (i + offset) % size) for i in range(size)])  52.9 us
    ppermute x29, waiting for transfers between devices, send(): lax.ppermute(array, axis, [(i, (i + offset) % size) for i in range(size)])  23.5 us
    pallas_call x1, Pallas kernels, edge_pass(): pl.pallas_call(first_kernel, in_specs=[smem] + [vmem] * 8, out_specs=[vme...  5.93 us
    pallas_call x1, Pallas kernels, edge_pass(): pl.pallas_call(second_kernel, in_specs=[smem] + [vmem] * 10, out_specs=[v...  4.83 us
    unnamed x15, local copies, waits for them, and re-layouts  4.66 us
    dynamic_slice x3, local copies, waits for them, and re-layouts, mine(): return lax.dynamic_slice_in_dim(weight, my_x * 256, 256, axis)  2.23 us
  transfers between devices with their start and end apart: 29, of which 11 were waited for; matrix products, arithmetic and copies ran while one was open for 6% of the time, Pallas kernels for 7%

profile of v3, /device:TPU:1, one launch (start us, length us, event | category | flops | bytes accessed | tf_op | source)
XLA Modules:
  0.0 106.3 jit_solution(17301432667533275022)
XLA Ops:
  1.5 0.7 shift-right-arithmetic_convert_fusion
  2.2 0.1 pad.64.clone
  2.3 1.1 %fusion.18 = (bf16[1,800,128]{2,1,0:T(8,128)(2,1)S(1)}, bf16[800,128]{1,0:T(8,128)(2,1)S(1)}) fusion(bf16[800]{0:T(1024)(128)(2,1)S(1)} %pad.64.clone, bf16[24,128]{1,0:T(8,128)(2,1)S(1)} %convert_element_type.76, bf16[768,128]{1,0:T(8,128)(2,1)} %bitcast.128), kind=kLoop, calls=%fused_computation.101 | loop fusion | flops 614400 | bytes 613952 | tf_op jit(solution)/shard_map/stack | solution.py:226
  3.4 3.7 %collective-permute-start.8 = (bf16[800,128]{1,0:T(8,128)(2,1)S(1)}, bf16[800,128]{1,0:T(8,128)(2,1)S(1)}, u32[]{:S(2)}, u32[]{:S(2)}) collective-permute-start(bf16[800,128]{1,0:T(8,128)(2,1)S(1)} %get-tuple-element.68), channel_id=1, source_target_pairs={{0,16},{8,24},{16,0},{24,8},{1,17},{9,25},{17,1},{25,9},{2,18},{10... | collective-permute-start | bytes 614408 | tf_op jit(solution)/shard_map/ppermute | solution.py:23
  7.1 0.8 pad_maximum_fusion.15
  7.8 3.0 %collective-permute-start.2 = (bf16[2,16,1024]{2,1,0:T(8,128)(2,1)S(1)}, bf16[2,16,1024]{2,1,0:T(8,128)(2,1)S(1)}, u32[]{:S(2)}, u32[]{:S(2)}) collective-permute-start(bf16[2,16,1024]{2,1,0:T(8,128)(2,1)S(1)} %bitcast.116), channel_id=1, source_target_pairs={{0,2},{2,4},{4,6},{6,0},{1,3},{3,5},{5,7},{7,1},{8,10},{10,12},{12... | collective-permute-start | bytes 196616 | tf_op jit(solution)/shard_map/ppermute | solution.py:23
  10.8 3.1 %collective-permute-start = (bf16[2,16,1024]{2,1,0:T(8,128)(2,1)S(1)}, bf16[2,16,1024]{2,1,0:T(8,128)(2,1)S(1)}, u32[]{:S(2)}, u32[]{:S(2)}) collective-permute-start(bf16[2,16,1024]{2,1,0:T(8,128)(2,1)S(1)} %bitcast.117), channel_id=1, source_target_pairs={{0,6},{2,0},{4,2},{6,4},{1,7},{3,1},{5,3},{7,5},{8,14},{10,8},{12,... | collective-permute-start | bytes 196616 | tf_op jit(solution)/shard_map/ppermute | solution.py:23
  13.9 4.4 %collective-permute-start.1 = (bf16[2,16,1024]{2,1,0:T(8,128)(2,1)S(1)}, bf16[2,16,1024]{2,1,0:T(8,128)(2,1)S(1)}, u32[]{:S(2)}, u32[]{:S(2)}) collective-permute-start(bf16[2,16,1024]{2,1,0:T(8,128)(2,1)S(1)} %bitcast.118), channel_id=1, source_target_pairs={{0,4},{2,6},{4,0},{6,2},{1,5},{3,7},{5,1},{7,3},{8,12},{10,14},{12... | collective-permute-start | bytes 196616 | tf_op jit(solution)/shard_map/ppermute | solution.py:23
  18.3 0.9 collective-permute-start.6
  19.2 0.6 collective-permute-start.7
  19.9 2.4 %collective-permute-start.9 = (bf16[2,800,128]{2,1,0:T(8,128)(2,1)S(1)}, bf16[2,800,128]{2,1,0:T(8,128)(2,1)S(1)}, u32[]{:S(2)}, u32[]{:S(2)}) collective-permute-start(bf16[2,800,128]{2,1,0:T(8,128)(2,1)S(1)} %pad_maximum_fusion.3.edge_ref), channel_id=1, source_target_pairs={{0,1},{1,0},{2,3},{3,2},{4,5},{5,4},{6,7},{7,6},{8,9},{9,8},{10,11... | collective-permute-start | bytes 1228808 | tf_op jit(solution)/shard_map/ppermute | solution.py:23
  22.4 2.1 %collective-permute-start.3 = (bf16[4,2,16,1024]{3,2,1,0:T(8,128)(2,1)S(1)}, bf16[4,2,16,1024]{3,2,1,0:T(8,128)(2,1)S(1)}, u32[]{:S(2)}, u32[]{:S(2)}) collective-permute-start(bf16[4,2,16,1024]{3,2,1,0:T(8,128)(2,1)S(1)} %get-tuple-element.66), channel_id=1, source_target_pairs={{0,24},{8,0},{16,8},{24,16},{1,25},{9,1},{17,9},{25,17},{2,26},{10... | collective-permute-start | bytes 786440 | tf_op jit(solution)/shard_map/ppermute | solution.py:23
  24.5 0.6 collective-permute-start.5
  25.2 0.8 pad_maximum_fusion.2.edge_ref
  26.0 4.6 %collective-permute-done.3 = bf16[4,2,16,1024]{3,2,1,0:T(8,128)(2,1)S(1)} collective-permute-done((bf16[4,2,16,1024]{3,2,1,0:T(8,128)(2,1)S(1)}, bf16[4,2,16,1024]{3,2,1,0:T(8,128)(2,1)S(1)}, u32[]{:S(2)}, u32[]{:S(2)}) %collective-permute-start.3) | collective-permute-done | bytes 262176 | tf_op jit(solution)/shard_map/ppermute | solution.py:23
  30.6 2.5 %collective-permute-done.4 = bf16[4,2,16,1024]{3,2,1,0:T(8,128)(2,1)S(1)} collective-permute-done((bf16[4,2,16,1024]{3,2,1,0:T(8,128)(2,1)S(1)}, bf16[4,2,16,1024]{3,2,1,0:T(8,128)(2,1)S(1)}, u32[]{:S(2)}, u32[]{:S(2)}) %collective-permute-start.4) | collective-permute-done | bytes 262176 | tf_op jit(solution)/shard_map/ppermute | solution.py:23
  33.1 6.2 %collective-permute-done.5 = bf16[4,2,16,1024]{3,2,1,0:T(8,128)(2,1)S(1)} collective-permute-done((bf16[4,2,16,1024]{3,2,1,0:T(8,128)(2,1)S(1)}, bf16[4,2,16,1024]{3,2,1,0:T(8,128)(2,1)S(1)}, u32[]{:S(2)}, u32[]{:S(2)}) %collective-permute-start.5) | collective-permute-done | bytes 262176 | tf_op jit(solution)/shard_map/ppermute | solution.py:23
  39.3 0.1 pad_maximum_fusion.mine_ref
  39.4 0.8 copy-done.5
  40.2 0.8 collective-permute-start.11
  41.0 0.9 constant_dynamic-slice_fusion.20.wr
  42.0 1.3 %constant_dynamic-slice_fusion.22 = (bf16[1024,256]{1,0:T(8,128)(2,1)S(1)}, bf16[1024,256]{1,0:T(8,128)(2,1)S(1)}) fusion(bf16[1024,1024]{1,0:T(8,128)(2,1)} %wt_ref.1, s32[]{:T(128)S(6)} %select_n.154, bf16[1024,1024]{1,0:T(8,128)(2,1)} %ws_ref.1), kind=kLoop, calls=%fused_computation.82 | loop fusion | bytes 2097156 | tf_op jit(solution)/shard_map/dynamic_slice | solution.py:231
  43.2 0.3 collective-permute-start.10
  43.5 0.1 pad_add_fusion.at_ref
  43.7 5.9 %shard_map.137 = (bf16[512,1024]{1,0:T(8,128)(2,1)S(1)}, bf16[512,1024]{1,0:T(8,128)(2,1)S(1)}, bf16[128,512]{1,0:T(8,128)(2,1)S(1)}, bf16[256,512]{1,0:T(8,128)...) custom-call(s32[4]{0:T(128)S(1)} %pad_add_fusion.at_ref, ...), custom_call_target="tpu_custom_call" | custom-call | flops 3000000000 | bytes 4000000 | tf_op jit(solution)/shard_map/pallas_call | solution.py:166
  49.6 4.8 %shard_map.138 = (bf16[4,2,2,16,128]{4,3,2,1,0:T(8,128)(2,1)S(1)}, bf16[4,2,2,16,128]{4,3,2,1,0:T(8,128)(2,1)S(1)}, bf16[4,2,2,16,128]{4,3,2,1,0:T(8,128)(2,1)S(...) custom-call(s32[4]{0:T(128)S(1)} %pad_add_fusion.at_ref, ...), custom_call_target="tpu_custom_call" | custom-call | flops 3000000000 | bytes 4000000 | tf_op jit(solution)/shard_map/pallas_call | solution.py:181
  54.4 1.4 %collective-permute-start.12 = (bf16[800,128]{1,0:T(8,128)(2,1)S(1)}, bf16[800,128]{1,0:T(8,128)(2,1)S(1)}, u32[]{:S(2)}, u32[]{:S(2)}) collective-permute-start(bf16[800,128]{1,0:T(8,128)(2,1)S(1)} %get-tuple-element.44), channel_id=1, source_target_pairs={{0,32},{32,64},{64,96},{96,0},{1,33},{33,65},{65,97},{97,1},{2,34}... | collective-permute-start | bytes 614408 | tf_op jit(solution)/shard_map/ppermute | solution.py:23
  55.8 2.6 %collective-permute-start.13 = (bf16[800,128]{1,0:T(8,128)(2,1)S(1)}, bf16[800,128]{1,0:T(8,128)(2,1)}, u32[]{:S(2)}, u32[]{:S(2)}) collective-permute-start(bf16[800,128]{1,0:T(8,128)(2,1)S(1)} %get-tuple-element.45), channel_id=1, source_target_pairs={{0,64},{32,96},{64,0},{96,32},{1,65},{33,97},{65,1},{97,33},{2,66}... | collective-permute-start | bytes 614408 | tf_op jit(solution)/shard_map/ppermute | solution.py:23
  58.4 1.1 %collective-permute-start.14 = (bf16[800,128]{1,0:T(8,128)(2,1)S(1)}, bf16[800,128]{1,0:T(8,128)(2,1)}, u32[]{:S(2)}, u32[]{:S(2)}) collective-permute-start(bf16[800,128]{1,0:T(8,128)(2,1)S(1)} %get-tuple-element.46), channel_id=1, source_target_pairs={{0,96},{32,0},{64,32},{96,64},{1,97},{33,1},{65,33},{97,65},{2,98}... | collective-permute-start | bytes 614408 | tf_op jit(solution)/shard_map/ppermute | solution.py:23
  59.5 2.6 %collective-permute-start.19 = (bf16[4,2,2,16,128]{4,3,2,1,0:T(8,128)(2,1)S(1)}, bf16[4,2,2,16,128]{4,3,2,1,0:T(8,128)(2,1)S(1)}, u32[]{:S(2)}, u32[]{:S(2)}) collective-permute-start(bf16[4,2,2,16,128]{4,3,2,1,0:T(8,128)(2,1)S(1)} %get-tuple-element.49), channel_id=1, source_target_pairs={{0,4},{2,6},{4,0},{6,2},{1,5},{3,7},{5,1},{7,3},{8,12},{10,14},{12... | collective-permute-start | bytes 196616 | tf_op jit(solution)/shard_map/ppermute | solution.py:23
  62.1 3.6 %collective-permute-start.20 = (bf16[4,2,2,16,128]{4,3,2,1,0:T(8,128)(2,1)S(1)}, bf16[4,2,2,16,128]{4,3,2,1,0:T(8,128)(2,1)S(1)}, u32[]{:S(2)}, u32[]{:S(2)}) collective-permute-start(bf16[4,2,2,16,128]{4,3,2,1,0:T(8,128)(2,1)S(1)} %get-tuple-element.50), channel_id=1, source_target_pairs={{0,6},{2,0},{4,2},{6,4},{1,7},{3,1},{5,3},{7,5},{8,14},{10,8},{12,... | collective-permute-start | bytes 196616 | tf_op jit(solution)/shard_map/ppermute | solution.py:23
  65.7 1.9 %collective-permute-done.13 = bf16[800,128]{1,0:T(8,128)(2,1)} collective-permute-done((bf16[800,128]{1,0:T(8,128)(2,1)S(1)}, bf16[800,128]{1,0:T(8,128)(2,1)}, u32[]{:S(2)}, u32[]{:S(2)}) %collective-permute-start.13) | collective-permute-done | bytes 204832 | tf_op jit(solution)/shard_map/ppermute | solution.py:23
  67.6 1.1 %add_convert_fusion = bf16[800,128]{1,0:T(8,128)(2,1)S(1)} fusion(bf16[800,128]{1,0:T(8,128)(2,1)} %collective-permute-done.14, bf16[800,128]{1,0:T(8,128)(2,1)} %collective-permute-done.13, bf16[800,128]{1,0:T(8,128)(2,1)S(1)} %collective-permute-done.12, bf16[800,128]{1,0:T(8,128)(2,1)S(1)} %get-tuple-element.43), kind=kLoop, calls=%fused_computation.4 | loop fusion | flops 819200 | bytes 1024000 | tf_op jit(solution)/shard_map/convert_element_type | solution.py:243
  68.9 0.1 collective-permute-start.15
  69.0 2.7 %collective-permute-start.16 = (bf16[224,128]{1,0:T(8,128)(2,1)S(1)}, bf16[224,128]{1,0:T(8,128)(2,1)S(1)}, u32[]{:S(2)}, u32[]{:S(2)}) collective-permute-start(bf16[224,128]{1,0:T(8,128)(2,1)S(1)} %get-tuple-element.105), channel_id=1, source_target_pairs={{0,4},{2,6},{4,0},{6,2},{1,5},{3,7},{5,1},{7,3},{8,12},{10,14},{12... | collective-permute-start | bytes 172040 | tf_op jit(solution)/shard_map/ppermute | solution.py:23
  71.7 3.5 %collective-permute-start.17 = (bf16[224,128]{1,0:T(8,128)(2,1)S(1)}, bf16[224,128]{1,0:T(8,128)(2,1)S(1)}, u32[]{:S(2)}, u32[]{:S(2)}) collective-permute-start(bf16[224,128]{1,0:T(8,128)(2,1)S(1)} %get-tuple-element.103), channel_id=1, source_target_pairs={{0,6},{2,0},{4,2},{6,4},{1,7},{3,1},{5,3},{7,5},{8,14},{10,8},{12,... | collective-permute-start | bytes 172040 | tf_op jit(solution)/shard_map/ppermute | solution.py:23
  75.2 1.5 %collective-permute-done.16 = bf16[224,128]{1,0:T(8,128)(2,1)S(1)} collective-permute-done((bf16[224,128]{1,0:T(8,128)(2,1)S(1)}, bf16[224,128]{1,0:T(8,128)(2,1)S(1)}, u32[]{:S(2)}, u32[]{:S(2)}) %collective-permute-start.16) | collective-permute-done | bytes 57376 | tf_op jit(solution)/shard_map/ppermute | solution.py:23
  76.7 0.8 collective-permute-done.17
  77.6 1.1 %collective-permute-start.21 = (bf16[224,128]{1,0:T(8,128)(2,1)S(1)}, bf16[224,128]{1,0:T(8,128)(2,1)S(1)}, u32[]{:S(2)}, u32[]{:S(2)}) collective-permute-start(bf16[224,128]{1,0:T(8,128)(2,1)S(1)} %pad_maximum_fusion.20), channel_id=1, source_target_pairs={{0,128},{128,0},{1,129},{129,1},{2,130},{130,2},{3,131},{131,3},{4... | collective-permute-start | bytes 172040 | tf_op jit(solution)/shard_map/ppermute | solution.py:23
  78.8 2.3 %collective-permute-done.21 = bf16[224,128]{1,0:T(8,128)(2,1)S(1)} collective-permute-done((bf16[224,128]{1,0:T(8,128)(2,1)S(1)}, bf16[224,128]{1,0:T(8,128)(2,1)S(1)}, u32[]{:S(2)}, u32[]{:S(2)}) %collective-permute-start.21) | collective-permute-done | bytes 57376 | tf_op jit(solution)/shard_map/ppermute | solution.py:23
  81.2 0.7 collective-permute-start.22
  81.9 3.8 %collective-permute-start.23 = (bf16[128,128]{1,0:T(8,128)(2,1)S(1)}, bf16[128,128]{1,0:T(8,128)(2,1)S(1)}, u32[]{:S(2)}, u32[]{:S(2)}) collective-permute-start(bf16[128,128]{1,0:T(8,128)(2,1)S(1)} %get-tuple-element.101), channel_id=1, source_target_pairs={{0,16},{8,24},{16,0},{24,8},{1,17},{9,25},{17,1},{25,9},{2,18},{10... | collective-permute-start | bytes 98312 | tf_op jit(solution)/shard_map/ppermute | solution.py:23
  85.7 0.1 collective-permute-done.22
  85.8 1.5 %collective-permute-done.23 = bf16[128,128]{1,0:T(8,128)(2,1)S(1)} collective-permute-done((bf16[128,128]{1,0:T(8,128)(2,1)S(1)}, bf16[128,128]{1,0:T(8,128)(2,1)S(1)}, u32[]{:S(2)}, u32[]{:S(2)}) %collective-permute-start.23) | collective-permute-done | bytes 32800 | tf_op jit(solution)/shard_map/ppermute | solution.py:23
  87.3 1.1 %collective-permute-done.24 = bf16[128,128]{1,0:T(8,128)(2,1)S(1)} collective-permute-done((bf16[128,128]{1,0:T(8,128)(2,1)S(1)}, bf16[128,128]{1,0:T(8,128)(2,1)S(1)}, u32[]{:S(2)}, u32[]{:S(2)}) %collective-permute-start.24) | collective-permute-done | bytes 32800 | tf_op jit(solution)/shard_map/ppermute | solution.py:23
  88.6 3.7 %collective-permute-start.25 = (bf16[4,80,128]{2,1,0:T(8,128)(2,1)S(1)}, bf16[4,80,128]{2,1,0:T(8,128)(2,1)S(1)}, u32[]{:S(2)}, u32[]{:S(2)}) collective-permute-start(bf16[4,80,128]{2,1,0:T(8,128)(2,1)S(1)} %get-tuple-element.71), channel_id=1, source_target_pairs={{0,1},{1,0},{2,3},{3,2},{4,5},{5,4},{6,7},{7,6},{8,9},{9,8},{10,11... | collective-permute-start | bytes 245768 | tf_op jit(solution)/shard_map/ppermute | solution.py:23
  92.4 0.9 collective-permute-done.25
  93.2 0.1 fusion.9
  93.3 0.2 copy.45
  93.5 0.1 slice.154
  93.7 0.1 copy.49
  93.9 1.2 %collective-permute-start.26 = (bf16[56,1024]{1,0:T(8,128)(2,1)S(1)}, bf16[56,1024]{1,0:T(8,128)(2,1)S(1)}, u32[]{:S(2)}, u32[]{:S(2)}) collective-permute-start(bf16[56,1024]{1,0:T(8,128)(2,1)S(1)} %get-tuple-element.82), channel_id=1, source_target_pairs={{0,32},{32,64},{64,96},{96,0},{1,33},{33,65},{65,97},{97,1},{2,34}... | collective-permute-start | bytes 344072 | tf_op jit(solution)/shard_map/ppermute | solution.py:23
  95.0 2.8 %collective-permute-start.27 = (bf16[56,1024]{1,0:T(8,128)(2,1)S(1)}, bf16[56,1024]{1,0:T(8,128)(2,1)S(1)}, u32[]{:S(2)}, u32[]{:S(2)}) collective-permute-start(bf16[56,1024]{1,0:T(8,128)(2,1)S(1)} %get-tuple-element.82), channel_id=1, source_target_pairs={{0,64},{32,96},{64,0},{96,32},{1,65},{33,97},{65,1},{97,33},{2,66}... | collective-permute-start | bytes 344072 | tf_op jit(solution)/shard_map/ppermute | solution.py:23
  97.9 0.1 collective-permute-start.28
  98.0 0.4 copy.46
  98.4 0.3 slice.133.sums_ref
  98.7 1.6 %copy-done.1 = bf16[1024,1024]{1,0:T(8,128)(2,1)S(1)} copy-done((bf16[1024,1024]{1,0:T(8,128)(2,1)S(1)}, bf16[1024,1024]{1,0:T(8,128)(2,1)}, u32[]{:S(2)}) %copy-start.1) | copy-done | bytes 2097176
  100.2 1.6 %copy-done.2 = bf16[1024,1024]{1,0:T(8,128)(2,1)S(1)} copy-done((bf16[1024,1024]{1,0:T(8,128)(2,1)S(1)}, bf16[1024,1024]{1,0:T(8,128)(2,1)}, u32[]{:S(2)}) %copy-start.2) | copy-done | bytes 2097176
  101.8 1.9 %shard_map.139 = f32[16,1024]{1,0:T(8,128)} custom-call(bf16[32,1024]{1,0:T(8,128)(2,1)S(1)} %slice.133.sums_ref, bf16[16,1024]{1,0:T(8,128)(2,1)S(1)} %bitcast.108, bf16[1024,1024]{1,0:T(8,128)(2,1)S(1)} %copy-done.2, bf16[1024,1024]{1,0:T(8,128)(2,1)S(1)} %copy-done.1), custom_call_target="tpu_custom_call" | custom-call | flops 70000000 | bytes 4300000 | tf_op jit(solution)/shard_map/pallas_call | solution.py:202
  103.7 0.1 pad_maximum_fusion.1
  103.9 0.8 fusion
  104.7 0.7 maximum_convert_fusion.1
  105.5 0.1 copy.50
  105.6 0.7 copy.52
  (77 shorter events, 0.8 us)
Async XLA Ops:
  0.6 43.0 %copy-start = (bf16[1024,1024]{1,0:T(8,128)(2,1)S(1)}, bf16[1024,1024]{1,0:T(8,128)(2,1)}, u32[]{:S(2)}) copy-start(bf16[1024,1024]{1,0:T(8,128)(2,1)} %param.18) | copy-start | bytes 6291460
  3.4 15.8 %collective-permute-start.8 = (bf16[800,128]{1,0:T(8,128)(2,1)S(1)}, bf16[800,128]{1,0:T(8,128)(2,1)S(1)}, u32[]{:S(2)}, u32[]{:S(2)}) collective-permute-start(bf16[800,128]{1,0:T(8,128)(2,1)S(1)} %get-tuple-element.68), channel_id=1, source_target_pairs={{0,16},{8,24},{16,0},{24,8},{1,17},{9,25},{17,1},{25,9},{2,18},{10... | collective-permute-start | bytes 614408 | tf_op jit(solution)/shard_map/ppermute | solution.py:23
  7.8 12.0 %collective-permute-start.2 = (bf16[2,16,1024]{2,1,0:T(8,128)(2,1)S(1)}, bf16[2,16,1024]{2,1,0:T(8,128)(2,1)S(1)}, u32[]{:S(2)}, u32[]{:S(2)}) collective-permute-start(bf16[2,16,1024]{2,1,0:T(8,128)(2,1)S(1)} %bitcast.116), channel_id=1, source_target_pairs={{0,2},{2,4},{4,6},{6,0},{1,3},{3,5},{5,7},{7,1},{8,10},{10,12},{12... | collective-permute-start | bytes 196616 | tf_op jit(solution)/shard_map/ppermute | solution.py:23
  10.8 11.5 %collective-permute-start = (bf16[2,16,1024]{2,1,0:T(8,128)(2,1)S(1)}, bf16[2,16,1024]{2,1,0:T(8,128)(2,1)S(1)}, u32[]{:S(2)}, u32[]{:S(2)}) collective-permute-start(bf16[2,16,1024]{2,1,0:T(8,128)(2,1)S(1)} %bitcast.117), channel_id=1, source_target_pairs={{0,6},{2,0},{4,2},{6,4},{1,7},{3,1},{5,3},{7,5},{8,14},{10,8},{12,... | collective-permute-start | bytes 196616 | tf_op jit(solution)/shard_map/ppermute | solution.py:23
  13.9 8.4 %collective-permute-start.1 = (bf16[2,16,1024]{2,1,0:T(8,128)(2,1)S(1)}, bf16[2,16,1024]{2,1,0:T(8,128)(2,1)S(1)}, u32[]{:S(2)}, u32[]{:S(2)}) collective-permute-start(bf16[2,16,1024]{2,1,0:T(8,128)(2,1)S(1)} %bitcast.118), channel_id=1, source_target_pairs={{0,4},{2,6},{4,0},{6,2},{1,5},{3,7},{5,1},{7,3},{8,12},{10,14},{12... | collective-permute-start | bytes 196616 | tf_op jit(solution)/shard_map/ppermute | solution.py:23
  18.3 6.2 %collective-permute-start.6 = (bf16[800,128]{1,0:T(8,128)(2,1)S(1)}, bf16[800,128]{1,0:T(8,128)(2,1)S(1)}, u32[]{:S(2)}, u32[]{:S(2)}) collective-permute-start(bf16[800,128]{1,0:T(8,128)(2,1)S(1)} %get-tuple-element.68), channel_id=1, source_target_pairs={{0,24},{8,0},{16,8},{24,16},{1,25},{9,1},{17,9},{25,17},{2,26},{10... | collective-permute-start | bytes 614408 | tf_op jit(solution)/shard_map/ppermute | solution.py:23
  19.2 6.0 %collective-permute-start.7 = (bf16[800,128]{1,0:T(8,128)(2,1)S(1)}, bf16[800,128]{1,0:T(8,128)(2,1)S(1)}, u32[]{:S(2)}, u32[]{:S(2)}) collective-permute-start(bf16[800,128]{1,0:T(8,128)(2,1)S(1)} %get-tuple-element.68), channel_id=1, source_target_pairs={{0,8},{8,16},{16,24},{24,0},{1,9},{9,17},{17,25},{25,1},{2,10},{10... | collective-permute-start | bytes 614408 | tf_op jit(solution)/shard_map/ppermute | solution.py:23
  19.9 19.5 %collective-permute-start.9 = (bf16[2,800,128]{2,1,0:T(8,128)(2,1)S(1)}, bf16[2,800,128]{2,1,0:T(8,128)(2,1)S(1)}, u32[]{:S(2)}, u32[]{:S(2)}) collective-permute-start(bf16[2,800,128]{2,1,0:T(8,128)(2,1)S(1)} %pad_maximum_fusion.3.edge_ref), channel_id=1, source_target_pairs={{0,1},{1,0},{2,3},{3,2},{4,5},{5,4},{6,7},{7,6},{8,9},{9,8},{10,11... | collective-permute-start | bytes 1228808 | tf_op jit(solution)/shard_map/ppermute | solution.py:23
  22.4 8.2 %collective-permute-start.3 = (bf16[4,2,16,1024]{3,2,1,0:T(8,128)(2,1)S(1)}, bf16[4,2,16,1024]{3,2,1,0:T(8,128)(2,1)S(1)}, u32[]{:S(2)}, u32[]{:S(2)}) collective-permute-start(bf16[4,2,16,1024]{3,2,1,0:T(8,128)(2,1)S(1)} %get-tuple-element.66), channel_id=1, source_target_pairs={{0,24},{8,0},{16,8},{24,16},{1,25},{9,1},{17,9},{25,17},{2,26},{10... | collective-permute-start | bytes 786440 | tf_op jit(solution)/shard_map/ppermute | solution.py:23
  24.5 8.6 %collective-permute-start.4 = (bf16[4,2,16,1024]{3,2,1,0:T(8,128)(2,1)S(1)}, bf16[4,2,16,1024]{3,2,1,0:T(8,128)(2,1)S(1)}, u32[]{:S(2)}, u32[]{:S(2)}) collective-permute-start(bf16[4,2,16,1024]{3,2,1,0:T(8,128)(2,1)S(1)} %get-tuple-element.66), channel_id=1, source_target_pairs={{0,16},{8,24},{16,0},{24,8},{1,17},{9,25},{17,1},{25,9},{2,18},{10... | collective-permute-start | bytes 786440 | tf_op jit(solution)/shard_map/ppermute | solution.py:23
  24.5 14.7 %collective-permute-start.5 = (bf16[4,2,16,1024]{3,2,1,0:T(8,128)(2,1)S(1)}, bf16[4,2,16,1024]{3,2,1,0:T(8,128)(2,1)S(1)}, u32[]{:S(2)}, u32[]{:S(2)}) collective-permute-start(bf16[4,2,16,1024]{3,2,1,0:T(8,128)(2,1)S(1)} %get-tuple-element.66), channel_id=1, source_target_pairs={{0,8},{8,16},{16,24},{24,0},{1,9},{9,17},{17,25},{25,1},{2,10},{10... | collective-permute-start | bytes 786440 | tf_op jit(solution)/shard_map/ppermute | solution.py:23
  39.4 0.8 copy-start.5
  40.2 3.4 %collective-permute-start.11 = (bf16[4,4,2,16,1024]{4,3,2,1,0:T(8,128)(2,1)S(1)}, bf16[4,4,2,16,1024]{4,3,2,1,0:T(8,128)(2,1)}, u32[]{:S(2)}, u32[]{:S(2)}) collective-permute-start(bf16[4,4,2,16,1024]{4,3,2,1,0:T(8,128)(2,1)S(1)} %pad_maximum_fusion.mine_ref), channel_id=1, source_target_pairs={{0,1},{1,0},{2,3},{3,2},{4,5},{5,4},{6,7},{7,6},{8,9},{9,8},{10,11... | collective-permute-start | bytes 3145736 | tf_op jit(solution)/shard_map/ppermute | solution.py:23
  41.0 2.2 %copy-start.3 = (bf16[2,800,128]{2,1,0:T(8,128)(2,1)S(1)}, bf16[2,800,128]{2,1,0:T(8,128)(2,1)}, u32[]{:S(2)}) copy-start(bf16[2,800,128]{2,1,0:T(8,128)(2,1)} %pad_maximum_fusion.2.edge_ref) | copy-start | bytes 1228804
  41.0 2.6 %copy-start.6 = (bf16[2,800,128]{2,1,0:T(8,128)(2,1)S(1)}, bf16[2,800,128]{2,1,0:T(8,128)(2,1)}, u32[]{:S(2)}) copy-start(bf16[2,800,128]{2,1,0:T(8,128)(2,1)} %copy-done.5) | copy-start | bytes 1228804
  43.2 6.4 %collective-permute-start.10 = (bf16[2,800,128]{2,1,0:T(8,128)(2,1)S(1)}, bf16[2,800,128]{2,1,0:T(8,128)(2,1)S(1)}, u32[]{:S(2)}, u32[]{:S(2)}) collective-permute-start(bf16[2,800,128]{2,1,0:T(8,128)(2,1)S(1)} %copy-done.3), channel_id=1, source_target_pairs={{0,1},{1,0},{2,3},{3,2},{4,5},{5,4},{6,7},{7,6},{8,9},{9,8},{10,11... | collective-permute-start | bytes 1228808 | tf_op jit(solution)/shard_map/ppermute | solution.py:23
  54.4 7.7 %collective-permute-start.12 = (bf16[800,128]{1,0:T(8,128)(2,1)S(1)}, bf16[800,128]{1,0:T(8,128)(2,1)S(1)}, u32[]{:S(2)}, u32[]{:S(2)}) collective-permute-start(bf16[800,128]{1,0:T(8,128)(2,1)S(1)} %get-tuple-element.44), channel_id=1, source_target_pairs={{0,32},{32,64},{64,96},{96,0},{1,33},{33,65},{65,97},{97,1},{2,34}... | collective-permute-start | bytes 614408 | tf_op jit(solution)/shard_map/ppermute | solution.py:23
  55.8 11.8 %collective-permute-start.13 = (bf16[800,128]{1,0:T(8,128)(2,1)S(1)}, bf16[800,128]{1,0:T(8,128)(2,1)}, u32[]{:S(2)}, u32[]{:S(2)}) collective-permute-start(bf16[800,128]{1,0:T(8,128)(2,1)S(1)} %get-tuple-element.45), channel_id=1, source_target_pairs={{0,64},{32,96},{64,0},{96,32},{1,65},{33,97},{65,1},{97,33},{2,66}... | collective-permute-start | bytes 614408 | tf_op jit(solution)/shard_map/ppermute | solution.py:23
  58.4 9.2 %collective-permute-start.14 = (bf16[800,128]{1,0:T(8,128)(2,1)S(1)}, bf16[800,128]{1,0:T(8,128)(2,1)}, u32[]{:S(2)}, u32[]{:S(2)}) collective-permute-start(bf16[800,128]{1,0:T(8,128)(2,1)S(1)} %get-tuple-element.46), channel_id=1, source_target_pairs={{0,96},{32,0},{64,32},{96,64},{1,97},{33,1},{65,33},{97,65},{2,98}... | collective-permute-start | bytes 614408 | tf_op jit(solution)/shard_map/ppermute | solution.py:23
  59.5 12.2 %collective-permute-start.18 = (bf16[4,2,2,16,128]{4,3,2,1,0:T(8,128)(2,1)S(1)}, bf16[4,2,2,16,128]{4,3,2,1,0:T(8,128)(2,1)S(1)}, u32[]{:S(2)}, u32[]{:S(2)}) collective-permute-start(bf16[4,2,2,16,128]{4,3,2,1,0:T(8,128)(2,1)S(1)} %get-tuple-element.48), channel_id=1, source_target_pairs={{0,2},{2,4},{4,6},{6,0},{1,3},{3,5},{5,7},{7,1},{8,10},{10,12},{12... | collective-permute-start | bytes 196616 | tf_op jit(solution)/shard_map/ppermute | solution.py:23
  59.5 15.7 %collective-permute-start.19 = (bf16[4,2,2,16,128]{4,3,2,1,0:T(8,128)(2,1)S(1)}, bf16[4,2,2,16,128]{4,3,2,1,0:T(8,128)(2,1)S(1)}, u32[]{:S(2)}, u32[]{:S(2)}) collective-permute-start(bf16[4,2,2,16,128]{4,3,2,1,0:T(8,128)(2,1)S(1)} %get-tuple-element.49), channel_id=1, source_target_pairs={{0,4},{2,6},{4,0},{6,2},{1,5},{3,7},{5,1},{7,3},{8,12},{10,14},{12... | collective-permute-start | bytes 196616 | tf_op jit(solution)/shard_map/ppermute | solution.py:23
  62.1 13.0 %collective-permute-start.20 = (bf16[4,2,2,16,128]{4,3,2,1,0:T(8,128)(2,1)S(1)}, bf16[4,2,2,16,128]{4,3,2,1,0:T(8,128)(2,1)S(1)}, u32[]{:S(2)}, u32[]{:S(2)}) collective-permute-start(bf16[4,2,2,16,128]{4,3,2,1,0:T(8,128)(2,1)S(1)} %get-tuple-element.50), channel_id=1, source_target_pairs={{0,6},{2,0},{4,2},{6,4},{1,7},{3,1},{5,3},{7,5},{8,14},{10,8},{12,... | collective-permute-start | bytes 196616 | tf_op jit(solution)/shard_map/ppermute | solution.py:23
  68.9 6.3 %collective-permute-start.15 = (bf16[224,128]{1,0:T(8,128)(2,1)S(1)}, bf16[224,128]{1,0:T(8,128)(2,1)S(1)}, u32[]{:S(2)}, u32[]{:S(2)}) collective-permute-start(bf16[224,128]{1,0:T(8,128)(2,1)S(1)} %get-tuple-element.104), channel_id=1, source_target_pairs={{0,2},{2,4},{4,6},{6,0},{1,3},{3,5},{5,7},{7,1},{8,10},{10,12},{12... | collective-permute-start | bytes 172040 | tf_op jit(solution)/shard_map/ppermute | solution.py:23
  69.0 7.7 %collective-permute-start.16 = (bf16[224,128]{1,0:T(8,128)(2,1)S(1)}, bf16[224,128]{1,0:T(8,128)(2,1)S(1)}, u32[]{:S(2)}, u32[]{:S(2)}) collective-permute-start(bf16[224,128]{1,0:T(8,128)(2,1)S(1)} %get-tuple-element.105), channel_id=1, source_target_pairs={{0,4},{2,6},{4,0},{6,2},{1,5},{3,7},{5,1},{7,3},{8,12},{10,14},{12... | collective-permute-start | bytes 172040 | tf_op jit(solution)/shard_map/ppermute | solution.py:23
  71.7 5.8 %collective-permute-start.17 = (bf16[224,128]{1,0:T(8,128)(2,1)S(1)}, bf16[224,128]{1,0:T(8,128)(2,1)S(1)}, u32[]{:S(2)}, u32[]{:S(2)}) collective-permute-start(bf16[224,128]{1,0:T(8,128)(2,1)S(1)} %get-tuple-element.103), channel_id=1, source_target_pairs={{0,6},{2,0},{4,2},{6,4},{1,7},{3,1},{5,3},{7,5},{8,14},{10,8},{12,... | collective-permute-start | bytes 172040 | tf_op jit(solution)/shard_map/ppermute | solution.py:23
  77.6 3.5 %collective-permute-start.21 = (bf16[224,128]{1,0:T(8,128)(2,1)S(1)}, bf16[224,128]{1,0:T(8,128)(2,1)S(1)}, u32[]{:S(2)}, u32[]{:S(2)}) collective-permute-start(bf16[224,128]{1,0:T(8,128)(2,1)S(1)} %pad_maximum_fusion.20), channel_id=1, source_target_pairs={{0,128},{128,0},{1,129},{129,1},{2,130},{130,2},{3,131},{131,3},{4... | collective-permute-start | bytes 172040 | tf_op jit(solution)/shard_map/ppermute | solution.py:23
  81.2 4.6 %collective-permute-start.22 = (bf16[128,128]{1,0:T(8,128)(2,1)S(1)}, bf16[128,128]{1,0:T(8,128)(2,1)S(1)}, u32[]{:S(2)}, u32[]{:S(2)}) collective-permute-start(bf16[128,128]{1,0:T(8,128)(2,1)S(1)} %get-tuple-element.100), channel_id=1, source_target_pairs={{0,8},{8,16},{16,24},{24,0},{1,9},{9,17},{17,25},{25,1},{2,10},{10... | collective-permute-start | bytes 98312 | tf_op jit(solution)/shard_map/ppermute | solution.py:23
  81.9 5.4 %collective-permute-start.23 = (bf16[128,128]{1,0:T(8,128)(2,1)S(1)}, bf16[128,128]{1,0:T(8,128)(2,1)S(1)}, u32[]{:S(2)}, u32[]{:S(2)}) collective-permute-start(bf16[128,128]{1,0:T(8,128)(2,1)S(1)} %get-tuple-element.101), channel_id=1, source_target_pairs={{0,16},{8,24},{16,0},{24,8},{1,17},{9,25},{17,1},{25,9},{2,18},{10... | collective-permute-start | bytes 98312 | tf_op jit(solution)/shard_map/ppermute | solution.py:23
  85.7 2.8 %collective-permute-start.24 = (bf16[128,128]{1,0:T(8,128)(2,1)S(1)}, bf16[128,128]{1,0:T(8,128)(2,1)S(1)}, u32[]{:S(2)}, u32[]{:S(2)}) collective-permute-start(bf16[128,128]{1,0:T(8,128)(2,1)S(1)} %get-tuple-element.102), channel_id=1, source_target_pairs={{0,24},{8,0},{16,8},{24,16},{1,25},{9,1},{17,9},{25,17},{2,26},{10... | collective-permute-start | bytes 98312 | tf_op jit(solution)/shard_map/ppermute | solution.py:23
  88.6 10.1 %copy-start.4 = (bf16[1,16,1024]{2,1,0:T(8,128)(2,1)S(1)}, bf16[1,16,1024]{2,1,0:T(8,128)(2,1)}, u32[]{:S(2)}) copy-start(bf16[1,16,1024]{2,1,0:T(8,128)(2,1)} %param.11) | copy-start | bytes 98308
  88.6 4.7 %collective-permute-start.25 = (bf16[4,80,128]{2,1,0:T(8,128)(2,1)S(1)}, bf16[4,80,128]{2,1,0:T(8,128)(2,1)S(1)}, u32[]{:S(2)}, u32[]{:S(2)}) collective-permute-start(bf16[4,80,128]{2,1,0:T(8,128)(2,1)S(1)} %get-tuple-element.71), channel_id=1, source_target_pairs={{0,1},{1,0},{2,3},{3,2},{4,5},{5,4},{6,7},{7,6},{8,9},{9,8},{10,11... | collective-permute-start | bytes 245768 | tf_op jit(solution)/shard_map/ppermute | solution.py:23
  93.9 9.9 %collective-permute-start.26 = (bf16[56,1024]{1,0:T(8,128)(2,1)S(1)}, bf16[56,1024]{1,0:T(8,128)(2,1)S(1)}, u32[]{:S(2)}, u32[]{:S(2)}) collective-permute-start(bf16[56,1024]{1,0:T(8,128)(2,1)S(1)} %get-tuple-element.82), channel_id=1, source_target_pairs={{0,32},{32,64},{64,96},{96,0},{1,33},{33,65},{65,97},{97,1},{2,34}... | collective-permute-start | bytes 344072 | tf_op jit(solution)/shard_map/ppermute | solution.py:23
  95.0 8.7 %collective-permute-start.27 = (bf16[56,1024]{1,0:T(8,128)(2,1)S(1)}, bf16[56,1024]{1,0:T(8,128)(2,1)S(1)}, u32[]{:S(2)}, u32[]{:S(2)}) collective-permute-start(bf16[56,1024]{1,0:T(8,128)(2,1)S(1)} %get-tuple-element.82), channel_id=1, source_target_pairs={{0,64},{32,96},{64,0},{96,32},{1,65},{33,97},{65,1},{97,33},{2,66}... | collective-permute-start | bytes 344072 | tf_op jit(solution)/shard_map/ppermute | solution.py:23
  97.9 5.9 %collective-permute-start.28 = (bf16[56,1024]{1,0:T(8,128)(2,1)S(1)}, bf16[56,1024]{1,0:T(8,128)(2,1)S(1)}, u32[]{:S(2)}, u32[]{:S(2)}) collective-permute-start(bf16[56,1024]{1,0:T(8,128)(2,1)S(1)} %get-tuple-element.82), channel_id=1, source_target_pairs={{0,96},{32,0},{64,32},{96,64},{1,97},{33,1},{65,33},{97,65},{2,98}... | collective-permute-start | bytes 344072 | tf_op jit(solution)/shard_map/ppermute | solution.py:23
  98.6 1.6 %copy-start.1 = (bf16[1024,1024]{1,0:T(8,128)(2,1)S(1)}, bf16[1024,1024]{1,0:T(8,128)(2,1)}, u32[]{:S(2)}) copy-start(bf16[1024,1024]{1,0:T(8,128)(2,1)} %wt_ref.1) | copy-start | bytes 6291460
  100.2 1.6 %copy-start.2 = (bf16[1024,1024]{1,0:T(8,128)(2,1)S(1)}, bf16[1024,1024]{1,0:T(8,128)(2,1)}, u32[]{:S(2)}) copy-start(bf16[1024,1024]{1,0:T(8,128)(2,1)} %ws_ref.1) | copy-start | bytes 6291460

commit v4 on v3

--- a/solution.py
+++ b/solution.py
@@ -191,22 +191,21 @@
     )(at, late, late_sib, *state)
 
 
-def node_kernel(sums_ref, cotan_ref, ws_ref, wt_ref, out_ref):
-    out_ref[...] = cotan_ref[...].astype(F32) + (
-        dot(ws_ref[...], sums_ref[:16], ((1,), (1,))) + dot(wt_ref[...], sums_ref[16:], ((1,), (1,)))
-    ).T
-
-
-def node_pass(sums, cotan, ws, wt):
+def node_kernel(sums_ref, start_ref, w_ref, out_ref):
+    push = dot(w_ref[...], sums_ref[...], ((1,), (1,)))
+    out_ref[...] = start_ref[...].astype(F32) + push.T
+
+
+def node_pass(sums, start, weight):
     vmem = pl.BlockSpec(memory_space=pltpu.VMEM)
     return pl.pallas_call(
         node_kernel,
-        in_specs=[vmem] * 4,
+        in_specs=[vmem] * 3,
         out_specs=vmem,
         out_shape=jax.ShapeDtypeStruct((16, 1024), F32),
         compiler_params=pltpu.CompilerParams(vmem_limit_bytes=8 * 1024 * 1024),
-        cost_estimate=pl.CostEstimate(flops=70_000_000, bytes_accessed=4_300_000, transcendentals=0),
-    )(sums, cotan, ws, wt)
+        cost_estimate=pl.CostEstimate(flops=35_000_000, bytes_accessed=2_200_000, transcendentals=0),
+    )(sums, start, weight)
 
 
 def per_device(
@@ -269,7 +268,8 @@
     both = jnp.stack(trade([c_piece(0), c_piece(1)], "core"))
     both = jnp.stack([pick(both, my_c, 0), pick(both, 1 - my_c, 0)])
     rows = natural(both.transpose(2, 1, 0, 3).reshape(80, 4, 2, 128), 80)
-    node_grad = node_pass(rows[:32], cotan, w_source, w_target)
+    node_grad = node_pass(rows[:16], cotan, w_source)
+    node_grad = node_pass(rows[16:32], node_grad, w_target)
     rows = in_order(trade([jnp.concatenate([rows[32:], w_o])] * 4, "y"), my_y).astype(F32)
     grad_out = rows[:, 48:].reshape(2, 2, 16, 512).transpose(1, 2, 0, 3).reshape(32, 1024)
     return (

time: 107 us -> 106 us (level)
  transfers between devices with their start and end apart: 29 -> 29, of which waited for: 11 -> 10; matrix products, arithmetic and copies ran while one was open for 6% -> 6% of each run, Pallas kernels for 7% -> 8%
where the time goes in v4:
time: 106 us
  starting transfers between devices  53.7 us (51%)
  waiting for transfers between devices  22.7 us (21%)
  Pallas kernels  12.8 us (12%)
  local copies, waits for them, and re-layouts  8.04 us (8%)
  other arithmetic  6.81 us (6%)
  between operations  1.93 us (2%)
    ppermute x29, starting transfers between devices, send(): lax.ppermute(array, axis, [(i, (i + offset) % size) for i in range(size)])  53.7 us
    ppermute x29, waiting for transfers between devices, send(): lax.ppermute(array, axis, [(i, (i + offset) % size) for i in range(size)])  22.7 us
    pallas_call x1, Pallas kernels, edge_pass(): pl.pallas_call(first_kernel, in_specs=[smem] + [vmem] * 8, out_specs=[vme...  5.95 us
    pallas_call x1, Pallas kernels, edge_pass(): pl.pallas_call(second_kernel, in_specs=[smem] + [vmem] * 10, out_specs=[v...  4.82 us
    unnamed x15, local copies, waits for them, and re-layouts  3.95 us
    dynamic_slice x3, local copies, waits for them, and re-layouts, mine(): return lax.dynamic_slice_in_dim(weight, my_x * 256, 256, axis)  2.23 us
  transfers between devices with their start and end apart: 29, of which 10 were waited for; matrix products, arithmetic and copies ran while one was open for 6% of the time, Pallas kernels for 8%

profile of v4, /device:TPU:1, one launch (start us, length us, event | category | flops | bytes accessed | tf_op | source)
XLA Modules:
  0.0 106.0 jit_solution(11170971837820453718)
XLA Ops:
  1.5 0.7 shift-right-arithmetic_convert_fusion
  2.3 1.1 %fusion.18 = (bf16[1,800,128]{2,1,0:T(8,128)(2,1)S(1)}, bf16[800,128]{1,0:T(8,128)(2,1)S(1)}) fusion(bf16[800]{0:T(1024)(128)(2,1)S(1)} %pad.64.clone, bf16[24,128]{1,0:T(8,128)(2,1)S(1)} %convert_element_type.76, bf16[768,128]{1,0:T(8,128)(2,1)} %bitcast.127), kind=kLoop, calls=%fused_computation.101 | loop fusion | flops 614400 | bytes 613952 | tf_op jit(solution)/shard_map/stack | solution.py:225
  3.4 3.7 %collective-permute-start.8 = (bf16[800,128]{1,0:T(8,128)(2,1)S(1)}, bf16[800,128]{1,0:T(8,128)(2,1)S(1)}, u32[]{:S(2)}, u32[]{:S(2)}) collective-permute-start(bf16[800,128]{1,0:T(8,128)(2,1)S(1)} %get-tuple-element.70), channel_id=1, source_target_pairs={{0,16},{8,24},{16,0},{24,8},{1,17},{9,25},{17,1},{25,9},{2,18},{10... | collective-permute-start | bytes 614408 | tf_op jit(solution)/shard_map/ppermute | solution.py:23
  7.1 0.8 pad_maximum_fusion.15
  7.8 3.0 %collective-permute-start.2 = (bf16[2,16,1024]{2,1,0:T(8,128)(2,1)S(1)}, bf16[2,16,1024]{2,1,0:T(8,128)(2,1)S(1)}, u32[]{:S(2)}, u32[]{:S(2)}) collective-permute-start(bf16[2,16,1024]{2,1,0:T(8,128)(2,1)S(1)} %bitcast.115), channel_id=1, source_target_pairs={{0,2},{2,4},{4,6},{6,0},{1,3},{3,5},{5,7},{7,1},{8,10},{10,12},{12... | collective-permute-start | bytes 196616 | tf_op jit(solution)/shard_map/ppermute | solution.py:23
  10.8 3.1 %collective-permute-start = (bf16[2,16,1024]{2,1,0:T(8,128)(2,1)S(1)}, bf16[2,16,1024]{2,1,0:T(8,128)(2,1)S(1)}, u32[]{:S(2)}, u32[]{:S(2)}) collective-permute-start(bf16[2,16,1024]{2,1,0:T(8,128)(2,1)S(1)} %bitcast.116), channel_id=1, source_target_pairs={{0,6},{2,0},{4,2},{6,4},{1,7},{3,1},{5,3},{7,5},{8,14},{10,8},{12,... | collective-permute-start | bytes 196616 | tf_op jit(solution)/shard_map/ppermute | solution.py:23
  13.9 4.4 %collective-permute-start.1 = (bf16[2,16,1024]{2,1,0:T(8,128)(2,1)S(1)}, bf16[2,16,1024]{2,1,0:T(8,128)(2,1)S(1)}, u32[]{:S(2)}, u32[]{:S(2)}) collective-permute-start(bf16[2,16,1024]{2,1,0:T(8,128)(2,1)S(1)} %bitcast.117), channel_id=1, source_target_pairs={{0,4},{2,6},{4,0},{6,2},{1,5},{3,7},{5,1},{7,3},{8,12},{10,14},{12... | collective-permute-start | bytes 196616 | tf_op jit(solution)/shard_map/ppermute | solution.py:23
  18.3 0.9 collective-permute-start.6
  19.2 0.6 collective-permute-start.7
  19.9 2.4 %collective-permute-start.9 = (bf16[2,800,128]{2,1,0:T(8,128)(2,1)S(1)}, bf16[2,800,128]{2,1,0:T(8,128)(2,1)S(1)}, u32[]{:S(2)}, u32[]{:S(2)}) collective-permute-start(bf16[2,800,128]{2,1,0:T(8,128)(2,1)S(1)} %pad_maximum_fusion.3.edge_ref), channel_id=1, source_target_pairs={{0,1},{1,0},{2,3},{3,2},{4,5},{5,4},{6,7},{7,6},{8,9},{9,8},{10,11... | collective-permute-start | bytes 1228808 | tf_op jit(solution)/shard_map/ppermute | solution.py:23
  22.4 2.1 %collective-permute-start.3 = (bf16[4,2,16,1024]{3,2,1,0:T(8,128)(2,1)S(1)}, bf16[4,2,16,1024]{3,2,1,0:T(8,128)(2,1)S(1)}, u32[]{:S(2)}, u32[]{:S(2)}) collective-permute-start(bf16[4,2,16,1024]{3,2,1,0:T(8,128)(2,1)S(1)} %get-tuple-element.68), channel_id=1, source_target_pairs={{0,24},{8,0},{16,8},{24,16},{1,25},{9,1},{17,9},{25,17},{2,26},{10... | collective-permute-start | bytes 786440 | tf_op jit(solution)/shard_map/ppermute | solution.py:23
  24.5 0.6 collective-permute-start.5
  25.2 0.8 pad_maximum_fusion.2.edge_ref
  26.0 4.6 %collective-permute-done.3 = bf16[4,2,16,1024]{3,2,1,0:T(8,128)(2,1)S(1)} collective-permute-done((bf16[4,2,16,1024]{3,2,1,0:T(8,128)(2,1)S(1)}, bf16[4,2,16,1024]{3,2,1,0:T(8,128)(2,1)S(1)}, u32[]{:S(2)}, u32[]{:S(2)}) %collective-permute-start.3) | collective-permute-done | bytes 262176 | tf_op jit(solution)/shard_map/ppermute | solution.py:23
  30.6 2.5 %collective-permute-done.4 = bf16[4,2,16,1024]{3,2,1,0:T(8,128)(2,1)S(1)} collective-permute-done((bf16[4,2,16,1024]{3,2,1,0:T(8,128)(2,1)S(1)}, bf16[4,2,16,1024]{3,2,1,0:T(8,128)(2,1)S(1)}, u32[]{:S(2)}, u32[]{:S(2)}) %collective-permute-start.4) | collective-permute-done | bytes 262176 | tf_op jit(solution)/shard_map/ppermute | solution.py:23
  33.1 6.2 %collective-permute-done.5 = bf16[4,2,16,1024]{3,2,1,0:T(8,128)(2,1)S(1)} collective-permute-done((bf16[4,2,16,1024]{3,2,1,0:T(8,128)(2,1)S(1)}, bf16[4,2,16,1024]{3,2,1,0:T(8,128)(2,1)S(1)}, u32[]{:S(2)}, u32[]{:S(2)}) %collective-permute-start.5) | collective-permute-done | bytes 262176 | tf_op jit(solution)/shard_map/ppermute | solution.py:23
  39.3 0.1 pad_maximum_fusion.mine_ref
  39.4 0.8 copy-done.5
  40.2 0.8 collective-permute-start.11
  41.0 0.9 constant_dynamic-slice_fusion.20.wr
  41.9 1.3 %constant_dynamic-slice_fusion.22 = (bf16[1024,256]{1,0:T(8,128)(2,1)S(1)}, bf16[1024,256]{1,0:T(8,128)(2,1)S(1)}) fusion(bf16[1024,1024]{1,0:T(8,128)(2,1)} %w_ref.3, s32[]{:T(128)S(6)} %select_n.154, bf16[1024,1024]{1,0:T(8,128)(2,1)} %w_ref.2), kind=kLoop, calls=%fused_computation.82 | loop fusion | bytes 2097156 | tf_op jit(solution)/shard_map/dynamic_slice | solution.py:230
  43.2 0.3 collective-permute-start.10
  43.5 0.1 pad_add_fusion.at_ref
  43.7 5.9 %shard_map.137 = (bf16[512,1024]{1,0:T(8,128)(2,1)S(1)}, bf16[512,1024]{1,0:T(8,128)(2,1)S(1)}, bf16[128,512]{1,0:T(8,128)(2,1)S(1)}, bf16[256,512]{1,0:T(8,128)...) custom-call(s32[4]{0:T(128)S(1)} %pad_add_fusion.at_ref, ...), custom_call_target="tpu_custom_call" | custom-call | flops 3000000000 | bytes 4000000 | tf_op jit(solution)/shard_map/pallas_call | solution.py:166
  49.6 4.8 %shard_map.138 = (bf16[4,2,2,16,128]{4,3,2,1,0:T(8,128)(2,1)S(1)}, bf16[4,2,2,16,128]{4,3,2,1,0:T(8,128)(2,1)S(1)}, bf16[4,2,2,16,128]{4,3,2,1,0:T(8,128)(2,1)S(...) custom-call(s32[4]{0:T(128)S(1)} %pad_add_fusion.at_ref, ...), custom_call_target="tpu_custom_call" | custom-call | flops 3000000000 | bytes 4000000 | tf_op jit(solution)/shard_map/pallas_call | solution.py:181
  54.4 1.4 %collective-permute-start.12 = (bf16[800,128]{1,0:T(8,128)(2,1)S(1)}, bf16[800,128]{1,0:T(8,128)(2,1)S(1)}, u32[]{:S(2)}, u32[]{:S(2)}) collective-permute-start(bf16[800,128]{1,0:T(8,128)(2,1)S(1)} %get-tuple-element.44), channel_id=1, source_target_pairs={{0,32},{32,64},{64,96},{96,0},{1,33},{33,65},{65,97},{97,1},{2,34}... | collective-permute-start | bytes 614408 | tf_op jit(solution)/shard_map/ppermute | solution.py:23
  55.8 2.6 %collective-permute-start.13 = (bf16[800,128]{1,0:T(8,128)(2,1)S(1)}, bf16[800,128]{1,0:T(8,128)(2,1)}, u32[]{:S(2)}, u32[]{:S(2)}) collective-permute-start(bf16[800,128]{1,0:T(8,128)(2,1)S(1)} %get-tuple-element.45), channel_id=1, source_target_pairs={{0,64},{32,96},{64,0},{96,32},{1,65},{33,97},{65,1},{97,33},{2,66}... | collective-permute-start | bytes 614408 | tf_op jit(solution)/shard_map/ppermute | solution.py:23
  58.4 1.1 %collective-permute-start.14 = (bf16[800,128]{1,0:T(8,128)(2,1)S(1)}, bf16[800,128]{1,0:T(8,128)(2,1)}, u32[]{:S(2)}, u32[]{:S(2)}) collective-permute-start(bf16[800,128]{1,0:T(8,128)(2,1)S(1)} %get-tuple-element.46), channel_id=1, source_target_pairs={{0,96},{32,0},{64,32},{96,64},{1,97},{33,1},{65,33},{97,65},{2,98}... | collective-permute-start | bytes 614408 | tf_op jit(solution)/shard_map/ppermute | solution.py:23
  59.5 2.6 %collective-permute-start.19 = (bf16[4,2,2,16,128]{4,3,2,1,0:T(8,128)(2,1)S(1)}, bf16[4,2,2,16,128]{4,3,2,1,0:T(8,128)(2,1)S(1)}, u32[]{:S(2)}, u32[]{:S(2)}) collective-permute-start(bf16[4,2,2,16,128]{4,3,2,1,0:T(8,128)(2,1)S(1)} %get-tuple-element.49), channel_id=1, source_target_pairs={{0,4},{2,6},{4,0},{6,2},{1,5},{3,7},{5,1},{7,3},{8,12},{10,14},{12... | collective-permute-start | bytes 196616 | tf_op jit(solution)/shard_map/ppermute | solution.py:23
  62.1 3.6 %collective-permute-start.20 = (bf16[4,2,2,16,128]{4,3,2,1,0:T(8,128)(2,1)S(1)}, bf16[4,2,2,16,128]{4,3,2,1,0:T(8,128)(2,1)S(1)}, u32[]{:S(2)}, u32[]{:S(2)}) collective-permute-start(bf16[4,2,2,16,128]{4,3,2,1,0:T(8,128)(2,1)S(1)} %get-tuple-element.50), channel_id=1, source_target_pairs={{0,6},{2,0},{4,2},{6,4},{1,7},{3,1},{5,3},{7,5},{8,14},{10,8},{12,... | collective-permute-start | bytes 196616 | tf_op jit(solution)/shard_map/ppermute | solution.py:23
  65.7 1.9 %collective-permute-done.13 = bf16[800,128]{1,0:T(8,128)(2,1)} collective-permute-done((bf16[800,128]{1,0:T(8,128)(2,1)S(1)}, bf16[800,128]{1,0:T(8,128)(2,1)}, u32[]{:S(2)}, u32[]{:S(2)}) %collective-permute-start.13) | collective-permute-done | bytes 204832 | tf_op jit(solution)/shard_map/ppermute | solution.py:23
  67.6 1.1 %add_convert_fusion = bf16[800,128]{1,0:T(8,128)(2,1)S(1)} fusion(bf16[800,128]{1,0:T(8,128)(2,1)} %collective-permute-done.14, bf16[800,128]{1,0:T(8,128)(2,1)} %collective-permute-done.13, bf16[800,128]{1,0:T(8,128)(2,1)S(1)} %collective-permute-done.12, bf16[800,128]{1,0:T(8,128)(2,1)S(1)} %get-tuple-element.43), kind=kLoop, calls=%fused_computation.4 | loop fusion | flops 819200 | bytes 1024000 | tf_op jit(solution)/shard_map/convert_element_type | solution.py:242
  68.9 0.1 collective-permute-start.15
  69.0 2.7 %collective-permute-start.16 = (bf16[224,128]{1,0:T(8,128)(2,1)S(1)}, bf16[224,128]{1,0:T(8,128)(2,1)S(1)}, u32[]{:S(2)}, u32[]{:S(2)}) collective-permute-start(bf16[224,128]{1,0:T(8,128)(2,1)S(1)} %get-tuple-element.107), channel_id=1, source_target_pairs={{0,4},{2,6},{4,0},{6,2},{1,5},{3,7},{5,1},{7,3},{8,12},{10,14},{12... | collective-permute-start | bytes 172040 | tf_op jit(solution)/shard_map/ppermute | solution.py:23
  71.7 3.5 %collective-permute-start.17 = (bf16[224,128]{1,0:T(8,128)(2,1)S(1)}, bf16[224,128]{1,0:T(8,128)(2,1)S(1)}, u32[]{:S(2)}, u32[]{:S(2)}) collective-permute-start(bf16[224,128]{1,0:T(8,128)(2,1)S(1)} %get-tuple-element.105), channel_id=1, source_target_pairs={{0,6},{2,0},{4,2},{6,4},{1,7},{3,1},{5,3},{7,5},{8,14},{10,8},{12,... | collective-permute-start | bytes 172040 | tf_op jit(solution)/shard_map/ppermute | solution.py:23
  75.2 1.5 %collective-permute-done.16 = bf16[224,128]{1,0:T(8,128)(2,1)S(1)} collective-permute-done((bf16[224,128]{1,0:T(8,128)(2,1)S(1)}, bf16[224,128]{1,0:T(8,128)(2,1)S(1)}, u32[]{:S(2)}, u32[]{:S(2)}) %collective-permute-start.16) | collective-permute-done | bytes 57376 | tf_op jit(solution)/shard_map/ppermute | solution.py:23
  76.8 2.0 %collective-permute-start.21 = (bf16[224,128]{1,0:T(8,128)(2,1)S(1)}, bf16[224,128]{1,0:T(8,128)(2,1)S(1)}, u32[]{:S(2)}, u32[]{:S(2)}) collective-permute-start(bf16[224,128]{1,0:T(8,128)(2,1)S(1)} %pad_maximum_fusion.20), channel_id=1, source_target_pairs={{0,128},{128,0},{1,129},{129,1},{2,130},{130,2},{3,131},{131,3},{4... | collective-permute-start | bytes 172040 | tf_op jit(solution)/shard_map/ppermute | solution.py:23
  78.8 2.3 %collective-permute-done.21 = bf16[224,128]{1,0:T(8,128)(2,1)S(1)} collective-permute-done((bf16[224,128]{1,0:T(8,128)(2,1)S(1)}, bf16[224,128]{1,0:T(8,128)(2,1)S(1)}, u32[]{:S(2)}, u32[]{:S(2)}) %collective-permute-start.21) | collective-permute-done | bytes 57376 | tf_op jit(solution)/shard_map/ppermute | solution.py:23
  81.2 0.7 collective-permute-start.22
  81.9 3.6 %collective-permute-start.23 = (bf16[128,128]{1,0:T(8,128)(2,1)S(1)}, bf16[128,128]{1,0:T(8,128)(2,1)S(1)}, u32[]{:S(2)}, u32[]{:S(2)}) collective-permute-start(bf16[128,128]{1,0:T(8,128)(2,1)S(1)} %get-tuple-element.103), channel_id=1, source_target_pairs={{0,16},{8,24},{16,0},{24,8},{1,17},{9,25},{17,1},{25,9},{2,18},{10... | collective-permute-start | bytes 98312 | tf_op jit(solution)/shard_map/ppermute | solution.py:23
  85.5 0.1 collective-permute-done.22
  85.6 1.5 %collective-permute-done.23 = bf16[128,128]{1,0:T(8,128)(2,1)S(1)} collective-permute-done((bf16[128,128]{1,0:T(8,128)(2,1)S(1)}, bf16[128,128]{1,0:T(8,128)(2,1)S(1)}, u32[]{:S(2)}, u32[]{:S(2)}) %collective-permute-start.23) | collective-permute-done | bytes 32800 | tf_op jit(solution)/shard_map/ppermute | solution.py:23
  87.1 1.1 %collective-permute-done.24 = bf16[128,128]{1,0:T(8,128)(2,1)S(1)} collective-permute-done((bf16[128,128]{1,0:T(8,128)(2,1)S(1)}, bf16[128,128]{1,0:T(8,128)(2,1)S(1)}, u32[]{:S(2)}, u32[]{:S(2)}) %collective-permute-start.24) | collective-permute-done | bytes 32800 | tf_op jit(solution)/shard_map/ppermute | solution.py:23
  88.4 3.9 %collective-permute-start.25 = (bf16[4,80,128]{2,1,0:T(8,128)(2,1)S(1)}, bf16[4,80,128]{2,1,0:T(8,128)(2,1)S(1)}, u32[]{:S(2)}, u32[]{:S(2)}) collective-permute-start(bf16[4,80,128]{2,1,0:T(8,128)(2,1)S(1)} %get-tuple-element.73), channel_id=1, source_target_pairs={{0,1},{1,0},{2,3},{3,2},{4,5},{5,4},{6,7},{7,6},{8,9},{9,8},{10,11... | collective-permute-start | bytes 245768 | tf_op jit(solution)/shard_map/ppermute | solution.py:23
  92.4 0.9 collective-permute-done.25
  93.4 0.2 copy.48
  93.6 0.1 slice.163
  93.7 0.1 copy.53
  93.9 1.1 %collective-permute-start.26 = (bf16[56,1024]{1,0:T(8,128)(2,1)S(1)}, bf16[56,1024]{1,0:T(8,128)(2,1)S(1)}, u32[]{:S(2)}, u32[]{:S(2)}) collective-permute-start(bf16[56,1024]{1,0:T(8,128)(2,1)S(1)} %get-tuple-element.84), channel_id=1, source_target_pairs={{0,32},{32,64},{64,96},{96,0},{1,33},{33,65},{65,97},{97,1},{2,34}... | collective-permute-start | bytes 344072 | tf_op jit(solution)/shard_map/ppermute | solution.py:23
  95.0 2.8 %collective-permute-start.27 = (bf16[56,1024]{1,0:T(8,128)(2,1)S(1)}, bf16[56,1024]{1,0:T(8,128)(2,1)S(1)}, u32[]{:S(2)}, u32[]{:S(2)}) collective-permute-start(bf16[56,1024]{1,0:T(8,128)(2,1)S(1)} %get-tuple-element.84), channel_id=1, source_target_pairs={{0,64},{32,96},{64,0},{96,32},{1,65},{33,97},{65,1},{97,33},{2,66}... | collective-permute-start | bytes 344072 | tf_op jit(solution)/shard_map/ppermute | solution.py:23
  97.9 0.1 collective-permute-start.28
  98.0 0.1 fusion.20
  98.1 0.2 copy.50
  98.3 0.2 slice.141.sums_ref
  98.5 0.2 copy.49
  98.8 0.2 slice.139.sums_ref
  99.0 1.6 %copy-done.1 = bf16[1024,1024]{1,0:T(8,128)(2,1)S(1)} copy-done((bf16[1024,1024]{1,0:T(8,128)(2,1)S(1)}, bf16[1024,1024]{1,0:T(8,128)(2,1)}, u32[]{:S(2)}) %copy-start.1) | copy-done | bytes 2097176
  100.5 0.7 shard_map.139.start_ref
  101.2 0.9 copy-done.2
  102.1 1.3 %shard_map.140 = f32[16,1024]{1,0:T(8,128)} custom-call(bf16[16,1024]{1,0:T(8,128)(2,1)S(1)} %slice.139.sums_ref, f32[16,1024]{1,0:T(8,128)S(1)} %shard_map.139.start_ref, bf16[1024,1024]{1,0:T(8,128)(2,1)S(1)} %copy-done.2), custom_call_target="tpu_custom_call" | custom-call | flops 35000000 | bytes 2200000 | tf_op jit(solution)/shard_map/pallas_call | solution.py:201
  103.6 0.8 fusion
  104.5 0.7 maximum_convert_fusion.1
  105.2 0.1 copy.54
  105.3 0.7 copy.56
  (81 shorter events, 1.0 us)
Async XLA Ops:
  0.6 43.0 %copy-start = (bf16[1024,1024]{1,0:T(8,128)(2,1)S(1)}, bf16[1024,1024]{1,0:T(8,128)(2,1)}, u32[]{:S(2)}) copy-start(bf16[1024,1024]{1,0:T(8,128)(2,1)} %param.18) | copy-start | bytes 6291460
  3.4 15.8 %collective-permute-start.8 = (bf16[800,128]{1,0:T(8,128)(2,1)S(1)}, bf16[800,128]{1,0:T(8,128)(2,1)S(1)}, u32[]{:S(2)}, u32[]{:S(2)}) collective-permute-start(bf16[800,128]{1,0:T(8,128)(2,1)S(1)} %get-tuple-element.70), channel_id=1, source_target_pairs={{0,16},{8,24},{16,0},{24,8},{1,17},{9,25},{17,1},{25,9},{2,18},{10... | collective-permute-start | bytes 614408 | tf_op jit(solution)/shard_map/ppermute | solution.py:23
  7.8 12.0 %collective-permute-start.2 = (bf16[2,16,1024]{2,1,0:T(8,128)(2,1)S(1)}, bf16[2,16,1024]{2,1,0:T(8,128)(2,1)S(1)}, u32[]{:S(2)}, u32[]{:S(2)}) collective-permute-start(bf16[2,16,1024]{2,1,0:T(8,128)(2,1)S(1)} %bitcast.115), channel_id=1, source_target_pairs={{0,2},{2,4},{4,6},{6,0},{1,3},{3,5},{5,7},{7,1},{8,10},{10,12},{12... | collective-permute-start | bytes 196616 | tf_op jit(solution)/shard_map/ppermute | solution.py:23
  10.8 11.5 %collective-permute-start = (bf16[2,16,1024]{2,1,0:T(8,128)(2,1)S(1)}, bf16[2,16,1024]{2,1,0:T(8,128)(2,1)S(1)}, u32[]{:S(2)}, u32[]{:S(2)}) collective-permute-start(bf16[2,16,1024]{2,1,0:T(8,128)(2,1)S(1)} %bitcast.116), channel_id=1, source_target_pairs={{0,6},{2,0},{4,2},{6,4},{1,7},{3,1},{5,3},{7,5},{8,14},{10,8},{12,... | collective-permute-start | bytes 196616 | tf_op jit(solution)/shard_map/ppermute | solution.py:23
  13.9 8.4 %collective-permute-start.1 = (bf16[2,16,1024]{2,1,0:T(8,128)(2,1)S(1)}, bf16[2,16,1024]{2,1,0:T(8,128)(2,1)S(1)}, u32[]{:S(2)}, u32[]{:S(2)}) collective-permute-start(bf16[2,16,1024]{2,1,0:T(8,128)(2,1)S(1)} %bitcast.117), channel_id=1, source_target_pairs={{0,4},{2,6},{4,0},{6,2},{1,5},{3,7},{5,1},{7,3},{8,12},{10,14},{12... | collective-permute-start | bytes 196616 | tf_op jit(solution)/shard_map/ppermute | solution.py:23
  18.3 6.2 %collective-permute-start.6 = (bf16[800,128]{1,0:T(8,128)(2,1)S(1)}, bf16[800,128]{1,0:T(8,128)(2,1)S(1)}, u32[]{:S(2)}, u32[]{:S(2)}) collective-permute-start(bf16[800,128]{1,0:T(8,128)(2,1)S(1)} %get-tuple-element.70), channel_id=1, source_target_pairs={{0,24},{8,0},{16,8},{24,16},{1,25},{9,1},{17,9},{25,17},{2,26},{10... | collective-permute-start | bytes 614408 | tf_op jit(solution)/shard_map/ppermute | solution.py:23
  19.2 6.0 %collective-permute-start.7 = (bf16[800,128]{1,0:T(8,128)(2,1)S(1)}, bf16[800,128]{1,0:T(8,128)(2,1)S(1)}, u32[]{:S(2)}, u32[]{:S(2)}) collective-permute-start(bf16[800,128]{1,0:T(8,128)(2,1)S(1)} %get-tuple-element.70), channel_id=1, source_target_pairs={{0,8},{8,16},{16,24},{24,0},{1,9},{9,17},{17,25},{25,1},{2,10},{10... | collective-permute-start | bytes 614408 | tf_op jit(solution)/shard_map/ppermute | solution.py:23
  19.9 19.5 %collective-permute-start.9 = (bf16[2,800,128]{2,1,0:T(8,128)(2,1)S(1)}, bf16[2,800,128]{2,1,0:T(8,128)(2,1)S(1)}, u32[]{:S(2)}, u32[]{:S(2)}) collective-permute-start(bf16[2,800,128]{2,1,0:T(8,128)(2,1)S(1)} %pad_maximum_fusion.3.edge_ref), channel_id=1, source_target_pairs={{0,1},{1,0},{2,3},{3,2},{4,5},{5,4},{6,7},{7,6},{8,9},{9,8},{10,11... | collective-permute-start | bytes 1228808 | tf_op jit(solution)/shard_map/ppermute | solution.py:23
  22.4 8.2 %collective-permute-start.3 = (bf16[4,2,16,1024]{3,2,1,0:T(8,128)(2,1)S(1)}, bf16[4,2,16,1024]{3,2,1,0:T(8,128)(2,1)S(1)}, u32[]{:S(2)}, u32[]{:S(2)}) collective-permute-start(bf16[4,2,16,1024]{3,2,1,0:T(8,128)(2,1)S(1)} %get-tuple-element.68), channel_id=1, source_target_pairs={{0,24},{8,0},{16,8},{24,16},{1,25},{9,1},{17,9},{25,17},{2,26},{10... | collective-permute-start | bytes 786440 | tf_op jit(solution)/shard_map/ppermute | solution.py:23
  24.5 8.6 %collective-permute-start.4 = (bf16[4,2,16,1024]{3,2,1,0:T(8,128)(2,1)S(1)}, bf16[4,2,16,1024]{3,2,1,0:T(8,128)(2,1)S(1)}, u32[]{:S(2)}, u32[]{:S(2)}) collective-permute-start(bf16[4,2,16,1024]{3,2,1,0:T(8,128)(2,1)S(1)} %get-tuple-element.68), channel_id=1, source_target_pairs={{0,16},{8,24},{16,0},{24,8},{1,17},{9,25},{17,1},{25,9},{2,18},{10... | collective-permute-start | bytes 786440 | tf_op jit(solution)/shard_map/ppermute | solution.py:23
  24.5 14.7 %collective-permute-start.5 = (bf16[4,2,16,1024]{3,2,1,0:T(8,128)(2,1)S(1)}, bf16[4,2,16,1024]{3,2,1,0:T(8,128)(2,1)S(1)}, u32[]{:S(2)}, u32[]{:S(2)}) collective-permute-start(bf16[4,2,16,1024]{3,2,1,0:T(8,128)(2,1)S(1)} %get-tuple-element.68), channel_id=1, source_target_pairs={{0,8},{8,16},{16,24},{24,0},{1,9},{9,17},{17,25},{25,1},{2,10},{10... | collective-permute-start | bytes 786440 | tf_op jit(solution)/shard_map/ppermute | solution.py:23
  39.4 0.8 copy-start.5
  40.2 3.4 %collective-permute-start.11 = (bf16[4,4,2,16,1024]{4,3,2,1,0:T(8,128)(2,1)S(1)}, bf16[4,4,2,16,1024]{4,3,2,1,0:T(8,128)(2,1)}, u32[]{:S(2)}, u32[]{:S(2)}) collective-permute-start(bf16[4,4,2,16,1024]{4,3,2,1,0:T(8,128)(2,1)S(1)} %pad_maximum_fusion.mine_ref), channel_id=1, source_target_pairs={{0,1},{1,0},{2,3},{3,2},{4,5},{5,4},{6,7},{7,6},{8,9},{9,8},{10,11... | collective-permute-start | bytes 3145736 | tf_op jit(solution)/shard_map/ppermute | solution.py:23
  41.0 2.2 %copy-start.3 = (bf16[2,800,128]{2,1,0:T(8,128)(2,1)S(1)}, bf16[2,800,128]{2,1,0:T(8,128)(2,1)}, u32[]{:S(2)}) copy-start(bf16[2,800,128]{2,1,0:T(8,128)(2,1)} %pad_maximum_fusion.2.edge_ref) | copy-start | bytes 1228804
  41.0 2.6 %copy-start.6 = (bf16[2,800,128]{2,1,0:T(8,128)(2,1)S(1)}, bf16[2,800,128]{2,1,0:T(8,128)(2,1)}, u32[]{:S(2)}) copy-start(bf16[2,800,128]{2,1,0:T(8,128)(2,1)} %copy-done.5) | copy-start | bytes 1228804
  43.2 6.4 %collective-permute-start.10 = (bf16[2,800,128]{2,1,0:T(8,128)(2,1)S(1)}, bf16[2,800,128]{2,1,0:T(8,128)(2,1)S(1)}, u32[]{:S(2)}, u32[]{:S(2)}) collective-permute-start(bf16[2,800,128]{2,1,0:T(8,128)(2,1)S(1)} %copy-done.3), channel_id=1, source_target_pairs={{0,1},{1,0},{2,3},{3,2},{4,5},{5,4},{6,7},{7,6},{8,9},{9,8},{10,11... | collective-permute-start | bytes 1228808 | tf_op jit(solution)/shard_map/ppermute | solution.py:23
  54.4 7.7 %collective-permute-start.12 = (bf16[800,128]{1,0:T(8,128)(2,1)S(1)}, bf16[800,128]{1,0:T(8,128)(2,1)S(1)}, u32[]{:S(2)}, u32[]{:S(2)}) collective-permute-start(bf16[800,128]{1,0:T(8,128)(2,1)S(1)} %get-tuple-element.44), channel_id=1, source_target_pairs={{0,32},{32,64},{64,96},{96,0},{1,33},{33,65},{65,97},{97,1},{2,34}... | collective-permute-start | bytes 614408 | tf_op jit(solution)/shard_map/ppermute | solution.py:23
  55.8 11.8 %collective-permute-start.13 = (bf16[800,128]{1,0:T(8,128)(2,1)S(1)}, bf16[800,128]{1,0:T(8,128)(2,1)}, u32[]{:S(2)}, u32[]{:S(2)}) collective-permute-start(bf16[800,128]{1,0:T(8,128)(2,1)S(1)} %get-tuple-element.45), channel_id=1, source_target_pairs={{0,64},{32,96},{64,0},{96,32},{1,65},{33,97},{65,1},{97,33},{2,66}... | collective-permute-start | bytes 614408 | tf_op jit(solution)/shard_map/ppermute | solution.py:23
  58.4 9.2 %collective-permute-start.14 = (bf16[800,128]{1,0:T(8,128)(2,1)S(1)}, bf16[800,128]{1,0:T(8,128)(2,1)}, u32[]{:S(2)}, u32[]{:S(2)}) collective-permute-start(bf16[800,128]{1,0:T(8,128)(2,1)S(1)} %get-tuple-element.46), channel_id=1, source_target_pairs={{0,96},{32,0},{64,32},{96,64},{1,97},{33,1},{65,33},{97,65},{2,98}... | collective-permute-start | bytes 614408 | tf_op jit(solution)/shard_map/ppermute | solution.py:23
  59.5 12.2 %collective-permute-start.18 = (bf16[4,2,2,16,128]{4,3,2,1,0:T(8,128)(2,1)S(1)}, bf16[4,2,2,16,128]{4,3,2,1,0:T(8,128)(2,1)S(1)}, u32[]{:S(2)}, u32[]{:S(2)}) collective-permute-start(bf16[4,2,2,16,128]{4,3,2,1,0:T(8,128)(2,1)S(1)} %get-tuple-element.48), channel_id=1, source_target_pairs={{0,2},{2,4},{4,6},{6,0},{1,3},{3,5},{5,7},{7,1},{8,10},{10,12},{12... | collective-permute-start | bytes 196616 | tf_op jit(solution)/shard_map/ppermute | solution.py:23
  59.5 15.7 %collective-permute-start.19 = (bf16[4,2,2,16,128]{4,3,2,1,0:T(8,128)(2,1)S(1)}, bf16[4,2,2,16,128]{4,3,2,1,0:T(8,128)(2,1)S(1)}, u32[]{:S(2)}, u32[]{:S(2)}) collective-permute-start(bf16[4,2,2,16,128]{4,3,2,1,0:T(8,128)(2,1)S(1)} %get-tuple-element.49), channel_id=1, source_target_pairs={{0,4},{2,6},{4,0},{6,2},{1,5},{3,7},{5,1},{7,3},{8,12},{10,14},{12... | collective-permute-start | bytes 196616 | tf_op jit(solution)/shard_map/ppermute | solution.py:23
  62.1 13.0 %collective-permute-start.20 = (bf16[4,2,2,16,128]{4,3,2,1,0:T(8,128)(2,1)S(1)}, bf16[4,2,2,16,128]{4,3,2,1,0:T(8,128)(2,1)S(1)}, u32[]{:S(2)}, u32[]{:S(2)}) collective-permute-start(bf16[4,2,2,16,128]{4,3,2,1,0:T(8,128)(2,1)S(1)} %get-tuple-element.50), channel_id=1, source_target_pairs={{0,6},{2,0},{4,2},{6,4},{1,7},{3,1},{5,3},{7,5},{8,14},{10,8},{12,... | collective-permute-start | bytes 196616 | tf_op jit(solution)/shard_map/ppermute | solution.py:23
  68.9 6.3 %collective-permute-start.15 = (bf16[224,128]{1,0:T(8,128)(2,1)S(1)}, bf16[224,128]{1,0:T(8,128)(2,1)S(1)}, u32[]{:S(2)}, u32[]{:S(2)}) collective-permute-start(bf16[224,128]{1,0:T(8,128)(2,1)S(1)} %get-tuple-element.106), channel_id=1, source_target_pairs={{0,2},{2,4},{4,6},{6,0},{1,3},{3,5},{5,7},{7,1},{8,10},{10,12},{12... | collective-permute-start | bytes 172040 | tf_op jit(solution)/shard_map/ppermute | solution.py:23
  69.0 7.7 %collective-permute-start.16 = (bf16[224,128]{1,0:T(8,128)(2,1)S(1)}, bf16[224,128]{1,0:T(8,128)(2,1)S(1)}, u32[]{:S(2)}, u32[]{:S(2)}) collective-permute-start(bf16[224,128]{1,0:T(8,128)(2,1)S(1)} %get-tuple-element.107), channel_id=1, source_target_pairs={{0,4},{2,6},{4,0},{6,2},{1,5},{3,7},{5,1},{7,3},{8,12},{10,14},{12... | collective-permute-start | bytes 172040 | tf_op jit(solution)/shard_map/ppermute | solution.py:23
  71.7 5.0 %collective-permute-start.17 = (bf16[224,128]{1,0:T(8,128)(2,1)S(1)}, bf16[224,128]{1,0:T(8,128)(2,1)S(1)}, u32[]{:S(2)}, u32[]{:S(2)}) collective-permute-start(bf16[224,128]{1,0:T(8,128)(2,1)S(1)} %get-tuple-element.105), channel_id=1, source_target_pairs={{0,6},{2,0},{4,2},{6,4},{1,7},{3,1},{5,3},{7,5},{8,14},{10,8},{12,... | collective-permute-start | bytes 172040 | tf_op jit(solution)/shard_map/ppermute | solution.py:23
  76.8 4.3 %collective-permute-start.21 = (bf16[224,128]{1,0:T(8,128)(2,1)S(1)}, bf16[224,128]{1,0:T(8,128)(2,1)S(1)}, u32[]{:S(2)}, u32[]{:S(2)}) collective-permute-start(bf16[224,128]{1,0:T(8,128)(2,1)S(1)} %pad_maximum_fusion.20), channel_id=1, source_target_pairs={{0,128},{128,0},{1,129},{129,1},{2,130},{130,2},{3,131},{131,3},{4... | collective-permute-start | bytes 172040 | tf_op jit(solution)/shard_map/ppermute | solution.py:23
  81.2 4.4 %collective-permute-start.22 = (bf16[128,128]{1,0:T(8,128)(2,1)S(1)}, bf16[128,128]{1,0:T(8,128)(2,1)S(1)}, u32[]{:S(2)}, u32[]{:S(2)}) collective-permute-start(bf16[128,128]{1,0:T(8,128)(2,1)S(1)} %get-tuple-element.102), channel_id=1, source_target_pairs={{0,8},{8,16},{16,24},{24,0},{1,9},{9,17},{17,25},{25,1},{2,10},{10... | collective-permute-start | bytes 98312 | tf_op jit(solution)/shard_map/ppermute | solution.py:23
  81.9 5.2 %collective-permute-start.23 = (bf16[128,128]{1,0:T(8,128)(2,1)S(1)}, bf16[128,128]{1,0:T(8,128)(2,1)S(1)}, u32[]{:S(2)}, u32[]{:S(2)}) collective-permute-start(bf16[128,128]{1,0:T(8,128)(2,1)S(1)} %get-tuple-element.103), channel_id=1, source_target_pairs={{0,16},{8,24},{16,0},{24,8},{1,17},{9,25},{17,1},{25,9},{2,18},{10... | collective-permute-start | bytes 98312 | tf_op jit(solution)/shard_map/ppermute | solution.py:23
  85.5 2.8 %collective-permute-start.24 = (bf16[128,128]{1,0:T(8,128)(2,1)S(1)}, bf16[128,128]{1,0:T(8,128)(2,1)S(1)}, u32[]{:S(2)}, u32[]{:S(2)}) collective-permute-start(bf16[128,128]{1,0:T(8,128)(2,1)S(1)} %get-tuple-element.104), channel_id=1, source_target_pairs={{0,24},{8,0},{16,8},{24,16},{1,25},{9,1},{17,9},{25,17},{2,26},{10... | collective-permute-start | bytes 98312 | tf_op jit(solution)/shard_map/ppermute | solution.py:23
  88.4 4.8 %collective-permute-start.25 = (bf16[4,80,128]{2,1,0:T(8,128)(2,1)S(1)}, bf16[4,80,128]{2,1,0:T(8,128)(2,1)S(1)}, u32[]{:S(2)}, u32[]{:S(2)}) collective-permute-start(bf16[4,80,128]{2,1,0:T(8,128)(2,1)S(1)} %get-tuple-element.73), channel_id=1, source_target_pairs={{0,1},{1,0},{2,3},{3,2},{4,5},{5,4},{6,7},{7,6},{8,9},{9,8},{10,11... | collective-permute-start | bytes 245768 | tf_op jit(solution)/shard_map/ppermute | solution.py:23
  93.4 5.6 %copy-start.4 = (bf16[1,16,1024]{2,1,0:T(8,128)(2,1)S(1)}, bf16[1,16,1024]{2,1,0:T(8,128)(2,1)}, u32[]{:S(2)}) copy-start(bf16[1,16,1024]{2,1,0:T(8,128)(2,1)} %param.11) | copy-start | bytes 98308
  93.9 9.6 %collective-permute-start.26 = (bf16[56,1024]{1,0:T(8,128)(2,1)S(1)}, bf16[56,1024]{1,0:T(8,128)(2,1)S(1)}, u32[]{:S(2)}, u32[]{:S(2)}) collective-permute-start(bf16[56,1024]{1,0:T(8,128)(2,1)S(1)} %get-tuple-element.84), channel_id=1, source_target_pairs={{0,32},{32,64},{64,96},{96,0},{1,33},{33,65},{65,97},{97,1},{2,34}... | collective-permute-start | bytes 344072 | tf_op jit(solution)/shard_map/ppermute | solution.py:23
  95.0 8.5 %collective-permute-start.27 = (bf16[56,1024]{1,0:T(8,128)(2,1)S(1)}, bf16[56,1024]{1,0:T(8,128)(2,1)S(1)}, u32[]{:S(2)}, u32[]{:S(2)}) collective-permute-start(bf16[56,1024]{1,0:T(8,128)(2,1)S(1)} %get-tuple-element.84), channel_id=1, source_target_pairs={{0,64},{32,96},{64,0},{96,32},{1,65},{33,97},{65,1},{97,33},{2,66}... | collective-permute-start | bytes 344072 | tf_op jit(solution)/shard_map/ppermute | solution.py:23
  97.9 5.6 %collective-permute-start.28 = (bf16[56,1024]{1,0:T(8,128)(2,1)S(1)}, bf16[56,1024]{1,0:T(8,128)(2,1)S(1)}, u32[]{:S(2)}, u32[]{:S(2)}) collective-permute-start(bf16[56,1024]{1,0:T(8,128)(2,1)S(1)} %get-tuple-element.84), channel_id=1, source_target_pairs={{0,96},{32,0},{64,32},{96,64},{1,97},{33,1},{65,33},{97,65},{2,98}... | collective-permute-start | bytes 344072 | tf_op jit(solution)/shard_map/ppermute | solution.py:23
  98.9 1.6 %copy-start.1 = (bf16[1024,1024]{1,0:T(8,128)(2,1)S(1)}, bf16[1024,1024]{1,0:T(8,128)(2,1)}, u32[]{:S(2)}) copy-start(bf16[1024,1024]{1,0:T(8,128)(2,1)} %w_ref.2) | copy-start | bytes 6291460
  100.5 1.6 %copy-start.2 = (bf16[1024,1024]{1,0:T(8,128)(2,1)S(1)}, bf16[1024,1024]{1,0:T(8,128)(2,1)}, u32[]{:S(2)}) copy-start(bf16[1024,1024]{1,0:T(8,128)(2,1)} %w_ref.3) | copy-start | bytes 6291460
